TPU v7x, 32 devices: a whole 2x2x4 slice. The times are simulated.
32 devices in a mesh: dp: 8 (over z, core), ctx: 4 (over y, x).
Axes of the slice: x: 2, y: 2, z: 4, core: 2. Of those that a mesh axis runs over, the one named last changes fastest.
Arguments:
- residual_in: bfloat16 [8, 1024, 2048], P('dp', 'ctx'), may hold values from -6 to 6
- document_ids: int32 [8, 1024], P('dp', 'ctx'), may hold values from 0 to 8191, as said below
- attention_gain: bfloat16 [2048], P(('dp', 'ctx')), may hold values from 0.099609375 to 1.8984375
- attention_shift: bfloat16 [2048], P(('dp', 'ctx')), may hold values from -3 to 3
- query_key_value: bfloat16 [2048, 6144], P(('dp', 'ctx')), may hold values from -0.125 to 0.125
- query_value_bias: bfloat16 [4096], P(('dp', 'ctx')), may hold values from -3 to 3
- output_weight: bfloat16 [2048, 2048], P(('dp', 'ctx')), may hold values from -0.5 to 0.5
- output_bias: bfloat16 [2048], P(('dp', 'ctx')), may hold values from -3 to 3
- feedforward_gain: bfloat16 [2048], P(('dp', 'ctx')), may hold values from 0.099609375 to 1.8984375
- feedforward_shift: bfloat16 [2048], P(('dp', 'ctx')), may hold values from -3 to 3
- expand_weight: bfloat16 [2048, 8192], P(('dp', 'ctx')), may hold values from -0.125 to 0.125
- expand_bias: bfloat16 [8192], P(('dp', 'ctx')), may hold values from -3 to 3
- contract_weight: bfloat16 [8192, 2048], P(('dp', 'ctx')), may hold values from -0.09375 to 0.09375
- contract_bias: bfloat16 [2048], P(('dp', 'ctx')), may hold values from -3 to 3
- output_grad: bfloat16 [8, 1024, 2048], P('dp', 'ctx'), may hold values from -6 to 6
Outputs:
- layer_output: bfloat16 [8, 1024, 2048], P('dp', 'ctx')
- input_grad: bfloat16 [8, 1024, 2048], P('dp', 'ctx')
- attention_gain_grad: float32 [2048], P(('dp', 'ctx'))
- attention_shift_grad: float32 [2048], P(('dp', 'ctx'))
- query_key_value_grad: float32 [2048, 6144], P(('dp', 'ctx'))
- query_value_bias_grad: float32 [4096], P(('dp', 'ctx'))
- output_weight_grad: float32 [2048, 2048], P(('dp', 'ctx'))
- output_bias_grad: float32 [2048], P(('dp', 'ctx'))
- feedforward_gain_grad: float32 [2048], P(('dp', 'ctx'))
- feedforward_shift_grad: float32 [2048], P(('dp', 'ctx'))
- expand_weight_grad: float32 [2048, 8192], P(('dp', 'ctx'))
- expand_bias_grad: float32 [8192], P(('dp', 'ctx'))
- contract_weight_grad: float32 [8192, 2048], P(('dp', 'ctx'))
- contract_bias_grad: float32 [2048], P(('dp', 'ctx'))
Inputs may be any that keep to these rules, and one draw needn't show every extreme that they name: document_ids[b, p] = b * 1024 + s, where s is the first position of the document that holds position p of sequence b; every document is a run of consecutive positions of one sequence, so values stay below 8192.
All inputs are finite; a program needn't handle non-finite values.
Results may differ from a plain program's by a relative error of at most 0.013.
Values may be sent and summed in bfloat16 or wider, within the bound.
No kernel may reach another device: no remote copies, remote signals or barrier semaphores. Data moves between devices by JAX's collectives and lax.ppermute only.
A program may use at most 512 MiB of HBM per device.

v0:
```python
import jax
import jax.numpy as jnp
from jax import lax
from jax.sharding import PartitionSpec as P

HEADS = 32
HEAD_DIM = 64


epsilon = 1e-05


def norm_forward(value, gain, shift):
    mean = jnp.mean(value, axis=-1, keepdims=True)
    centred = value - mean
    scale = lax.rsqrt(jnp.mean(centred * centred, axis=-1, keepdims=True) + epsilon)
    unit = centred * scale
    return (unit * gain + shift, unit, scale)


def norm_backward(grad, unit, scale, gain):
    scaled = grad * gain
    level = jnp.mean(scaled, axis=-1, keepdims=True)
    along = jnp.mean(scaled * unit, axis=-1, keepdims=True)
    return (
        scale * (scaled - level - unit * along),
        jnp.sum(grad * unit, axis=0),
        jnp.sum(grad, axis=0),
    )


def alibi_scores(queries, keys, query_place, query_docs, key_docs):
    heads = queries.shape[1]
    key_place = jnp.arange(keys.shape[0], dtype=jnp.int32)
    slopes = jnp.exp2(-8.0 * (jnp.arange(heads, dtype=jnp.float32) + 1.0) / heads)
    products = jnp.einsum("qhd,khd->hqk", queries, keys, preferred_element_type=jnp.float32)
    distance = (query_place[:, None] - key_place[None, :]).astype(jnp.float32)
    scores = products * 0.125 - slopes[:, None, None] * distance[None]
    visible = (query_docs[:, None] == key_docs[None, :]) & (
        key_place[None, :] <= query_place[:, None]
    )
    return jnp.where(visible[None], scores, -1e30)


def shards(
    residual_in,
    document_ids,
    attention_gain,
    attention_shift,
    query_key_value,
    query_value_bias,
    output_weight,
    output_bias,
    feedforward_gain,
    feedforward_shift,
    expand_weight,
    expand_bias,
    contract_weight,
    contract_bias,
    output_grad,
):
    seqs, stretch, width = residual_in.shape
    length = stretch * lax.axis_size("ctx")
    query_place = lax.axis_index("ctx") * stretch + jnp.arange(stretch, dtype=jnp.int32)
    head_shape = (seqs, -1, HEADS, HEAD_DIM)
    attention_params = (
        lax.all_gather(attention_gain, ("dp", "ctx"), axis=0, tiled=True),
        lax.all_gather(attention_shift, ("dp", "ctx"), axis=0, tiled=True),
        lax.all_gather(query_key_value, ("dp", "ctx"), axis=0, tiled=True),
        lax.all_gather(query_value_bias, ("dp", "ctx"), axis=0, tiled=True),
        lax.all_gather(output_weight, ("dp", "ctx"), axis=0, tiled=True),
        lax.all_gather(output_bias, ("dp", "ctx"), axis=0, tiled=True),
    )
    att_gain, att_shift, qkv_weight, qv_bias, out_weight, out_bias = attention_params
    rows = residual_in.reshape(-1, width).astype(jnp.float32)
    normed, unit_in, scale_in = norm_forward(
        rows, att_gain.astype(jnp.float32), att_shift.astype(jnp.float32)
    )
    normed_low = normed.astype(jnp.bfloat16)
    projected = jnp.dot(normed_low, qkv_weight, preferred_element_type=jnp.float32)
    queries = (projected[:, :width] + qv_bias[:width]).astype(jnp.bfloat16)
    keys = projected[:, width : 2 * width].astype(jnp.bfloat16)
    values = (projected[:, 2 * width :] + qv_bias[width:]).astype(jnp.bfloat16)
    local_pairs = jnp.concatenate([keys, values], axis=-1).reshape(seqs, stretch, 2 * width)
    gathered_pairs, key_docs = (
        lax.all_gather(local_pairs, "ctx", axis=1, tiled=True),
        lax.all_gather(document_ids, "ctx", axis=1, tiled=True),
    )
    query_heads = queries.reshape(head_shape)

    def attend_forward(item):
        query_part, pairs, query_docs, docs_all = item
        key_part = pairs[:, :width].reshape(length, HEADS, HEAD_DIM)
        value_part = pairs[:, width:].reshape(length, HEADS, HEAD_DIM)
        scores = alibi_scores(query_part, key_part, query_place, query_docs, docs_all)
        top = jnp.max(scores, axis=-1, keepdims=True)
        weights = jnp.exp(scores - top)
        total = jnp.sum(weights, axis=-1, keepdims=True)
        probs = (weights / total).astype(jnp.bfloat16)
        mixed = jnp.einsum("hqk,khd->qhd", probs, value_part, preferred_element_type=jnp.float32)
        return (mixed.reshape(stretch, width).astype(jnp.bfloat16), (top + jnp.log(total))[..., 0])

    attended, log_total = lax.map(
        attend_forward, (query_heads, gathered_pairs, document_ids, key_docs)
    )
    attended_rows = attended.reshape(-1, width)
    middle = (
        rows + jnp.dot(attended_rows, out_weight, preferred_element_type=jnp.float32) + out_bias
    )
    feedforward_params = (
        lax.all_gather(feedforward_gain, ("dp", "ctx"), axis=0, tiled=True),
        lax.all_gather(feedforward_shift, ("dp", "ctx"), axis=0, tiled=True),
        lax.all_gather(expand_weight, ("dp", "ctx"), axis=0, tiled=True),
        lax.all_gather(expand_bias, ("dp", "ctx"), axis=0, tiled=True),
        lax.all_gather(contract_weight, ("dp", "ctx"), axis=0, tiled=True),
        lax.all_gather(contract_bias, ("dp", "ctx"), axis=0, tiled=True),
    )
    ff_gain, ff_shift, exp_weight, exp_bias, con_weight, con_bias = feedforward_params
    normed_mid, unit_mid, scale_mid = norm_forward(
        middle, ff_gain.astype(jnp.float32), ff_shift.astype(jnp.float32)
    )
    normed_mid_low = normed_mid.astype(jnp.bfloat16)
    inner = jnp.dot(normed_mid_low, exp_weight, preferred_element_type=jnp.float32) + exp_bias
    cumulative = (1.0 + lax.erf(inner * 0.7071067811865476)) * 0.5
    active = (inner * cumulative).astype(jnp.bfloat16)
    result = middle + jnp.dot(active, con_weight, preferred_element_type=jnp.float32) + con_bias
    layer_output = result.astype(jnp.bfloat16).reshape(seqs, stretch, width)
    grad_out = output_grad.reshape(-1, width)
    grad_out_full = grad_out.astype(jnp.float32)
    contract_term = jnp.dot(active.T, grad_out, preferred_element_type=jnp.float32)
    contract_bias_term = jnp.sum(grad_out_full, axis=0)
    grad_active = jnp.dot(grad_out, con_weight.T, preferred_element_type=jnp.float32)
    density = jnp.exp(-0.5 * inner * inner) * 0.3989422804014327
    grad_inner = (grad_active * (cumulative + inner * density)).astype(jnp.bfloat16)
    expand_term = jnp.dot(normed_mid_low.T, grad_inner, preferred_element_type=jnp.float32)
    expand_bias_term = jnp.sum(grad_inner.astype(jnp.float32), axis=0)
    grad_normed_mid = jnp.dot(grad_inner, exp_weight.T, preferred_element_type=jnp.float32)
    grad_mid_norm, ff_gain_term, ff_shift_term = norm_backward(
        grad_normed_mid, unit_mid, scale_mid, ff_gain.astype(jnp.float32)
    )
    grad_middle = grad_out_full + grad_mid_norm
    ff_grads = (
        lax.psum_scatter(ff_gain_term, ("dp", "ctx"), scatter_dimension=0, tiled=True),
        lax.psum_scatter(ff_shift_term, ("dp", "ctx"), scatter_dimension=0, tiled=True),
        lax.psum_scatter(expand_term, ("dp", "ctx"), scatter_dimension=0, tiled=True),
        lax.psum_scatter(expand_bias_term, ("dp", "ctx"), scatter_dimension=0, tiled=True),
        lax.psum_scatter(contract_term, ("dp", "ctx"), scatter_dimension=0, tiled=True),
        lax.psum_scatter(contract_bias_term, ("dp", "ctx"), scatter_dimension=0, tiled=True),
    )
    grad_branch = grad_middle.astype(jnp.bfloat16)
    out_weight_term = jnp.dot(attended_rows.T, grad_branch, preferred_element_type=jnp.float32)
    out_bias_term = jnp.sum(grad_branch.astype(jnp.float32), axis=0)
    grad_attended = jnp.dot(grad_branch, out_weight.T, preferred_element_type=jnp.float32).astype(
        jnp.bfloat16
    )

    def attend_backward(item):
        query_part, pairs, query_docs, docs_all, totals, grad_mixed = item
        key_part = pairs[:, :width].reshape(length, HEADS, HEAD_DIM)
        value_part = pairs[:, width:].reshape(length, HEADS, HEAD_DIM)
        scores = alibi_scores(query_part, key_part, query_place, query_docs, docs_all)
        probs = jnp.exp(scores - totals[..., None])
        grad_probs = jnp.einsum(
            "qhd,khd->hqk", grad_mixed, value_part, preferred_element_type=jnp.float32
        )
        grad_scores = (
            probs * (grad_probs - jnp.sum(probs * grad_probs, axis=-1, keepdims=True))
        ).astype(jnp.bfloat16)
        grad_query_part = (
            jnp.einsum("hqk,khd->qhd", grad_scores, key_part, preferred_element_type=jnp.float32)
            * 0.125
        )
        grad_key_part = (
            jnp.einsum("hqk,qhd->khd", grad_scores, query_part, preferred_element_type=jnp.float32)
            * 0.125
        )
        grad_value_part = jnp.einsum(
            "hqk,qhd->khd",
            probs.astype(jnp.bfloat16),
            grad_mixed,
            preferred_element_type=jnp.float32,
        )
        pair_terms = jnp.concatenate(
            [grad_key_part.reshape(length, width), grad_value_part.reshape(length, width)], axis=-1
        )
        return (grad_query_part.reshape(stretch, width).astype(jnp.bfloat16), pair_terms)

    grad_query_rows, pair_terms = lax.map(
        attend_backward,
        (
            query_heads,
            gathered_pairs,
            document_ids,
            key_docs,
            log_total,
            grad_attended.reshape(head_shape),
        ),
    )
    grad_pairs = lax.psum_scatter(pair_terms, "ctx", scatter_dimension=1, tiled=True).astype(
        jnp.bfloat16
    )
    grad_projected = jnp.concatenate(
        [grad_query_rows.reshape(-1, width), grad_pairs.reshape(-1, 2 * width)], axis=-1
    )
    qkv_term = jnp.dot(normed_low.T, grad_projected, preferred_element_type=jnp.float32)
    grad_full = grad_projected.astype(jnp.float32)
    qv_bias_term = jnp.concatenate(
        [jnp.sum(grad_full[:, :width], axis=0), jnp.sum(grad_full[:, 2 * width :], axis=0)]
    )
    grad_normed_in = jnp.dot(grad_projected, qkv_weight.T, preferred_element_type=jnp.float32)
    grad_in_norm, att_gain_term, att_shift_term = norm_backward(
        grad_normed_in, unit_in, scale_in, att_gain.astype(jnp.float32)
    )
    input_grad = (grad_middle + grad_in_norm).astype(jnp.bfloat16).reshape(seqs, stretch, width)
    att_grads = (
        lax.psum_scatter(att_gain_term, ("dp", "ctx"), scatter_dimension=0, tiled=True),
        lax.psum_scatter(att_shift_term, ("dp", "ctx"), scatter_dimension=0, tiled=True),
        lax.psum_scatter(qkv_term, ("dp", "ctx"), scatter_dimension=0, tiled=True),
        lax.psum_scatter(qv_bias_term, ("dp", "ctx"), scatter_dimension=0, tiled=True),
        lax.psum_scatter(out_weight_term, ("dp", "ctx"), scatter_dimension=0, tiled=True),
        lax.psum_scatter(out_bias_term, ("dp", "ctx"), scatter_dimension=0, tiled=True),
    )
    return (
        layer_output,
        input_grad,
        att_grads[0],
        att_grads[1],
        att_grads[2],
        att_grads[3],
        att_grads[4],
        att_grads[5],
        ff_grads[0],
        ff_grads[1],
        ff_grads[2],
        ff_grads[3],
        ff_grads[4],
        ff_grads[5],
    )


def solution(mesh):
    in_specs = (
        P("dp", "ctx", None),
        P("dp", "ctx"),
        P(("dp", "ctx")),
        P(("dp", "ctx")),
        P(("dp", "ctx"), None),
        P(("dp", "ctx")),
        P(("dp", "ctx"), None),
        P(("dp", "ctx")),
        P(("dp", "ctx")),
        P(("dp", "ctx")),
        P(("dp", "ctx"), None),
        P(("dp", "ctx")),
        P(("dp", "ctx"), None),
        P(("dp", "ctx")),
        P("dp", "ctx", None),
    )
    out_specs = (
        P("dp", "ctx", None),
        P("dp", "ctx", None),
        P(("dp", "ctx")),
        P(("dp", "ctx")),
        P(("dp", "ctx"), None),
        P(("dp", "ctx")),
        P(("dp", "ctx"), None),
        P(("dp", "ctx")),
        P(("dp", "ctx")),
        P(("dp", "ctx")),
        P(("dp", "ctx"), None),
        P(("dp", "ctx")),
        P(("dp", "ctx"), None),
        P(("dp", "ctx")),
    )
    return jax.shard_map(shards, mesh=mesh, in_specs=in_specs, out_specs=out_specs, check_vma=False)
```

profile of v0, /device:TPU:0, one launch (start us, length us, event | category | flops | bytes accessed | tf_op | source)
XLA Modules:
  0.0 4795.6 jit_solution(3215040659975436182)
XLA Ops:
  7.2 0.7 all-gather.9.cloned.1.call-update
  8.0 0.9 dynamic-update-slice.4
  8.8 0.8 dynamic-update-slice.5
  9.7 0.8 dynamic-update-slice.2
  10.5 0.8 dynamic-update-slice
  11.4 0.8 dynamic-update-slice.1
  12.2 0.8 dynamic-update-slice.3
  13.1 43.6 all-reduce.15
  56.7 66.8 %all-gather.1 = bf16[32,1,128]{2,1,0:T(2,128)(2,1)S(1)} all-gather(bf16[1,1,128]{2,1,0:T(2,128)(2,1)} %bitcast.124), channel_id=1, replica_groups=mesh['dp'=8,'ctx'=4] {'dp','ctx'}, dimensions={0}, use_global_device_ids=true | all-gather | bytes 8448 | tf_op jit(solution)/shard_map/all_gather | solution.py:70
  123.5 1.4 convert_reduce_fusion.2
  125.0 1.6 fusion.31
  126.7 43.5 all-gather.9.cloned.1.call-done
  170.2 12.0 fusion.49
  182.9 1.5 pad_maximum_fusion.1
  186.4 65.6 %all-gather.2 = bf16[32,1,256]{2,1,0:T(2,128)(2,1)S(1)} all-gather(bf16[1,1,256]{2,1,0:T(2,128)(2,1)S(1)} %reshape.251), channel_id=1, replica_groups=mesh['dp'=8,'ctx'=4] {'dp','ctx'}, dimensions={0}, use_global_device_ids=true | all-gather | bytes 16896 | tf_op jit(solution)/shard_map/all_gather | solution.py:114
  252.1 6.7 all_gather.49
  259.3 0.7 copy.42
  260.0 10.8 all-gather.17.cloned.1.call-done
  270.8 6.0 fusion.52
  276.8 6.4 copy.43
  283.2 6.4 copy.41
  289.6 17.8 fusion.53
  307.4 14.3 fusion
  321.8 16.2 fusion.34
  338.0 13.3 all-gather.11.cloned.1.call-done
  351.2 6.2 fusion.54
  357.8 189.5 %all-gather.13.cloned.1.call-done = bf16[2048,8192]{1,0:T(8,128)(2,1)} async-done(((bf16[64,8192]{1,0:T(8,128)(2,1)}), bf16[2048,8192]{1,0:T(8,128)(2,1)}) %all-gather.13.cloned.1.call-update) | async-done | bytes 33554448 | tf_op jit(solution)/shard_map/all_gather | solution.py:113
  547.4 18.3 convolution_add_fusion
  565.7 177.4 %all-gather.15.cloned.1.call-done = bf16[8192,2048]{1,0:T(8,128)(2,1)} async-done(((bf16[256,2048]{1,0:T(8,128)(2,1)}), bf16[8192,2048]{1,0:T(8,128)(2,1)}) %all-gather.15.cloned.1.call-update) | async-done | bytes 33554448 | tf_op jit(solution)/shard_map/all_gather | solution.py:115
  743.1 20.2 convert_reduce_fusion
  763.3 18.7 multiply_reduce_fusion.1
  782.1 3.4 convert_reduce_fusion.3
  785.4 1.3 copy-done.5
  786.8 5.7 convolution_convert_fusion
  793.1 16.7 fusion.2
  809.8 23.8 multiply_reduce_fusion
  833.7 27.9 multiply_convert_fusion
  861.5 8.9 broadcast_multiply_fusion
  870.5 7.2 maximum_bitcast_fusion
  877.9 12.9 multiply_convert_fusion.2
  890.9 138.9 %reduce-scatter.6.cloned.1.call-done = f32[1,256,4096]{1,2,0:T(8,128)} async-done(((f32[1,1024,4096]{1,2,0:T(8,128)}), f32[1,256,4096]{1,2,0:T(8,128)}) %reduce-scatter.6.cloned.1.call-update) | async-done | bytes 4194320 | tf_op jit(solution)/shard_map/reduce_scatter | solution.py:199
  1029.8 2.4 convert_bitcast_fusion.1
  1034.0 13.8 fusion.30
  1047.9 10.1 fusion.45
  1058.7 21.0 fusion.41
  1079.8 1.1 copy-done.10
  1080.9 27.0 fusion.36
  1108.3 1.2 copy-done.1
  1109.5 25.6 fusion.51
  1135.8 22.8 fusion.22
  1158.5 4.0 fusion.35
  1162.5 9.3 all-reduce.18.cloned.1.call-done
  1171.9 1.3 dynamic-slice
  1173.1 1.3 dynamic-slice.1
  1174.4 1.3 dynamic-slice.3
  1175.7 1.3 dynamic-slice.4
  1176.9 1.3 dynamic-slice.5
  1178.2 1.3 dynamic-slice.7
  1179.4 1.3 dynamic-slice.2
  1180.7 1.3 dynamic-slice.6
  1182.0 351.5 %reduce-scatter.10.cloned.1.call-done = f32[64,2048]{1,0:T(8,128)} async-done(((f32[2048,2048]{1,0:T(8,128)}), f32[64,2048]{1,0:T(8,128)}) %reduce-scatter.10.cloned.1.call-update) | async-done | bytes 524304 | tf_op jit(solution)/shard_map/reduce_scatter | solution.py:220
  1533.5 441.2 %reduce-scatter.8.cloned.1.call-done = f32[64,6144]{1,0:T(8,128)} async-done(((f32[2048,6144]{1,0:T(8,128)}), f32[64,6144]{1,0:T(8,128)}) %reduce-scatter.8.cloned.1.call-update) | async-done | bytes 1572880 | tf_op jit(solution)/shard_map/reduce_scatter | solution.py:218
  1974.8 1406.3 %reduce-scatter.14.cloned.1.call-done = f32[256,2048]{1,0:T(8,128)} async-done(((f32[8192,2048]{1,0:T(8,128)}), f32[256,2048]{1,0:T(8,128)}) %reduce-scatter.14.cloned.1.call-update) | async-done | bytes 2097168 | tf_op jit(solution)/shard_map/reduce_scatter | solution.py:147
  3381.0 1407.6 %reduce-scatter.12.cloned.1.call-done = f32[64,8192]{1,0:T(8,128)} async-done(((f32[2048,8192]{1,0:T(8,128)}), f32[64,8192]{1,0:T(8,128)}) %reduce-scatter.12.cloned.1.call-update) | async-done | bytes 2097168 | tf_op jit(solution)/shard_map/reduce_scatter | solution.py:145
  (112 shorter events, 8.0 us)
Async XLA Ops:
  7.2 163.0 %all-gather.9.cloned.1.call-start = ((), (), s32[]{:S(2)}) async-start(), calls=%async_computation.5 | async-start | bytes 25952256 | tf_op jit(solution)/shard_map/all_gather | solution.py:69
  7.9 262.9 %all-gather.17.cloned.1.call-start = ((), (), s32[]{:S(2)}) async-start(), calls=%async_computation.14 | async-start | bytes 10485760 | tf_op jit(solution)/shard_map/all_gather | solution.py:86
  56.7 125.5 %copy-start.17 = (f32[2048]{0:T(1024)}, f32[2048]{0:T(1024)S(1)}, u32[]{:S(2)}) copy-start(f32[2048]{0:T(1024)S(1)} %convert_element_type.127) | copy-start | bytes 24580
  56.7 125.5 %copy-start.15 = (f32[2048]{0:T(1024)}, f32[2048]{0:T(1024)S(1)}, u32[]{:S(2)}) copy-start(f32[2048]{0:T(1024)S(1)} %convert_element_type.126) | copy-start | bytes 24580
  125.0 57.3 %copy-start.23 = (f32[256]{0:T(256)}, f32[256]{0:T(256)S(1)}, u32[]{:S(2)}) copy-start(f32[256]{0:T(256)S(1)} %broadcast_multiply_fusion.6) | copy-start | bytes 3076
  126.6 55.6 %copy-start.25 = (f32[256]{0:T(256)}, f32[256]{0:T(256)S(1)}, u32[]{:S(2)}) copy-start(f32[256]{0:T(256)S(1)} %add_rsqrt_fusion.1) | copy-start | bytes 3076
  182.9 3.5 copy-start.29
  182.9 69.2 %copy-start.27 = (s32[1,256]{1,0:T(1,128)S(1)}, s32[1,256]{1,0:T(1,128)}, u32[]{:S(2)}) copy-start(s32[1,256]{1,0:T(1,128)} %param.16) | copy-start | bytes 3076
  184.4 166.8 %all-gather.11.cloned.1.call-start = ((), (), s32[]{:S(2)}) async-start(), calls=%async_computation.6 | async-start | bytes 8650752 | tf_op jit(solution)/shard_map/all_gather | solution.py:71
  185.1 362.2 %all-gather.13.cloned.1.call-start = ((), (), s32[]{:S(2)}) async-start(), calls=%async_computation.7 | async-start | bytes 34603008 | tf_op jit(solution)/shard_map/all_gather | solution.py:113
  185.7 557.4 %all-gather.15.cloned.1.call-start = ((), (), s32[]{:S(2)}) async-start(), calls=%async_computation.8 | async-start | bytes 34603008 | tf_op jit(solution)/shard_map/all_gather | solution.py:115
  186.3 843.5 %reduce-scatter.6.cloned.1.call-start = ((), (), s32[]{:S(2)}) async-start(), calls=%async_computation.9 | async-start | bytes 20971520 | tf_op jit(solution)/shard_map/reduce_scatter | solution.py:199
  186.4 595.7 %copy-start.11 = (f32[2048]{0:T(1024)}, f32[2048]{0:T(1024)S(1)}, u32[]{:S(2)}) copy-start(f32[2048]{0:T(1024)S(1)} %convert_element_type.139) | copy-start | bytes 24580
  186.4 361.0 %copy-start.13 = (f32[2048]{0:T(1024)}, f32[2048]{0:T(1024)S(1)}, u32[]{:S(2)}) copy-start(f32[2048]{0:T(1024)S(1)} %convert_element_type.140) | copy-start | bytes 24580
  260.0 29.6 copy-start.7
  321.7 29.5 copy-start.3
  357.4 424.6 %copy-start = (f32[256,2048]{1,0:T(8,128)}, f32[256,2048]{1,0:T(8,128)S(1)}, u32[]{:S(2)}) copy-start(f32[256,2048]{1,0:T(8,128)S(1)} %get-tuple-element.104) | copy-start | bytes 6291460
  357.4 424.6 %copy-start.19 = (f32[256]{0:T(256)}, f32[256]{0:T(256)S(1)}, u32[]{:S(2)}) copy-start(f32[256]{0:T(256)S(1)} %broadcast_multiply_fusion.5) | copy-start | bytes 3076
  357.8 424.3 %copy-start.21 = (f32[256]{0:T(256)}, f32[256]{0:T(256)S(1)}, u32[]{:S(2)}) copy-start(f32[256]{0:T(256)S(1)} %add_rsqrt_fusion) | copy-start | bytes 3076
  547.4 195.7 %copy-start.9 = (bf16[1,256,2048]{2,1,0:T(8,128)(2,1)S(1)}, bf16[1,256,2048]{2,1,0:T(8,128)(2,1)}, u32[]{:S(2)}) copy-start(bf16[1,256,2048]{2,1,0:T(8,128)(2,1)} %param.29) | copy-start | bytes 3145732
  785.4 1.3 copy-start.5
  833.7 27.9 copy-start.8
  861.5 9.0 copy-start.2
  877.7 294.2 %all-reduce.18.cloned.1.call-start = ((), (), s32[]{:S(2)}) async-start(), calls=%async_computation.15 | async-start | bytes 196608
  890.9 141.4 %copy-start.6 = (bf16[32,64,256]{2,1,0:T(8,128)(2,1)}, bf16[32,64,256]{2,1,0:T(8,128)(2,1)S(1)}, u32[]{:S(2)}) copy-start(bf16[32,64,256]{2,1,0:T(8,128)(2,1)S(1)} %multiply_convert_fusion.2) | copy-start | bytes 3145732
  1032.7 1.3 copy-start.4
  1032.7 1.3 copy-start.16
  1032.7 1.3 copy-start.24
  1032.8 1.2 copy-start.26
  1047.9 485.7 %reduce-scatter.10.cloned.1.call-start = ((), (), s32[]{:S(2)}) async-start(), calls=%async_computation.11 | async-start | bytes 17301504 | tf_op jit(solution)/shard_map/reduce_scatter | solution.py:220
  1058.0 0.7 copy-start.18
  1058.0 916.8 %reduce-scatter.8.cloned.1.call-start = ((), (), s32[]{:S(2)}) async-start(), calls=%async_computation.10 | async-start | bytes 51904512 | tf_op jit(solution)/shard_map/reduce_scatter | solution.py:218
  1079.7 1.2 copy-start.10
  1079.7 2301.3 %reduce-scatter.14.cloned.1.call-start = ((), (), s32[]{:S(2)}) async-start(), calls=%async_computation.13 | async-start | bytes 69206016 | tf_op jit(solution)/shard_map/reduce_scatter | solution.py:147
  1107.9 1.6 copy-start.1
  1107.9 1.6 copy-start.12
  1107.9 1.6 copy-start.14
  1107.9 1.6 copy-start.20
  1107.9 1.6 copy-start.22
  1108.0 3680.7 %reduce-scatter.12.cloned.1.call-start = ((), (), s32[]{:S(2)}) async-start(), calls=%async_computation.12 | async-start | bytes 69206016 | tf_op jit(solution)/shard_map/reduce_scatter | solution.py:145
  1135.1 0.7 copy-start.28
Sparse Core Ops, SparseCore 0:
  10.9 159.2 all-gather.8
  184.5 86.2 all-gather.16
  273.7 77.5 all-gather.10
  354.0 193.3 all-gather.12
  550.1 192.9 all-gather.14
  877.8 151.9 reduce-scatter.5
  1048.0 123.8 all-reduce.17
  1174.8 358.6 reduce-scatter.9
  1541.7 433.0 reduce-scatter.7
  1977.7 1403.3 reduce-scatter.13
  3384.1 1404.4 reduce-scatter.11
where the time goes:
time: 4800 us
  waiting for transfers between devices  4190 us (87%)
  matrix products  298 us (6%)
  blocking collectives  183 us (4%)
  other arithmetic  66.8 us (1%)
    reduce_scatter x1, waiting for transfers between devices, shards(): lax.psum_scatter(expand_term, ('dp', 'ctx'), scatter_dimension=0, tiled=T...  1410 us
    reduce_scatter x1, waiting for transfers between devices, shards(): lax.psum_scatter(contract_term, ('dp', 'ctx'), scatter_dimension=0, tiled...  1410 us
    reduce_scatter x1, waiting for transfers between devices, shards(): lax.psum_scatter(qkv_term, ('dp', 'ctx'), scatter_dimension=0, tiled=True)  441 us
    reduce_scatter x1, waiting for transfers between devices, shards(): lax.psum_scatter(out_weight_term, ('dp', 'ctx'), scatter_dimension=0, til...  352 us
    all_gather x1, waiting for transfers between devices, shards(): lax.all_gather(expand_weight, ('dp', 'ctx'), axis=0, tiled=True)  190 us
    all_gather x1, waiting for transfers between devices, shards(): lax.all_gather(contract_weight, ('dp', 'ctx'), axis=0, tiled=True)  177 us
    reduce_scatter x1, waiting for transfers between devices, shards(): lax.psum_scatter(pair_terms, 'ctx', scatter_dimension=1, tiled=True)  139 us
  transfers between devices with their start and end apart: 11, of which 11 were waited for; matrix products, arithmetic and copies ran while one was open for 5% of the time, Pallas kernels for 0%

commit v1 on v0

v1 whole, which is shorter than its diff:
```python
import jax
import jax.numpy as jnp
from jax import lax
from jax.experimental import pallas as pl
from jax.experimental.pallas import tpu as pltpu
from jax.sharding import PartitionSpec as P

HEADS = 32
HEAD_DIM = 64
PAIR = 2 * HEAD_DIM

bf16 = jnp.bfloat16
f32 = jnp.float32
epsilon = 1e-05


def unit_rows(value):
    mean = jnp.mean(value, axis=-1, keepdims=True)
    centred = value - mean
    scale = lax.rsqrt(jnp.mean(centred * centred, axis=-1, keepdims=True) + epsilon)
    return centred * scale, scale


def norm_backward(grad, unit, scale, gain):
    scaled = grad * gain
    level = jnp.mean(scaled, axis=-1, keepdims=True)
    along = jnp.mean(scaled * unit, axis=-1, keepdims=True)
    return (
        scale * (scaled - level - unit * along),
        jnp.sum(grad * unit, axis=0),
        jnp.sum(grad, axis=0),
    )


def dot(left, right, contract=((1,), (0,))):
    return lax.dot_general(left, right, (contract, ((), ())), preferred_element_type=f32)


def lane_mask(half):
    lane = lax.broadcasted_iota(jnp.int32, (1, PAIR), 1)
    return (lane >= HEAD_DIM) if half else (lane < HEAD_DIM)


def attend_forward_kernel(slope_ref, start_ref, q_ref, k_ref, v_ref, out_ref, probs_ref):
    length = q_ref.shape[0]
    block = min(256, length)
    pair = pl.program_id(0)
    for index in range(length // block):
        rows = pl.ds(index * block, block)
        span = (index + 1) * block
        starts = start_ref[rows, :]
        q_place = index * block + lax.broadcasted_iota(jnp.int32, (block, span), 0)
        k_place = lax.broadcasted_iota(jnp.int32, (block, span), 1)
        visible = (k_place >= starts) & (k_place <= q_place)
        k_row = lax.broadcasted_iota(jnp.int32, (1, span), 1).astype(f32)
        mixed = []
        for half in range(2):
            slope = slope_ref[pair * 2 + half]
            query = jnp.where(lane_mask(half), q_ref[rows, :] * bf16(0.125), bf16(0))
            scores = dot(query, k_ref[:span, :], ((1,), (1,))) + slope * k_row
            scores = jnp.where(visible, scores, -1e30)
            top = jnp.max(scores, axis=-1, keepdims=True)
            weights = jnp.exp(scores - top)
            total = jnp.sum(weights, axis=-1, keepdims=True)
            probs = (weights * (1.0 / total)).astype(bf16)
            probs_ref[half, rows, :span] = probs
            mixed.append(dot(probs, v_ref[:span, :]))
        out_ref[rows, :] = jnp.where(lane_mask(0), mixed[0], mixed[1]).astype(bf16)


def attend_backward_kernel(probs_ref, q_ref, k_ref, v_ref, g_ref, dq_ref, dk_ref, dv_ref, dk_sum, dv_sum):
    length = q_ref.shape[0]
    block = min(256, length)
    dk_sum[...] = jnp.zeros_like(dk_sum)
    dv_sum[...] = jnp.zeros_like(dv_sum)
    for index in range(length // block):
        rows = pl.ds(index * block, block)
        span = (index + 1) * block
        parts = []
        for half in range(2):
            mask = lane_mask(half)
            grad = jnp.where(mask, g_ref[rows, :], bf16(0))
            query = jnp.where(mask, q_ref[rows, :] * bf16(0.125), bf16(0))
            probs_low = probs_ref[half, rows, :span]
            probs = probs_low.astype(f32)
            grad_probs = dot(grad, v_ref[:span, :], ((1,), (1,)))
            along = jnp.sum(probs * grad_probs, axis=-1, keepdims=True)
            grad_scores = (probs * (grad_probs - along)).astype(bf16)
            parts.append(dot(grad_scores, k_ref[:span, :]))
            dk_sum[:span, :] += dot(grad_scores, query, ((0,), (0,)))
            dv_sum[:span, :] += dot(probs_low, grad, ((0,), (0,)))
        dq_ref[rows, :] = (jnp.where(lane_mask(0), parts[0], parts[1]) * 0.125).astype(bf16)
    dk_ref[...] = dk_sum[...].astype(bf16)
    dv_ref[...] = dv_sum[...].astype(bf16)


def attend_forward(slopes, starts, projected):
    length = projected.shape[0]
    heads = projected.shape[1] // (3 * HEAD_DIM)
    pairs = heads // 2
    column = lambda first: pl.BlockSpec((length, PAIR), lambda p: (0, first + p))
    return pl.pallas_call(
        attend_forward_kernel,
        grid=(pairs,),
        in_specs=[
            pl.BlockSpec(memory_space=pltpu.SMEM),
            pl.BlockSpec((length, 1), lambda p: (0, 0)),
            column(0),
            column(pairs),
            column(2 * pairs),
        ],
        out_specs=[column(0), pl.BlockSpec((2, length, length), lambda p: (p, 0, 0))],
        out_shape=[
            jax.ShapeDtypeStruct((length, heads * HEAD_DIM), bf16),
            jax.ShapeDtypeStruct((heads, length, length), bf16),
        ],
        compiler_params=pltpu.CompilerParams(vmem_limit_bytes=50 * 2**20),
        cost_estimate=pl.CostEstimate(
            flops=4 * heads * length * length * PAIR,
            bytes_accessed=2 * heads * length * length,
            transcendentals=heads * length * length,
        ),
        name="attend_forward",
    )(slopes, starts, projected, projected, projected)


def attend_backward(probs, projected, grad):
    length = projected.shape[0]
    heads = projected.shape[1] // (3 * HEAD_DIM)
    pairs = heads // 2
    column = lambda first: pl.BlockSpec((length, PAIR), lambda p: (0, first + p))
    shape = jax.ShapeDtypeStruct((length, heads * HEAD_DIM), bf16)
    return pl.pallas_call(
        attend_backward_kernel,
        grid=(pairs,),
        in_specs=[
            pl.BlockSpec((2, length, length), lambda p: (p, 0, 0)),
            column(0),
            column(pairs),
            column(2 * pairs),
            column(0),
        ],
        out_specs=[column(0), column(0), column(0)],
        out_shape=[shape, shape, shape],
        scratch_shapes=[pltpu.VMEM((length, PAIR), f32), pltpu.VMEM((length, PAIR), f32)],
        compiler_params=pltpu.CompilerParams(vmem_limit_bytes=50 * 2**20),
        cost_estimate=pl.CostEstimate(
            flops=8 * heads * length * length * PAIR,
            bytes_accessed=2 * heads * length * length,
            transcendentals=0,
        ),
        name="attend_backward",
    )(probs, projected, projected, projected, grad)


ALL = ("dp", "ctx")


def swap(value):
    return lax.all_to_all(value, "ctx", 0, 0, tiled=True)


def shards(
    residual_in,
    document_ids,
    attention_gain,
    attention_shift,
    query_key_value,
    query_value_bias,
    output_weight,
    output_bias,
    feedforward_gain,
    feedforward_shift,
    expand_weight,
    expand_bias,
    contract_weight,
    contract_bias,
    output_grad,
):
    groups, ways = lax.axis_size("dp"), lax.axis_size("ctx")
    me_dp, me = lax.axis_index("dp"), lax.axis_index("ctx")
    seqs, stretch, width = residual_in.shape
    assert seqs == 1
    length = stretch * ways
    slab = query_key_value.shape[0]
    inner_slab = contract_weight.shape[0]
    features = width // ways
    heads = HEADS // ways

    def gather_ctx(value):
        return lax.all_gather(value, "ctx", axis=0, tiled=True)

    def scatter_ctx(value):
        return lax.psum_scatter(value.astype(bf16), "ctx", scatter_dimension=0, tiled=True).astype(f32)

    def gather_dp(value):
        return lax.all_gather(value, "dp", axis=0, tiled=True)

    def scatter_dp(value):
        return lax.psum_scatter(value.astype(bf16), "dp", scatter_dimension=0, tiled=True)

    small = (
        attention_gain,
        attention_shift,
        output_bias,
        feedforward_gain,
        feedforward_shift,
        contract_bias,
        query_value_bias,
        expand_bias,
    )
    packed = lax.all_gather(jnp.concatenate(small), ALL, axis=0).astype(f32)
    whole, at = [], 0
    for item in small:
        whole.append(packed[:, at : at + item.shape[0]].reshape(-1))
        at += item.shape[0]
    att_gain, att_shift, out_bias, ff_gain, ff_shift, con_bias, qv_bias, exp_bias = whole
    exp_bias = lax.dynamic_index_in_dim(
        exp_bias.reshape(groups, ways, inner_slab), me, 1, keepdims=False
    ).reshape(-1)
    qv_bias = lax.dynamic_index_in_dim(qv_bias.reshape(2, ways, features), me, 1, keepdims=False)

    qkv_rows = query_key_value.reshape(slab, 3, ways, features).transpose(2, 0, 1, 3)
    qkv_weight = gather_dp(swap(qkv_rows.reshape(ways * slab, 3 * features)))
    out_weight = lax.all_gather(output_weight, ALL, axis=0, tiled=True)
    exp_rows = expand_weight.reshape(slab, groups, ways, inner_slab).transpose(2, 0, 1, 3)
    exp_weight = gather_dp(swap(exp_rows.reshape(ways * slab, groups * inner_slab)))
    con_weight = gather_dp(contract_weight)

    block = residual_in[0]
    block_all = gather_ctx(block)
    grad_out = output_grad[0]
    grad_out_all = gather_ctx(grad_out)
    docs_all = gather_ctx(document_ids[0])
    starts = (docs_all - me_dp * length)[:, None]
    slopes = jnp.exp2(
        -8.0 * ((me * heads + jnp.arange(heads, dtype=jnp.int32)).astype(f32) + 1.0) / HEADS
    )

    rows = block.astype(f32)
    unit_in, scale_in = unit_rows(rows)
    normed_low = (unit_rows(block_all.astype(f32))[0] * att_gain + att_shift).astype(bf16)
    bias = jnp.concatenate([qv_bias[0], jnp.zeros((features,), f32), qv_bias[1]])
    projected = (dot(normed_low, qkv_weight) + bias).astype(bf16)
    attended, probs = attend_forward(slopes, starts, projected)
    attended_rows = lax.all_to_all(attended, "ctx", 0, 1, tiled=True)
    middle = rows + dot(attended_rows, out_weight) + out_bias

    unit_mid, scale_mid = unit_rows(middle)
    normed_mid = gather_ctx((unit_mid * ff_gain + ff_shift).astype(bf16))
    inner = dot(normed_mid, exp_weight) + exp_bias
    cumulative = (1.0 + lax.erf(inner * 0.7071067811865476)) * 0.5
    active = (inner * cumulative).astype(bf16)
    result = middle + scatter_ctx(dot(active, con_weight)) + con_bias
    layer_output = result.astype(bf16)[None]

    con_grad = scatter_dp(dot(active, grad_out_all, ((0,), (0,)))).astype(f32)
    grad_active = dot(grad_out_all, con_weight, ((1,), (1,)))
    density = jnp.exp(-0.5 * inner * inner) * 0.3989422804014327
    grad_inner = (grad_active * (cumulative + inner * density)).astype(bf16)
    exp_grad = swap(scatter_dp(dot(normed_mid, grad_inner, ((0,), (0,)))))
    exp_grad = (
        exp_grad.reshape(ways, slab, groups, inner_slab)
        .transpose(1, 2, 0, 3)
        .reshape(slab, -1)
        .astype(f32)
    )
    exp_bias_term = jnp.sum(grad_inner.astype(f32), axis=0)
    grad_normed_mid = scatter_ctx(dot(grad_inner, exp_weight, ((1,), (1,))))
    grad_mid_norm, ff_gain_term, ff_shift_term = norm_backward(
        grad_normed_mid, unit_mid, scale_mid, ff_gain
    )
    grad_out_full = grad_out.astype(f32)
    grad_middle = grad_out_full + grad_mid_norm
    grad_branch = grad_middle.astype(bf16)

    grad_attended = dot(grad_branch, out_weight, ((1,), (1,))).astype(bf16)
    grad_heads = lax.all_to_all(grad_attended, "ctx", 1, 0, tiled=True)
    grad_projected = jnp.concatenate(attend_backward(probs, projected, grad_heads), axis=1)
    out_grad = lax.psum_scatter(
        dot(attended_rows, grad_branch, ((0,), (0,))).astype(bf16),
        ALL,
        scatter_dimension=0,
        tiled=True,
    ).astype(f32)
    grad_normed_in = scatter_ctx(dot(grad_projected, qkv_weight, ((1,), (1,))))
    qkv_grad = swap(scatter_dp(dot(normed_low, grad_projected, ((0,), (0,)))))
    qkv_grad = (
        qkv_grad.reshape(ways, slab, 3, features)
        .transpose(1, 2, 0, 3)
        .reshape(slab, -1)
        .astype(f32)
    )
    grad_in_norm, att_gain_term, att_shift_term = norm_backward(
        grad_normed_in, unit_in, scale_in, att_gain
    )
    input_grad = (grad_middle + grad_in_norm).astype(bf16)[None]

    bias_sums = jnp.sum(grad_projected.astype(f32), axis=0).reshape(3, features)
    qv_term = lax.dynamic_update_slice(
        jnp.zeros((2, ways, features), f32),
        jnp.stack([bias_sums[0], bias_sums[2]])[:, None],
        (0, me, 0),
    ).reshape(-1)
    exp_term = lax.dynamic_update_slice(
        jnp.zeros((groups, ways, inner_slab), f32),
        exp_bias_term.reshape(groups, 1, inner_slab),
        (0, me, 0),
    ).reshape(-1)
    terms = (
        att_gain_term,
        att_shift_term,
        jnp.sum(grad_branch.astype(f32), axis=0),
        ff_gain_term,
        ff_shift_term,
        jnp.sum(grad_out_full, axis=0),
        qv_term,
        exp_term,
    )
    count = groups * ways
    sums = lax.psum_scatter(
        jnp.concatenate([item.reshape(count, -1) for item in terms], axis=1),
        ALL,
        scatter_dimension=0,
        tiled=True,
    ).reshape(-1)
    own, at = [], 0
    for item in small:
        own.append(sums[at : at + item.shape[0]])
        at += item.shape[0]
    return (
        layer_output,
        input_grad,
        own[0],
        own[1],
        qkv_grad,
        own[6],
        out_grad,
        own[2],
        own[3],
        own[4],
        exp_grad,
        own[7],
        con_grad,
        own[5],
    )


def solution(mesh):
    tokens = P("dp", "ctx", None)
    vector = P(ALL)
    matrix = P(ALL, None)
    in_specs = (
        tokens,
        P("dp", "ctx"),
        vector,
        vector,
        matrix,
        vector,
        matrix,
        vector,
        vector,
        vector,
        matrix,
        vector,
        matrix,
        vector,
        tokens,
    )
    out_specs = (
        tokens,
        tokens,
        vector,
        vector,
        matrix,
        vector,
        matrix,
        vector,
        vector,
        vector,
        matrix,
        vector,
        matrix,
        vector,
    )
    return jax.shard_map(shards, mesh=mesh, in_specs=in_specs, out_specs=out_specs, check_vma=False)
```

time: 4800 us -> 1320 us (0.28)
  waiting for transfers between devices: 4190 us -> 916 us
  matrix products: 298 us -> 137 us
  blocking collectives: 183 us -> 132 us
    reduce_scatter x5 -> x7, waiting for transfers between devices: 3750 us -> 499 us  [the longest x3 228 us: scatter_dp(): lax.psum_scatter(value.astype(bf16), 'dp', scatter_dimension=0, tiled=True)]
    dot_general x18 -> x12, matrix products: 298 us -> 137 us  [dot(): lax.dot_general(left, right, (contract, ((), ())), preferred_element_type...]
    all_gather x5 -> x7, waiting for transfers between devices: 434 us -> 280 us  [the longest x3 162 us: gather_dp(): return lax.all_gather(value, 'dp', axis=0, tiled=True)]
    unnamed x12 -> x16, waiting for transfers between devices: 11.9 us -> 121 us
    all_gather x3 -> x2, blocking collectives: 139 us -> 74.6 us  [the longest x1 67 us: shards(): packed = lax.all_gather(jnp.concatenate(small), ALL, axis=0).astype(f32)]
    all_to_all x0 -> x3, blocking collectives: none -> 57.8 us  [the longest x2 40.1 us: swap(): return lax.all_to_all(value, 'ctx', 0, 0, tiled=True)]
  transfers between devices with their start and end apart: 11 -> 18, of which waited for: 11 -> 15; matrix products, arithmetic and copies ran while one was open for 5% -> 11% of each run, Pallas kernels for 0% -> 2%
where the time goes in v1:
time: 1320 us
  waiting for transfers between devices  916 us (69%)
  matrix products  137 us (10%)
  blocking collectives  132 us (10%)
  Pallas kernels  42.9 us (3%)
  local copies, waits for them, and re-layouts  34.7 us (3%)
  other arithmetic  25.1 us (2%)
  between operations  14.8 us (1%)
  starting transfers between devices  13.7 us (1%)
    reduce_scatter x3, waiting for transfers between devices, scatter_dp(): lax.psum_scatter(value.astype(bf16), 'dp', scatter_dimension=0, tiled=True)  228 us
    reduce_scatter x1, waiting for transfers between devices, shards(): lax.psum_scatter(dot(attended_rows, grad_branch, ((0,), (0,))).astype(bf1...  174 us
    all_gather x3, waiting for transfers between devices, gather_dp(): return lax.all_gather(value, 'dp', axis=0, tiled=True)  162 us
    dot_general x12, matrix products, dot(): lax.dot_general(left, right, (contract, ((), ())), preferred_element_type...  137 us
    unnamed x16, waiting for transfers between devices  121 us
    reduce_scatter x3, waiting for transfers between devices, scatter_ctx(): lax.psum_scatter(value.astype(bf16), 'ctx', scatter_dimension=0, tiled=True)  97 us
    all_gather x3, waiting for transfers between devices, gather_ctx(): return lax.all_gather(value, 'ctx', axis=0, tiled=True)  92.2 us
    all_gather x1, blocking collectives, shards(): packed = lax.all_gather(jnp.concatenate(small), ALL, axis=0).astype(f32)  67 us
  transfers between devices with their start and end apart: 18, of which 15 were waited for; matrix products, arithmetic and copies ran while one was open for 11% of the time, Pallas kernels for 2%

profile of v1, /device:TPU:0, one launch (start us, length us, event | category | flops | bytes accessed | tf_op | source)
XLA Modules:
  0.0 1315.8 jit_solution(4010913065346459282)
XLA Ops:
  8.0 2.4 reshape.164
  10.8 1.1 all_to_all.56
  11.9 21.8 %all_to_all.80 = bf16[4,64,1536]{2,1,0:T(8,128)(2,1)} all-to-all(bf16[4,64,1536]{2,1,0:T(8,128)(2,1)S(1)} %all_to_all.56), channel_id=1, replica_groups=mesh['dp'=8,'ctx'=4] {'ctx'}, dimensions={0} | all-to-all | bytes 1572864 | tf_op jit(solution)/shard_map/all_to_all | solution.py:160
  34.5 0.8 reshape.165
  36.1 18.3 %all_to_all.81 = bf16[4,64,2048]{2,1,0:T(8,128)(2,1)} all-to-all(bf16[4,64,2048]{2,1,0:T(8,128)(2,1)S(1)} %all_to_all.63), channel_id=1, replica_groups=mesh['dp'=8,'ctx'=4] {'ctx'}, dimensions={0} | all-to-all | bytes 2097152 | tf_op jit(solution)/shard_map/all_to_all | solution.py:160
  54.6 67.0 %all-gather.4 = bf16[32,1,768]{2,1,0:T(2,128)(2,1)S(1)} all-gather(bf16[1,1,768]{2,1,0:T(2,128)(2,1)S(1)} %reshape.188), channel_id=4, replica_groups=mesh['dp'=8,'ctx'=4] {'dp','ctx'}, dimensions={0}, use_global_device_ids=true | all-gather | bytes 50688 | tf_op jit(solution)/shard_map/all_gather | solution.py:212
  121.8 7.6 all-gather
  129.8 3.0 convert_reduce_fusion
  133.3 1.2 fusion.3
  134.5 5.9 all-gather.13.cloned.1.call-done
  140.5 11.9 add_convert_fusion.q_ref.k_ref.v_ref
  152.3 21.0 %attend_forward.1 = (bf16[1024,512]{1,0:T(8,128)(2,1)S(1)}, bf16[8,1024,1024]{2,1,0:T(8,128)(2,1)}) custom-call(f32[8]{0:T(128)S(1)} %multiply_exponential_fusion.slope_ref, s32[1024,1]{1,0:T(8,128)S(1)} %copy.46.start_ref, bf16[1024,1536]{1,0:T(8,128)(2,1)} %add_convert_fusion.q_ref.k_ref.v_ref, bf16[1024,1536]{1,0:T(8,128)(2,1)} %add_convert_fusion.q_ref.k_ref.v_ref, ...), custom_call_target="tpu_custom_call" | custom-call | flops 4294967296 | bytes 16777216 | tf_op jit(solution)/shard_map/attend_forward/pallas_call | solution.py:102
  173.4 1.3 copy.47
  174.7 3.6 all-to-all-start.1
  178.5 15.6 %all-to-all-done.1 = bf16[4,256,512]{1,2,0:T(8,128)(2,1)S(1)} async-done(((bf16[4,256,512]{1,2,0:T(8,128)(2,1)}), bf16[4,256,512]{1,2,0:T(8,128)(2,1)S(1)}, u32[]{:S(2)}, u32[]{:S(2)}) %all-to-all-start.1) | async-done | bytes 1048608 | tf_op jit(solution)/shard_map/all_to_all | solution.py:246
  194.1 25.3 %all-gather.15.cloned.1.call-done = bf16[2048,2048]{1,0:T(8,128)(2,1)} async-done(((bf16[64,2048]{1,0:T(8,128)(2,1)}), bf16[2048,2048]{1,0:T(8,128)(2,1)}) %all-gather.15.cloned.1.call-update) | async-done | bytes 8388624 | tf_op jit(solution)/shard_map/all_gather | solution.py:225
  219.3 6.2 fusion.48
  225.9 1.4 add_convert_fusion.2
  229.0 72.5 %all-gather.19.cloned.1.call-done = bf16[2048,2048]{1,0:T(8,128)(2,1)} async-done(((bf16[256,2048]{1,0:T(8,128)(2,1)}), bf16[2048,2048]{1,0:T(8,128)(2,1)}) %all-gather.19.cloned.1.call-update) | async-done | bytes 8388624 | tf_op jit(solution)/shard_map/all_gather | solution.py:197
  301.5 53.5 %all-gather.17.cloned.1.call-done = bf16[1024,2048]{1,0:T(8,128)(2,1)} async-done(((bf16[256,2048]{1,0:T(8,128)(2,1)}), bf16[1024,2048]{1,0:T(8,128)(2,1)}) %all-gather.17.cloned.1.call-update) | async-done | bytes 4194320 | tf_op jit(solution)/shard_map/all_gather | solution.py:191
  355.0 15.8 %multiply_convert_fusion = (bf16[1024,2048]{1,0:T(8,128)(2,1)}, f32[1024,2048]{1,0:T(8,128)}) fusion(f32[2048]{0:T(1024)S(1)} %bitcast.163, bf16[1024,2048]{1,0:T(8,128)(2,1)} %all-gather.17.cloned.1.call-done, bf16[2048,2048]{1,0:T(8,128)(2,1)} %all-gather.19.cloned.1.call-done), kind=kOutput, calls=%fused_computation.17 | convolution fusion | flops 8602517504 | bytes 25174016 | tf_op jit(solution)/shard_map/dot_general | solution.py:36
  370.8 38.7 %all-gather.25.cloned.1.call-done = bf16[1,1024,2048]{2,1,0:T(8,128)(2,1)} async-done(((bf16[1,256,2048]{2,1,0:T(8,128)(2,1)}), bf16[1,1024,2048]{2,1,0:T(8,128)(2,1)}) %all-gather.25.cloned.1.call-update) | async-done | bytes 4194320 | tf_op jit(solution)/shard_map/all_gather | solution.py:191
  409.5 83.7 %all-gather.21.cloned.1.call-done = bf16[2048,2048]{1,0:T(8,128)(2,1)} async-done(((bf16[256,2048]{1,0:T(8,128)(2,1)}), bf16[2048,2048]{1,0:T(8,128)(2,1)}) %all-gather.21.cloned.1.call-update) | async-done | bytes 8388624 | tf_op jit(solution)/shard_map/all_gather | solution.py:197
  493.2 16.4 %convert_reduce_fusion.1 = (f32[2048]{0:T(1024)S(1)}, bf16[1024,2048]{1,0:T(8,128)(2,1)S(1)}) fusion(f32[1024,2048]{1,0:T(8,128)} %get-tuple-element.54, f32[2048]{0:T(1024)S(1)} %bitcast.164, bf16[2048,2048]{1,0:T(8,128)(2,1)} %all-gather.21.cloned.1.call-done, bf16[1,1024,2048]{2,1,0:T(8,128)(2,1)} %all-gather.25.cloned.1.call-done), kind=kOutput, calls=%fused_computation.16 | convolution fusion | flops 8617195520 | bytes 25182208 | tf_op jit(solution)/shard_map/dot_general | solution.py:36
  509.6 1.9 copy-done.27
  511.5 10.5 convolution_convert_fusion.5
  522.5 13.9 %convolution_convert_fusion.6 = bf16[1024,2048]{1,0:T(8,128)(2,1)} fusion(bf16[1024,2048]{1,0:T(8,128)(2,1)} %get-tuple-element.53, bf16[2048,2048]{1,0:T(8,128)(2,1)} %all-gather.21.cloned.1.call-done), kind=kOutput, calls=%fused_computation.29 | convolution fusion | flops 8592031744 | bytes 16777216 | tf_op jit(solution)/shard_map/dot_general | solution.py:36
  536.5 36.9 %reduce-scatter.10.cloned.1.call-done = bf16[256,2048]{1,0:T(8,128)(2,1)} async-done(((bf16[1024,2048]{1,0:T(8,128)(2,1)}), bf16[256,2048]{1,0:T(8,128)(2,1)}) %reduce-scatter.10.cloned.1.call-update) | async-done | bytes 1048592 | tf_op jit(solution)/shard_map/reduce_scatter | solution.py:194
  573.4 2.2 fusion.37
  575.6 53.7 %reduce-scatter.8.cloned.1.call-done = bf16[256,2048]{1,0:T(8,128)(2,1)} async-done(((bf16[1024,2048]{1,0:T(8,128)(2,1)}), bf16[256,2048]{1,0:T(8,128)(2,1)}) %reduce-scatter.8.cloned.1.call-update) | async-done | bytes 1048592 | tf_op jit(solution)/shard_map/reduce_scatter | solution.py:194
  629.3 3.6 convert_reduce_fusion.7
  633.0 6.5 convolution_convert_fusion.7
  639.6 17.7 %all_to_all.82 = bf16[256,4,512]{2,0,1:T(8,128)(2,1)} all-to-all(bf16[256,4,512]{2,0,1:T(8,128)(2,1)S(1)} %bitcast.153), channel_id=1, replica_groups=mesh['dp'=8,'ctx'=4] {'ctx'}, dimensions={1} | all-to-all | bytes 2097152 | tf_op jit(solution)/shard_map/all_to_all | solution.py:278
  657.4 21.9 %attend_backward.1 = (bf16[1024,512]{1,0:T(8,128)(2,1)S(1)}, bf16[1024,512]{1,0:T(8,128)(2,1)S(1)}, bf16[1024,512]{1,0:T(8,128)(2,1)S(1)}) custom-call(bf16[8,1024,1024]{2,1,0:T(8,128)(2,1)} %get-tuple-element.20.probs_ref, bf16[1024,1536]{1,0:T(8,128)(2,1)} %add_convert_fusion.q_ref.k_ref.v_ref, bf16[1024,1536]{1,0:T(8,128)(2,1)} %add_convert_fusion.q_ref.k_ref.v_ref, ...), custom_call_target="tpu_custom_call" | custom-call | flops 8589934592 | bytes 16777216 | tf_op jit(solution)/shard_map/attend_backward/pallas_call | solution.py:133
  679.5 1.7 copy-done.7
  681.2 8.2 convolution_convert_fusion.4
  689.5 14.0 %convolution_convert_fusion.1 = bf16[2048,2048]{1,0:T(8,128)(2,1)} fusion(bf16[1024,2048]{1,0:T(8,128)(2,1)} %all-gather.17.cloned.1.call-done, bf16[1024,2048]{1,0:T(8,128)(2,1)} %copy-done.27), kind=kOutput, calls=%fused_computation.20 | convolution fusion | flops 8594128896 | bytes 16777216 | tf_op jit(solution)/shard_map/dot_general | solution.py:36
  703.8 14.3 %convolution_convert_fusion = bf16[2048,2048]{1,0:T(8,128)(2,1)} fusion(bf16[1024,2048]{1,0:T(8,128)(2,1)} %get-tuple-element.53, bf16[1,1024,2048]{2,1,0:T(8,128)(2,1)} %all-gather.25.cloned.1.call-done), kind=kOutput, calls=%fused_computation.19 | convolution fusion | flops 8594128896 | bytes 16777216 | tf_op jit(solution)/shard_map/dot_general | solution.py:36
  718.9 11.9 convolution_convert_fusion.3
  731.1 0.9 copy-done.1
  733.0 2.4 convert_reduce_fusion.2
  735.5 6.3 reduce-scatter.12.cloned.1.call-done
  741.8 2.3 fusion.38
  744.2 0.7 concatenate.15
  745.3 7.1 convolution_convert_fusion.2
  752.5 81.4 %reduce-scatter.18.cloned.1.call-done = bf16[256,2048]{1,0:T(8,128)(2,1)} async-done(((bf16[2048,2048]{1,0:T(8,128)(2,1)}), bf16[256,2048]{1,0:T(8,128)(2,1)}) %reduce-scatter.18.cloned.1.call-update) | async-done | bytes 1048592 | tf_op jit(solution)/shard_map/reduce_scatter | solution.py:200
  833.9 4.3 all-to-all-start.5
  838.1 86.0 %reduce-scatter.20.cloned.1.call-done = bf16[256,2048]{1,0:T(8,128)(2,1)} async-done(((bf16[2048,2048]{1,0:T(8,128)(2,1)}), bf16[256,2048]{1,0:T(8,128)(2,1)}) %reduce-scatter.20.cloned.1.call-update) | async-done | bytes 1048592 | tf_op jit(solution)/shard_map/reduce_scatter | solution.py:200
  924.1 2.8 convert_element_type.147
  926.9 1.5 copy.54
  928.4 2.7 copy.60
  931.1 3.3 reshape.174
  934.4 60.3 %reduce-scatter.14.cloned.1.call-done = bf16[256,1536]{1,0:T(8,128)(2,1)} async-done(((bf16[2048,1536]{1,0:T(8,128)(2,1)}), bf16[256,1536]{1,0:T(8,128)(2,1)}) %reduce-scatter.14.cloned.1.call-update) | async-done | bytes 786448 | tf_op jit(solution)/shard_map/reduce_scatter | solution.py:200
  994.7 4.2 all-to-all-start.4
  998.9 3.1 fusion.40
  1002.0 118.6 %all-reduce.3.cloned.1.call-done = f32[32,768]{1,0:T(8,128)} async-done(((f32[32,768]{1,0:T(8,128)}), f32[32,768]{1,0:T(8,128)}) %all-reduce.3.cloned.1.call-update) | async-done | bytes 98320
  1120.6 1.3 dynamic-slice.9
  1121.9 1.3 dynamic-slice_bitcast_fusion.4
  1123.2 1.5 dynamic-slice_bitcast_fusion
  1124.7 2.7 reshape.175
  1127.5 2.2 copy.50
  1129.7 3.2 reshape.173
  1132.9 174.3 %reduce-scatter.16.cloned.1.call-done = bf16[64,2048]{1,0:T(8,128)(2,1)} async-done(((bf16[2048,2048]{1,0:T(8,128)(2,1)}), bf16[64,2048]{1,0:T(8,128)(2,1)}) %reduce-scatter.16.cloned.1.call-update) | async-done | bytes 262160 | tf_op jit(solution)/shard_map/reduce_scatter | solution.py:280
  1307.2 1.8 convert_element_type.140
  (147 shorter events, 9.8 us)
Async XLA Ops:
  7.2 122.6 %all-gather.23.cloned.1.call-start = ((), (), s32[]{:S(2)}) async-start(), calls=%async_computation.25 | async-start | bytes 5242880 | tf_op jit(solution)/shard_map/all_gather | solution.py:191
  7.9 26.5 %copy-start.8 = (bf16[64,8192]{1,0:T(8,128)(2,1)S(1)}, bf16[64,8192]{1,0:T(8,128)(2,1)}, u32[]{:S(2)}) copy-start(bf16[64,8192]{1,0:T(8,128)(2,1)} %param.25) | copy-start | bytes 3145732
  7.9 132.5 %all-gather.13.cloned.1.call-start = ((), (), s32[]{:S(2)}) async-start(), calls=%async_computation.13 | async-start | bytes 7077888 | tf_op jit(solution)/shard_map/all_gather | solution.py:197
  33.7 185.7 %all-gather.15.cloned.1.call-start = ((), (), s32[]{:S(2)}) async-start(), calls=%async_computation.14 | async-start | bytes 8650752 | tf_op jit(solution)/shard_map/all_gather | solution.py:225
  34.4 267.1 %all-gather.19.cloned.1.call-start = ((), (), s32[]{:S(2)}) async-start(), calls=%async_computation.16 | async-start | bytes 9437184 | tf_op jit(solution)/shard_map/all_gather | solution.py:197
  35.3 19.1 %copy-start.18 = (bf16[64]{0:T(256)(128)(2,1)S(1)}, bf16[64]{0:T(256)(128)(2,1)}, u32[]{:S(2)}) copy-start(bf16[64]{0:T(256)(128)(2,1)} %param.17) | copy-start | bytes 388
  35.3 19.1 %copy-start.19 = (bf16[64]{0:T(256)(128)(2,1)S(1)}, bf16[64]{0:T(256)(128)(2,1)}, u32[]{:S(2)}) copy-start(bf16[64]{0:T(256)(128)(2,1)} %param.18) | copy-start | bytes 388
  35.3 19.1 %copy-start.20 = (bf16[64]{0:T(256)(128)(2,1)S(1)}, bf16[64]{0:T(256)(128)(2,1)}, u32[]{:S(2)}) copy-start(bf16[64]{0:T(256)(128)(2,1)} %param.22) | copy-start | bytes 388
  35.3 19.1 %copy-start.21 = (bf16[64]{0:T(256)(128)(2,1)S(1)}, bf16[64]{0:T(256)(128)(2,1)}, u32[]{:S(2)}) copy-start(bf16[64]{0:T(256)(128)(2,1)} %param.23) | copy-start | bytes 388
  35.3 19.1 %copy-start.22 = (bf16[64]{0:T(256)(128)(2,1)S(1)}, bf16[64]{0:T(256)(128)(2,1)}, u32[]{:S(2)}) copy-start(bf16[64]{0:T(256)(128)(2,1)} %param.24) | copy-start | bytes 388
  35.3 19.1 %copy-start.23 = (bf16[64]{0:T(256)(128)(2,1)S(1)}, bf16[64]{0:T(256)(128)(2,1)}, u32[]{:S(2)}) copy-start(bf16[64]{0:T(256)(128)(2,1)} %param.28) | copy-start | bytes 388
  35.3 19.1 %copy-start.24 = (bf16[128]{0:T(256)(128)(2,1)S(1)}, bf16[128]{0:T(256)(128)(2,1)}, u32[]{:S(2)}) copy-start(bf16[128]{0:T(256)(128)(2,1)} %param.20) | copy-start | bytes 772
  35.3 19.1 %copy-start.25 = (bf16[256]{0:T(256)(128)(2,1)S(1)}, bf16[256]{0:T(256)(128)(2,1)}, u32[]{:S(2)}) copy-start(bf16[256]{0:T(256)(128)(2,1)} %param.26) | copy-start | bytes 1540
  35.4 86.4 %copy-start.17 = (s32[1,256]{1,0:T(1,128)S(1)}, s32[1,256]{1,0:T(1,128)}, u32[]{:S(2)}) copy-start(s32[1,256]{1,0:T(1,128)} %param.16) | copy-start | bytes 3076
  121.7 18.7 %copy-start.9 = (f32[2048]{0:T(1024)}, f32[2048]{0:T(1024)S(1)}, u32[]{:S(2)}) copy-start(f32[2048]{0:T(1024)S(1)} %mul.155) | copy-start | bytes 24580
  121.8 18.6 %copy-start.13 = (f32[2048]{0:T(1024)}, f32[2048]{0:T(1024)S(1)}, u32[]{:S(2)}) copy-start(f32[2048]{0:T(1024)S(1)} %add.144) | copy-start | bytes 24580
  129.8 3.5 copy-start.4
  133.3 19.1 %copy-start.11 = (f32[1024]{0:T(1024)}, f32[1024]{0:T(1024)S(1)}, u32[]{:S(2)}) copy-start(f32[1024]{0:T(1024)S(1)} %broadcast_multiply_fusion) | copy-start | bytes 12292
  134.5 5.9 copy-start.15
  173.4 46.0 %copy-start = (bf16[1,256,2048]{2,1,0:T(8,128)(2,1)S(1)}, bf16[1,256,2048]{2,1,0:T(8,128)(2,1)}, u32[]{:S(2)}) copy-start(bf16[1,256,2048]{2,1,0:T(8,128)(2,1)} %param.15) | copy-start | bytes 3145732
  174.7 19.4 %all-to-all-start.1 = ((bf16[4,256,512]{1,2,0:T(8,128)(2,1)}), bf16[4,256,512]{1,2,0:T(8,128)(2,1)S(1)}, u32[]{:S(2)}, u32[]{:S(2)}) async-start(bf16[4,256,512]{1,2,0:T(8,128)(2,1)} %copy.47), calls=%async_computation.1 | async-start | bytes 2097152 | tf_op jit(solution)/shard_map/all_to_all | solution.py:246
  178.3 176.8 %all-gather.17.cloned.1.call-start = ((), (), s32[]{:S(2)}) async-start(), calls=%async_computation.15 | async-start | bytes 5242880 | tf_op jit(solution)/shard_map/all_gather | solution.py:191
  194.1 25.3 %copy-start.5 = (bf16[4,256,512]{1,2,0:T(8,128)(2,1)}, bf16[4,256,512]{1,2,0:T(8,128)(2,1)S(1)}, u32[]{:S(2)}) copy-start(bf16[4,256,512]{1,2,0:T(8,128)(2,1)S(1)} %all-to-all-done.1) | copy-start | bytes 3145732
  227.3 182.1 %all-gather.25.cloned.1.call-start = ((), (), s32[]{:S(2)}) async-start(), calls=%async_computation.26 | async-start | bytes 5242880 | tf_op jit(solution)/shard_map/all_gather | solution.py:191
  227.9 265.3 %all-gather.21.cloned.1.call-start = ((), (), s32[]{:S(2)}) async-start(), calls=%async_computation.17 | async-start | bytes 9437184 | tf_op jit(solution)/shard_map/all_gather | solution.py:197
  228.7 344.7 %reduce-scatter.10.cloned.1.call-start = ((), (), s32[]{:S(2)}) async-start(), calls=%async_computation.19 | async-start | bytes 5242880 | tf_op jit(solution)/shard_map/reduce_scatter | solution.py:194
  493.2 18.3 %copy-start.26 = (bf16[2048,2048]{1,0:T(8,128)(2,1)S(1)}, bf16[2048,2048]{1,0:T(8,128)(2,1)}, u32[]{:S(2)}) copy-start(bf16[2048,2048]{1,0:T(8,128)(2,1)} %all-gather.19.cloned.1.call-done) | copy-start | bytes 25165828
  509.6 1.9 copy-start.27
  522.0 107.3 %reduce-scatter.8.cloned.1.call-start = ((), (), s32[]{:S(2)}) async-start(), calls=%async_computation.18 | async-start | bytes 5242880 | tf_op jit(solution)/shard_map/reduce_scatter | solution.py:194
  536.3 93.0 %copy-start.6 = (bf16[1,256,2048]{2,1,0:T(8,128)(2,1)S(1)}, bf16[1,256,2048]{2,1,0:T(8,128)(2,1)}, u32[]{:S(2)}) copy-start(bf16[1,256,2048]{2,1,0:T(8,128)(2,1)} %param.29) | copy-start | bytes 3145732
  536.4 205.5 %reduce-scatter.12.cloned.1.call-start = ((), (), s32[]{:S(2)}) async-start(), calls=%async_computation.20 | async-start | bytes 5242880 | tf_op jit(solution)/shard_map/reduce_scatter | solution.py:194
  633.0 6.5 copy-start.2
  657.4 23.8 %slice-start = ((s8[6291456]{0:T(1024)(128)(4,1)}), s8[4194304]{0:T(1024)(128)(4,1)S(1)}, s32[]{:S(2)}) async-start(s8[6291456]{0:T(1024)(128)(4,1)} %bitcast.170), calls=%async_computation.28 | async-start | bytes 8388608
  657.4 23.8 %slice-start.1 = ((s8[6291456]{0:T(1024)(128)(4,1)}), s8[2097152]{0:T(1024)(128)(4,1)S(1)}, s32[]{:S(2)}) async-start(s8[6291456]{0:T(1024)(128)(4,1)} %bitcast.170), calls=%async_computation.29 | async-start | bytes 4194304
  679.5 1.7 copy-start.7
  689.5 144.4 %reduce-scatter.18.cloned.1.call-start = ((), (), s32[]{:S(2)}) async-start(), calls=%async_computation.23 | async-start | bytes 9437184 | tf_op jit(solution)/shard_map/reduce_scatter | solution.py:200
  703.6 220.5 %reduce-scatter.20.cloned.1.call-start = ((), (), s32[]{:S(2)}) async-start(), calls=%async_computation.24 | async-start | bytes 9437184 | tf_op jit(solution)/shard_map/reduce_scatter | solution.py:200
  718.2 0.7 copy-start.10
  718.2 0.7 copy-start.12
  718.2 0.7 copy-start.14
  718.2 0.7 copy-start.16
  718.2 276.5 %reduce-scatter.14.cloned.1.call-start = ((), (), s32[]{:S(2)}) async-start(), calls=%async_computation.21 | async-start | bytes 7077888 | tf_op jit(solution)/shard_map/reduce_scatter | solution.py:200
  730.8 1.2 copy-start.1
  730.8 389.8 %all-reduce.3.cloned.1.call-start = ((), (), s32[]{:S(2)}) async-start(), calls=%async_computation.27 | async-start | bytes 196608
  731.0 14.3 %copy-start.3 = (f32[256,2048]{1,0:T(8,128)S(1)}, f32[256,2048]{1,0:T(8,128)}, u32[]{:S(2)}) copy-start(f32[256,2048]{1,0:T(8,128)} %copy-done.2) | copy-start | bytes 6291460
  745.0 562.2 %reduce-scatter.16.cloned.1.call-start = ((), (), s32[]{:S(2)}) async-start(), calls=%async_computation.22 | async-start | bytes 8650752 | tf_op jit(solution)/shard_map/reduce_scatter | solution.py:280
  833.9 93.1 %all-to-all-start.5 = ((bf16[4,64,2048]{2,1,0:T(8,128)(2,1)}), bf16[4,64,2048]{2,1,0:T(8,128)(2,1)}, u32[]{:S(2)}, u32[]{:S(2)}) async-start(bf16[4,64,2048]{2,1,0:T(8,128)(2,1)} %bitcast.155), calls=%async_computation.11 | async-start | bytes 2097152 | tf_op jit(solution)/shard_map/all_to_all | solution.py:160
  994.7 130.0 %all-to-all-start.4 = ((bf16[4,64,1536]{2,1,0:T(8,128)(2,1)}), bf16[4,64,1536]{2,1,0:T(8,128)(2,1)}, u32[]{:S(2)}, u32[]{:S(2)}) async-start(bf16[4,64,1536]{2,1,0:T(8,128)(2,1)} %bitcast.158), calls=%async_computation.8 | async-start | bytes 1572864 | tf_op jit(solution)/shard_map/all_to_all | solution.py:160
Sparse Core Ops, SparseCore 0:
  9.9 63.5 all-gather.22
  75.1 65.2 all-gather.12
  143.3 75.9 all-gather.14
  220.8 80.6 all-gather.18
  303.8 51.2 all-gather.16
  356.7 52.6 all-gather.24
  411.1 82.0 all-gather.20
  522.1 51.2 reduce-scatter.9
  576.6 52.6 reduce-scatter.7
  689.6 52.1 reduce-scatter.11
  744.2 89.5 reduce-scatter.17
  836.1 87.9 reduce-scatter.19
  926.5 68.1 reduce-scatter.13
  1001.6 118.9 all-reduce.2
  1122.9 184.3 reduce-scatter.15

commit v2 on v1

--- a/solution.py
+++ b/solution.py
@@ -1,3 +1,5 @@
+import functools
+
 import jax
 import jax.numpy as jnp
 from jax import lax
@@ -41,12 +43,25 @@
     return (lane >= HEAD_DIM) if half else (lane < HEAD_DIM)
 
 
-def attend_forward_kernel(slope_ref, start_ref, q_ref, k_ref, v_ref, out_ref, probs_ref):
+def stretch_rows(me_ref, index, block):
+    return pl.ds(pl.multiple_of((index ^ me_ref[0]) * block, block), block)
+
+
+def in_order(me_ref, source, target, block):
+    for index in range(source.shape[0] // block):
+        target[pl.ds(index * block, block), :] = source[stretch_rows(me_ref, index, block), :]
+
+
+def attend_forward_kernel(
+    block, me_ref, slope_ref, start_ref, q_ref, k_in, v_in, out_ref, probs_ref, k_ref, v_ref
+):
     length = q_ref.shape[0]
-    block = min(256, length)
     pair = pl.program_id(0)
+    in_order(me_ref, k_in, k_ref, block)
+    in_order(me_ref, v_in, v_ref, block)
     for index in range(length // block):
-        rows = pl.ds(index * block, block)
+        rows = stretch_rows(me_ref, index, block)
+        place = pl.ds(index * block, block)
         span = (index + 1) * block
         starts = start_ref[rows, :]
         q_place = index * block + lax.broadcasted_iota(jnp.int32, (block, span), 0)
@@ -63,25 +78,29 @@
             weights = jnp.exp(scores - top)
             total = jnp.sum(weights, axis=-1, keepdims=True)
             probs = (weights * (1.0 / total)).astype(bf16)
-            probs_ref[half, rows, :span] = probs
+            probs_ref[half, place, :span] = probs
             mixed.append(dot(probs, v_ref[:span, :]))
         out_ref[rows, :] = jnp.where(lane_mask(0), mixed[0], mixed[1]).astype(bf16)
 
 
-def attend_backward_kernel(probs_ref, q_ref, k_ref, v_ref, g_ref, dq_ref, dk_ref, dv_ref, dk_sum, dv_sum):
+def attend_backward_kernel(
+    block, me_ref, probs_ref, q_ref, k_in, v_in, g_ref, dq_ref, dk_ref, dv_ref, k_ref, v_ref, dk_sum, dv_sum
+):
     length = q_ref.shape[0]
-    block = min(256, length)
+    in_order(me_ref, k_in, k_ref, block)
+    in_order(me_ref, v_in, v_ref, block)
     dk_sum[...] = jnp.zeros_like(dk_sum)
     dv_sum[...] = jnp.zeros_like(dv_sum)
     for index in range(length // block):
-        rows = pl.ds(index * block, block)
+        rows = stretch_rows(me_ref, index, block)
+        place = pl.ds(index * block, block)
         span = (index + 1) * block
         parts = []
         for half in range(2):
             mask = lane_mask(half)
             grad = jnp.where(mask, g_ref[rows, :], bf16(0))
             query = jnp.where(mask, q_ref[rows, :] * bf16(0.125), bf16(0))
-            probs_low = probs_ref[half, rows, :span]
+            probs_low = probs_ref[half, place, :span]
             probs = probs_low.astype(f32)
             grad_probs = dot(grad, v_ref[:span, :], ((1,), (1,)))
             along = jnp.sum(probs * grad_probs, axis=-1, keepdims=True)
@@ -90,19 +109,23 @@
             dk_sum[:span, :] += dot(grad_scores, query, ((0,), (0,)))
             dv_sum[:span, :] += dot(probs_low, grad, ((0,), (0,)))
         dq_ref[rows, :] = (jnp.where(lane_mask(0), parts[0], parts[1]) * 0.125).astype(bf16)
-    dk_ref[...] = dk_sum[...].astype(bf16)
-    dv_ref[...] = dv_sum[...].astype(bf16)
-
-
-def attend_forward(slopes, starts, projected):
+    for index in range(length // block):
+        rows = stretch_rows(me_ref, index, block)
+        place = pl.ds(index * block, block)
+        dk_ref[rows, :] = dk_sum[place, :].astype(bf16)
+        dv_ref[rows, :] = dv_sum[place, :].astype(bf16)
+
+
+def attend_forward(block, me, slopes, starts, projected):
     length = projected.shape[0]
     heads = projected.shape[1] // (3 * HEAD_DIM)
     pairs = heads // 2
     column = lambda first: pl.BlockSpec((length, PAIR), lambda p: (0, first + p))
     return pl.pallas_call(
-        attend_forward_kernel,
+        functools.partial(attend_forward_kernel, block),
         grid=(pairs,),
         in_specs=[
+            pl.BlockSpec(memory_space=pltpu.SMEM),
             pl.BlockSpec(memory_space=pltpu.SMEM),
             pl.BlockSpec((length, 1), lambda p: (0, 0)),
             column(0),
@@ -114,6 +137,7 @@
             jax.ShapeDtypeStruct((length, heads * HEAD_DIM), bf16),
             jax.ShapeDtypeStruct((heads, length, length), bf16),
         ],
+        scratch_shapes=[pltpu.VMEM((length, PAIR), bf16), pltpu.VMEM((length, PAIR), bf16)],
         compiler_params=pltpu.CompilerParams(vmem_limit_bytes=50 * 2**20),
         cost_estimate=pl.CostEstimate(
             flops=4 * heads * length * length * PAIR,
@@ -121,19 +145,20 @@
             transcendentals=heads * length * length,
         ),
         name="attend_forward",
-    )(slopes, starts, projected, projected, projected)
-
-
-def attend_backward(probs, projected, grad):
+    )(me, slopes, starts, projected, projected, projected)
+
+
+def attend_backward(block, me, probs, projected, grad):
     length = projected.shape[0]
     heads = projected.shape[1] // (3 * HEAD_DIM)
     pairs = heads // 2
     column = lambda first: pl.BlockSpec((length, PAIR), lambda p: (0, first + p))
     shape = jax.ShapeDtypeStruct((length, heads * HEAD_DIM), bf16)
     return pl.pallas_call(
-        attend_backward_kernel,
+        functools.partial(attend_backward_kernel, block),
         grid=(pairs,),
         in_specs=[
+            pl.BlockSpec(memory_space=pltpu.SMEM),
             pl.BlockSpec((2, length, length), lambda p: (p, 0, 0)),
             column(0),
             column(pairs),
@@ -142,7 +167,12 @@
         ],
         out_specs=[column(0), column(0), column(0)],
         out_shape=[shape, shape, shape],
-        scratch_shapes=[pltpu.VMEM((length, PAIR), f32), pltpu.VMEM((length, PAIR), f32)],
+        scratch_shapes=[
+            pltpu.VMEM((length, PAIR), bf16),
+            pltpu.VMEM((length, PAIR), bf16),
+            pltpu.VMEM((length, PAIR), f32),
+            pltpu.VMEM((length, PAIR), f32),
+        ],
         compiler_params=pltpu.CompilerParams(vmem_limit_bytes=50 * 2**20),
         cost_estimate=pl.CostEstimate(
             flops=8 * heads * length * length * PAIR,
@@ -150,14 +180,177 @@
             transcendentals=0,
         ),
         name="attend_backward",
-    )(probs, projected, projected, projected, grad)
+    )(me, probs, projected, projected, projected, grad)
+
+
+def relative_slabs(value, me, ways, slab):
+    width = value.shape[1]
+    lane = lax.broadcasted_iota(jnp.int32, (1, width), 1)
+    bit = 1
+    while bit < ways:
+        size = bit * slab
+        upper, lower = pltpu.roll(value, size, 1), pltpu.roll(value, width - size, 1)
+        swapped = jnp.where((lane & size) != 0, upper, lower)
+        value = jnp.where((me & bit) != 0, swapped, value)
+        bit *= 2
+    return value
+
+
+def arrange_kernel(slab, spot_ref, *refs):
+    *part_refs, own_ref, other_ref, whole = refs
+    ways = len(part_refs)
+    me, core = spot_ref[0], spot_ref[1]
+    features, width = part_refs[0].shape[1], whole.shape[1]
+    for way, ref in enumerate(part_refs):
+        place = pl.ds(pl.multiple_of((me ^ way) * features, 128), features)
+        whole[:, place] = ref[...].astype(f32)
+    whole[...] = relative_slabs(whole[...], me, ways, slab)
+    size = ways * slab
+    for n in range(width // (2 * size)):
+        for which, ref in ((0, own_ref), (1, other_ref)):
+            place = pl.ds(pl.multiple_of((2 * n + (core ^ which)) * size, 128), size)
+            ref[:, n * size : (n + 1) * size] = whole[:, place].astype(bf16)
+
+
+def disarrange_kernel(slab, spot_ref, own_ref, other_ref, *refs):
+    *part_refs, whole = refs
+    ways = len(part_refs)
+    me, core = spot_ref[0], spot_ref[1]
+    features, width = part_refs[0].shape[1], whole.shape[1]
+    size = ways * slab
+    for n in range(width // (2 * size)):
+        for which, ref in ((0, own_ref), (1, other_ref)):
+            place = pl.ds(pl.multiple_of((2 * n + (core ^ which)) * size, 128), size)
+            whole[:, place] = ref[:, n * size : (n + 1) * size]
+    whole[...] = relative_slabs(whole[...], me, ways, slab)
+    for way, ref in enumerate(part_refs):
+        place = pl.ds(pl.multiple_of((me ^ way) * features, 128), features)
+        ref[...] = whole[:, place].astype(bf16)
+
+
+def arrange(slab, spot, parts):
+    rows, features = parts[0].shape
+    width = features * len(parts)
+    vmem = pl.BlockSpec(memory_space=pltpu.VMEM)
+    half = jax.ShapeDtypeStruct((rows, width // 2), bf16)
+    return pl.pallas_call(
+        functools.partial(arrange_kernel, slab),
+        in_specs=[pl.BlockSpec(memory_space=pltpu.SMEM)] + [vmem] * len(parts),
+        out_specs=[vmem, vmem],
+        out_shape=[half, half],
+        scratch_shapes=[pltpu.VMEM((rows, width), f32)],
+        compiler_params=pltpu.CompilerParams(vmem_limit_bytes=32 * 2**20),
+        cost_estimate=pl.CostEstimate(
+            flops=16 * rows * width, bytes_accessed=4 * rows * width, transcendentals=0
+        ),
+        name="arrange",
+    )(spot, *parts)
+
+
+def disarrange(slab, spot, own, other, ways):
+    rows, width = own.shape[0], 2 * own.shape[1]
+    vmem = pl.BlockSpec(memory_space=pltpu.VMEM)
+    part = jax.ShapeDtypeStruct((rows, width // ways), bf16)
+    return pl.pallas_call(
+        functools.partial(disarrange_kernel, slab),
+        in_specs=[pl.BlockSpec(memory_space=pltpu.SMEM), vmem, vmem],
+        out_specs=[vmem] * ways,
+        out_shape=[part] * ways,
+        scratch_shapes=[pltpu.VMEM((rows, width), f32)],
+        compiler_params=pltpu.CompilerParams(vmem_limit_bytes=32 * 2**20),
+        cost_estimate=pl.CostEstimate(
+            flops=16 * rows * width, bytes_accessed=6 * rows * width, transcendentals=0
+        ),
+        name="disarrange",
+    )(spot, own, other)
 
 
 ALL = ("dp", "ctx")
 
 
-def swap(value):
-    return lax.all_to_all(value, "ctx", 0, 0, tiled=True)
+def hop(value, way):
+    ways = lax.axis_size("ctx")
+    return lax.ppermute(value, "ctx", [(c, c ^ way) for c in range(ways)])
+
+
+def gather_near(value):
+    ways = lax.axis_size("ctx")
+    return [value] + [hop(value, way) for way in range(1, 3 if ways == 4 else ways)]
+
+
+def gather_far(parts):
+    if lax.axis_size("ctx") != 4:
+        return parts
+    half = parts[0].shape[0] // 2
+    far = [hop(parts[1][:half], 2), hop(parts[2][half:], 1)]
+    return parts + far
+
+
+def gather_rows(value):
+    return jnp.concatenate(gather_far(gather_near(value)), axis=0)
+
+
+def scatter_rows(far, near):
+    ways = lax.axis_size("ctx")
+    size = far.shape[0]
+    near = [near[way * size : (way + 1) * size] for way in range(ways - 1)]
+    far = far.astype(bf16)
+    if ways != 4:
+        total = near[0]
+        for way, part in enumerate(near[1:] + [far], 1):
+            total = total + hop(part.astype(bf16), way).astype(f32)
+        return total
+    half = size // 2
+    upper, lower = hop(far[:half], 1), hop(far[half:], 2)
+    nothing = jnp.zeros_like(upper)
+    one = near[1] + jnp.concatenate([nothing, lower], axis=0).astype(f32)
+    two = near[2] + jnp.concatenate([upper, nothing], axis=0).astype(f32)
+    one, two = hop(one.astype(bf16), 1), hop(two.astype(bf16), 2)
+    return near[0] + one.astype(f32) + two.astype(f32)
+
+
+def exchange(pieces):
+    return [pieces[0]] + [hop(piece, way) for way, piece in enumerate(pieces) if way]
+
+
+def place_parts(parts, axis):
+    me = lax.axis_index("ctx")
+    return jnp.concatenate(
+        [lax.select_n(me ^ place, *parts) for place in range(len(parts))], axis=axis
+    )
+
+
+def doubling(value, axis, bits):
+    size, me = lax.axis_size(axis), lax.axis_index(axis)
+    for bit in bits:
+        other = lax.ppermute(value, axis, [(d, d ^ bit) for d in range(size)])
+        upper = (me & bit) != 0
+        value = jnp.where(
+            upper,
+            jnp.concatenate([other, value], axis=0),
+            jnp.concatenate([value, other], axis=0),
+        )
+    return value
+
+
+def halving(value, axis, bits):
+    size, me = lax.axis_size(axis), lax.axis_index(axis)
+    for bit in bits:
+        half = value.shape[0] // 2
+        upper = (me & bit) != 0
+        keep = jnp.where(upper, value[half:], value[:half])
+        give = jnp.where(upper, value[:half], value[half:])
+        value = keep + lax.ppermute(give, axis, [(d, d ^ bit) for d in range(size)])
+    return value
+
+
+def bits_of(size):
+    return [1 << n for n in range(size.bit_length() - 1)]
+
+
+def core_swap(value):
+    groups = lax.axis_size("dp")
+    return lax.ppermute(value, "dp", [(d, d ^ 1) for d in range(groups)])
 
 
 def shards(
@@ -186,18 +379,58 @@
     inner_slab = contract_weight.shape[0]
     features = width // ways
     heads = HEADS // ways
-
-    def gather_ctx(value):
-        return lax.all_gather(value, "ctx", axis=0, tiled=True)
-
-    def scatter_ctx(value):
-        return lax.psum_scatter(value.astype(bf16), "ctx", scatter_dimension=0, tiled=True).astype(f32)
+    line, core, spot = groups // 2, me_dp & 1, me_dp >> 1
+
+    def rows_of(value, way):
+        return value[way * stretch : (way + 1) * stretch]
+
+    def pieces_of(value, count):
+        size = value.shape[1] // (count * ways)
+        absolute = [
+            jnp.concatenate(
+                [value[:, (n * ways + p) * size : (n * ways + p + 1) * size] for n in range(count)], 1
+            )
+            for p in range(ways)
+        ]
+        return [lax.select_n(me ^ way, *absolute) for way in range(ways)]
 
     def gather_dp(value):
         return lax.all_gather(value, "dp", axis=0, tiled=True)
 
+    def core_columns(value, core):
+        size = value.shape[1] // groups
+        return jnp.concatenate(
+            [lax.dynamic_slice_in_dim(value, (2 * n + core) * size, size, 1) for n in range(line)], 1
+        )
+
+    def core_term(left, right):
+        give = dot(core_columns(left, core ^ 1), right, ((0,), (0,))).astype(bf16)
+        keep = dot(core_columns(left, core), right, ((0,), (0,)))
+        return (keep + core_swap(give).astype(f32)).astype(bf16)
+
     def scatter_dp(value):
-        return lax.psum_scatter(value.astype(bf16), "dp", scatter_dimension=0, tiled=True)
+        return lax.psum_scatter(value, "dp", scatter_dimension=0, tiled=True)
+
+    def scatter_line(value):
+        lines = [[2 * n + core for n in range(line)] for core in range(2)]
+        return lax.psum_scatter(
+            value, "dp", scatter_dimension=0, tiled=True, axis_index_groups=lines
+        )
+
+    def split_rows(left, right, contract):
+        last = (ways - 1) * stretch
+        return dot(left[last:], right, contract), dot(left[:last], right, contract)
+
+    def own_rows(grad, count):
+        pieces = [
+            lax.dynamic_slice_in_dim(grad, (me ^ way) * slab, slab, 0) for way in range(ways)
+        ]
+        parts = exchange(pieces)
+        parts = [lax.select_n(me ^ place, *parts) for place in range(ways)]
+        size = grad.shape[1] // count
+        return jnp.concatenate(
+            [part[:, n * size : (n + 1) * size] for n in range(count) for part in parts], axis=1
+        ).astype(f32)
 
     small = (
         attention_gain,
@@ -209,7 +442,32 @@
         query_value_bias,
         expand_bias,
     )
-    packed = lax.all_gather(jnp.concatenate(small), ALL, axis=0).astype(f32)
+    every = range(ways)
+    packed = jnp.concatenate(small)[None]
+    qkv_parts = exchange(pieces_of(query_key_value, 3))
+    out_parts = [output_weight] + [
+        lax.ppermute(output_weight, "dp", [(d, (d + 2 * n) % groups) for d in range(groups)])
+        for n in range(1, line)
+    ]
+    block = residual_in[0]
+    docs_all = jnp.concatenate([hop(document_ids[0], way) if way else document_ids[0] for way in every])
+    packed = place_parts(
+        [hop(packed, way) if way else packed for way in every], 0
+    )
+    qkv_parts, out_parts, docs_all, expand_weight, block, packed = lax.optimization_barrier(
+        (qkv_parts, out_parts, docs_all, expand_weight, block, packed)
+    )
+    qkv_weight = gather_dp(place_parts(qkv_parts, 0))
+    exp_parts = exchange(pieces_of(expand_weight, groups))
+    packed = doubling(packed, "dp", bits_of(groups))
+    block_near = gather_near(block)
+    block_near, packed = lax.optimization_barrier((block_near, packed))
+    block_all = jnp.concatenate(gather_far(block_near), axis=0)
+    out_mine = jnp.concatenate(
+        [lax.select_n((spot - n + line) % line, *out_parts) for n in range(line)], axis=0
+    )
+    block_all, exp_parts, out_mine = lax.optimization_barrier((block_all, exp_parts, out_mine))
+    packed = packed.astype(f32)
     whole, at = [], 0
     for item in small:
         whole.append(packed[:, at : at + item.shape[0]].reshape(-1))
@@ -219,19 +477,10 @@
         exp_bias.reshape(groups, ways, inner_slab), me, 1, keepdims=False
     ).reshape(-1)
     qv_bias = lax.dynamic_index_in_dim(qv_bias.reshape(2, ways, features), me, 1, keepdims=False)
-
-    qkv_rows = query_key_value.reshape(slab, 3, ways, features).transpose(2, 0, 1, 3)
-    qkv_weight = gather_dp(swap(qkv_rows.reshape(ways * slab, 3 * features)))
-    out_weight = lax.all_gather(output_weight, ALL, axis=0, tiled=True)
-    exp_rows = expand_weight.reshape(slab, groups, ways, inner_slab).transpose(2, 0, 1, 3)
-    exp_weight = gather_dp(swap(exp_rows.reshape(ways * slab, groups * inner_slab)))
+    exp_weight = gather_dp(place_parts(exp_parts, 0))
     con_weight = gather_dp(contract_weight)
-
-    block = residual_in[0]
-    block_all = gather_ctx(block)
+    out_near = gather_near(out_mine)
     grad_out = output_grad[0]
-    grad_out_all = gather_ctx(grad_out)
-    docs_all = gather_ctx(document_ids[0])
     starts = (docs_all - me_dp * length)[:, None]
     slopes = jnp.exp2(
         -8.0 * ((me * heads + jnp.arange(heads, dtype=jnp.int32)).astype(f32) + 1.0) / HEADS
@@ -242,31 +491,41 @@
     normed_low = (unit_rows(block_all.astype(f32))[0] * att_gain + att_shift).astype(bf16)
     bias = jnp.concatenate([qv_bias[0], jnp.zeros((features,), f32), qv_bias[1]])
     projected = (dot(normed_low, qkv_weight) + bias).astype(bf16)
-    attended, probs = attend_forward(slopes, starts, projected)
-    attended_rows = lax.all_to_all(attended, "ctx", 0, 1, tiled=True)
-    middle = rows + dot(attended_rows, out_weight) + out_bias
+    projected, out_near = lax.optimization_barrier((projected, out_near))
+    out_own = [item.reshape(-1, slab, width) for item in gather_far(out_near)]
+    if ways == 4:
+        out_own[3:] = [jnp.concatenate(out_own[3:], axis=0)]
+    out_own = jnp.stack(out_own, axis=1).reshape(width // 2, width)
+    out_other = core_swap(out_own)
+    grad_near = gather_near(grad_out)
+    me_array = me.reshape(1)
+    attended, probs = attend_forward(stretch, me_array, slopes, starts, projected)
+    attended, grad_near = lax.optimization_barrier((attended, grad_near))
+    device = jnp.stack([me, core])
+    rows_own, rows_other = arrange(
+        slab, device, exchange([rows_of(attended, way) for way in every])
+    )
+    middle = rows + dot(rows_own, out_own) + dot(rows_other, out_other) + out_bias
 
     unit_mid, scale_mid = unit_rows(middle)
-    normed_mid = gather_ctx((unit_mid * ff_gain + ff_shift).astype(bf16))
+    normed_mid = gather_rows((unit_mid * ff_gain + ff_shift).astype(bf16))
+    normed_mid, grad_near[1] = lax.optimization_barrier((normed_mid, grad_near[1]))
+    grad_out_all = jnp.concatenate(gather_far(grad_near), axis=0)
     inner = dot(normed_mid, exp_weight) + exp_bias
     cumulative = (1.0 + lax.erf(inner * 0.7071067811865476)) * 0.5
     active = (inner * cumulative).astype(bf16)
-    result = middle + scatter_ctx(dot(active, con_weight)) + con_bias
-    layer_output = result.astype(bf16)[None]
-
-    con_grad = scatter_dp(dot(active, grad_out_all, ((0,), (0,)))).astype(f32)
+    con_term = dot(active, grad_out_all, ((0,), (0,))).astype(bf16)
+    con_term, con_weight = lax.optimization_barrier((con_term, con_weight))
+    con_sum = scatter_dp(con_term)
     grad_active = dot(grad_out_all, con_weight, ((1,), (1,)))
     density = jnp.exp(-0.5 * inner * inner) * 0.3989422804014327
     grad_inner = (grad_active * (cumulative + inner * density)).astype(bf16)
-    exp_grad = swap(scatter_dp(dot(normed_mid, grad_inner, ((0,), (0,)))))
-    exp_grad = (
-        exp_grad.reshape(ways, slab, groups, inner_slab)
-        .transpose(1, 2, 0, 3)
-        .reshape(slab, -1)
-        .astype(f32)
-    )
+    far, near = split_rows(grad_inner, exp_weight, ((1,), (1,)))
+    exp_term = dot(normed_mid, grad_inner, ((0,), (0,))).astype(bf16)
     exp_bias_term = jnp.sum(grad_inner.astype(f32), axis=0)
-    grad_normed_mid = scatter_ctx(dot(grad_inner, exp_weight, ((1,), (1,))))
+    grad_normed_mid = scatter_rows(far, near)
+    exp_term, grad_normed_mid = lax.optimization_barrier((exp_term, grad_normed_mid))
+    exp_sum = scatter_dp(exp_term)
     grad_mid_norm, ff_gain_term, ff_shift_term = norm_backward(
         grad_normed_mid, unit_mid, scale_mid, ff_gain
     )
@@ -274,23 +533,35 @@
     grad_middle = grad_out_full + grad_mid_norm
     grad_branch = grad_middle.astype(bf16)
 
-    grad_attended = dot(grad_branch, out_weight, ((1,), (1,))).astype(bf16)
-    grad_heads = lax.all_to_all(grad_attended, "ctx", 1, 0, tiled=True)
-    grad_projected = jnp.concatenate(attend_backward(probs, projected, grad_heads), axis=1)
-    out_grad = lax.psum_scatter(
-        dot(attended_rows, grad_branch, ((0,), (0,))).astype(bf16),
-        ALL,
-        scatter_dimension=0,
-        tiled=True,
-    ).astype(f32)
-    grad_normed_in = scatter_ctx(dot(grad_projected, qkv_weight, ((1,), (1,))))
-    qkv_grad = swap(scatter_dp(dot(normed_low, grad_projected, ((0,), (0,)))))
-    qkv_grad = (
-        qkv_grad.reshape(ways, slab, 3, features)
-        .transpose(1, 2, 0, 3)
-        .reshape(slab, -1)
-        .astype(f32)
-    )
+    grad_heads = disarrange(
+        slab,
+        device,
+        dot(grad_branch, out_own, ((1,), (1,))),
+        dot(grad_branch, out_other, ((1,), (1,))),
+        ways,
+    )
+    grad_heads = jnp.concatenate(exchange(grad_heads), axis=0)
+    grad_heads, active = lax.optimization_barrier((grad_heads, active))
+    result = dot(active, con_weight)
+    result = scatter_rows(result[(ways - 1) * stretch :], result)
+    layer_output = (middle + result + con_bias).astype(bf16)[None]
+    grad_projected = jnp.concatenate(
+        attend_backward(stretch, me_array, probs, projected, grad_heads), axis=1
+    )
+    qkv_term = dot(normed_low, grad_projected, ((0,), (0,))).astype(bf16)
+    qkv_term, con_sum = lax.optimization_barrier((qkv_term, con_sum))
+    give = dot(rows_other, grad_branch, ((0,), (0,))).astype(bf16)
+    out_term = dot(rows_own, grad_branch, ((0,), (0,))) + core_swap(give).astype(f32)
+    out_term = out_term.reshape(line, ways, slab, width)
+    out_term = [out_term[:, way].reshape(line * slab, width) for way in every]
+    out_term = scatter_rows(out_term[-1], jnp.concatenate(out_term[:-1], axis=0)).astype(bf16)
+    qkv_term, grad_projected, exp_sum, layer_output, out_term = lax.optimization_barrier(
+        (qkv_term, grad_projected, exp_sum, layer_output, out_term)
+    )
+    far, near = split_rows(grad_projected, qkv_weight, ((1,), (1,)))
+    grad_normed_in = scatter_rows(far, near)
+    exp_grad = own_rows(exp_sum, groups)
+    qkv_sum = scatter_dp(qkv_term)
     grad_in_norm, att_gain_term, att_shift_term = norm_backward(
         grad_normed_in, unit_in, scale_in, att_gain
     )
@@ -318,12 +589,15 @@
         exp_term,
     )
     count = groups * ways
-    sums = lax.psum_scatter(
-        jnp.concatenate([item.reshape(count, -1) for item in terms], axis=1),
-        ALL,
-        scatter_dimension=0,
-        tiled=True,
-    ).reshape(-1)
+    sums = jnp.concatenate([item.reshape(count, -1) for item in terms], axis=1)
+    out_grad = halving(out_term.reshape(line, slab, width), "dp", bits_of(groups)[:0:-1])
+    out_grad = out_grad[0].astype(f32)
+    sums = halving(sums, "dp", bits_of(groups)[::-1])
+    sums = halving(sums, "ctx", bits_of(ways)[::-1]).reshape(-1)
+    sums, qkv_sum, out_grad, exp_grad = lax.optimization_barrier(
+        (sums, qkv_sum, out_grad, exp_grad)
+    )
+    qkv_grad = own_rows(qkv_sum, 3)
     own, at = [], 0
     for item in small:
         own.append(sums[at : at + item.shape[0]])
@@ -341,7 +615,7 @@
         own[4],
         exp_grad,
         own[7],
-        con_grad,
+        con_sum.astype(f32),
         own[5],
     )
 

time: 1320 us -> 623 us (0.47)
  waiting for transfers between devices: 916 us -> 209 us
  blocking collectives: 132 us -> 0 us
  starting transfers between devices: 13.7 us -> 82.9 us
  other arithmetic: 25.1 us -> 65.5 us
  local copies, waits for them, and re-layouts: 34.7 us -> 50.9 us
    reduce_scatter x7 -> x3, waiting for transfers between devices: 499 us -> 0.02 us  [scatter_dp(): return lax.psum_scatter(value, 'dp', scatter_dimension=0, tiled=True)]
    ppermute x0 -> x71, waiting for transfers between devices: none -> 200 us  [the longest x56 130 us: hop(): return lax.ppermute(value, 'ctx', [(c, c ^ way) for c in range(ways)])]
    all_gather x3, waiting for transfers between devices: 162 us -> 9.29 us  [gather_dp(): return lax.all_gather(value, 'dp', axis=0, tiled=True)]
    unnamed x16 -> x6, waiting for transfers between devices: 121 us -> 0.1 us
    all_gather x4 -> x0, waiting for transfers between devices: 117 us -> none  [the longest x3 92.2 us: gather_ctx(): return lax.all_gather(value, 'ctx', axis=0, tiled=True)]
    ppermute x0 -> x71, starting transfers between devices: none -> 82.5 us  [the longest x56 66.9 us: hop(): return lax.ppermute(value, 'ctx', [(c, c ^ way) for c in range(ways)])]
    all_gather x2 -> x0, blocking collectives: 74.6 us -> none  [the longest x1 67 us: shards(): packed = lax.all_gather(jnp.concatenate(small), ALL, axis=0).astype(f32)]
    all_to_all x3 -> x0, blocking collectives: 57.8 us -> none  [the longest x2 40.1 us: swap(): return lax.all_to_all(value, 'ctx', 0, 0, tiled=True)]
  transfers between devices with their start and end apart: 18 -> 77, of which waited for: 15 -> 32; matrix products, arithmetic and copies ran while one was open for 11% -> 40% of each run, Pallas kernels for 2% -> 8%
where the time goes in v2:
time: 623 us; the launch traced here: 615 us
  waiting for transfers between devices  209 us (34%)
  matrix products  145 us (23%)
  starting transfers between devices  82.9 us (13%)
  other arithmetic  65.5 us (11%)
  local copies, waits for them, and re-layouts  50.9 us (8%)
  Pallas kernels  46.3 us (7%)
  between operations  15.9 us (3%)
    dot_general x17, matrix products, dot(): lax.dot_general(left, right, (contract, ((), ())), preferred_element_type...  145 us
    ppermute x56, waiting for transfers between devices, hop(): return lax.ppermute(value, 'ctx', [(c, c ^ way) for c in range(ways)])  130 us
    ppermute x56, starting transfers between devices, hop(): return lax.ppermute(value, 'ctx', [(c, c ^ way) for c in range(ways)])  66.9 us
    ppermute x7, waiting for transfers between devices, halving(): value = keep + lax.ppermute(give, axis, [(d, d ^ bit) for d in range(size)])  53 us
    unnamed x134, local copies, waits for them, and re-layouts  26.5 us
    pallas_call x1, Pallas kernels, attend_backward(): pl.pallas_call(functools.partial(attend_backward_kernel, block), grid=(pa...  22 us
    pallas_call x1, Pallas kernels, attend_forward(): pl.pallas_call(functools.partial(attend_forward_kernel, block), grid=(pai...  21.3 us
  transfers between devices with their start and end apart: 77, of which 32 were waited for; matrix products, arithmetic and copies ran while one was open for 40% of the time, Pallas kernels for 8%

profile of v2, /device:TPU:0, one launch (start us, length us, event | category | flops | bytes accessed | tf_op | source)
XLA Modules:
  0.0 614.9 jit_solution(15235946591637351678)
XLA Ops:
  7.2 4.0 collective-permute-start.8
  13.2 2.0 collective-permute-start
  15.2 5.4 concatenate.119
  21.1 2.0 collective-permute-start.10
  26.2 2.7 collective-permute-start.4
  32.2 5.0 collective-permute-done.1
  38.3 5.6 collective-permute-done.4
  56.0 6.2 %collective-permute-start.15 = (bf16[8,768]{1,0:T(8,128)(2,1)S(1)}, bf16[8,768]{1,0:T(8,128)(2,1)S(1)}, u32[]{:S(2)}, u32[]{:S(2)}) collective-permute-start(bf16[8,768]{1,0:T(8,128)(2,1)S(1)} %maximum_select_fusion.2), channel_id=1, source_target_pairs={{0,8},{4,12},{8,0},{12,4},{16,24},{20,28},{24,16},{28,20},{1,9},{5... | collective-permute-start | bytes 36872 | tf_op jit(solution)/shard_map/ppermute | solution.py:326
  62.3 4.0 collective-permute-done.15
  66.4 7.2 %collective-permute-done.16 = bf16[16,768]{1,0:T(8,128)(2,1)S(1)} collective-permute-done((bf16[16,768]{1,0:T(8,128)(2,1)S(1)}, bf16[16,768]{1,0:T(8,128)(2,1)S(1)}, u32[]{:S(2)}, u32[]{:S(2)}) %collective-permute-start.16) | collective-permute-done | bytes 24608 | tf_op jit(solution)/shard_map/ppermute | solution.py:326
  76.4 2.0 collective-permute-start.18
  80.6 12.2 %collective-permute-done.17 = bf16[128,2048]{1,0:T(8,128)(2,1)S(1)} collective-permute-done((bf16[128,2048]{1,0:T(8,128)(2,1)S(1)}, bf16[128,2048]{1,0:T(8,128)(2,1)S(1)}, u32[]{:S(2)}, u32[]{:S(2)}) %collective-permute-start.17) | collective-permute-done | bytes 524320 | tf_op jit(solution)/shard_map/ppermute | solution.py:273
  99.1 2.8 convert_reduce_fusion
  101.9 3.4 fusion.2
  105.4 9.3 %all-gather.4.cloned.1.call-done = bf16[2048,1536]{1,0:T(8,128)(2,1)} async-done(((bf16[256,1536]{1,0:T(8,128)(2,1)}), bf16[2048,1536]{1,0:T(8,128)(2,1)}) %all-gather.4.cloned.1.call-update) | async-done | bytes 6291472 | tf_op jit(solution)/shard_map/all_gather | solution.py:398
  114.7 11.8 %add_convert_fusion.q_ref.k_in.v_in = bf16[1024,1536]{1,0:T(8,128)(2,1)} fusion(bf16[2048,1536]{1,0:T(8,128)(2,1)} %all-gather.4.cloned.1.call-done, f32[1536]{0:T(1024)S(1)} %pad_maximum_fusion.9, bf16[1024,2048]{1,0:T(8,128)(2,1)} %constant_dynamic-update-slice_fusion, f32[2048]{0:T(1024)S(1)} %add.280, f32[2048]{0:T(1024)S(1)} %mul.169, ...), kind=kOutput, calls=%fused_computation.23 | convolution fusion | flops 6458179584 | bytes 13662208 | tf_op jit(solution)/shard_map/dot_general | solution.py:38
  131.3 10.9 %collective-permute-done.30 = bf16[128,2048]{1,0:T(8,128)(2,1)} collective-permute-done((bf16[128,2048]{1,0:T(8,128)(2,1)S(1)}, bf16[128,2048]{1,0:T(8,128)(2,1)}, u32[]{:S(2)}, u32[]{:S(2)}) %collective-permute-start.30) | collective-permute-done | bytes 524320 | tf_op jit(solution)/shard_map/ppermute | solution.py:273
  144.8 3.5 pad_maximum_fusion
  150.7 21.3 %attend_forward.1 = (bf16[1024,512]{1,0:T(8,128)(2,1)S(1)}, bf16[8,1024,1024]{2,1,0:T(8,128)(2,1)}) custom-call(s32[1]{0:T(128)} %bitcast.2.me_ref, f32[8]{0:T(128)S(1)} %multiply_exponential_fusion.slope_ref, s32[1024,1]{1,0:T(8,128)S(1)} %copy.29.start_ref, bf16[1024,1536]{1,0:T(8,128)(2,1)} %add_convert_fusion.q_ref.k_in.v_in, ...), custom_call_target="tpu_custom_call" | custom-call | flops 4294967296 | bytes 16777216 | tf_op jit(solution)/shard_map/attend_forward/pallas_call | solution.py:124
  178.2 5.5 collective-permute-done.26.refs_1_
  183.7 5.1 collective-permute-done.27.refs_2_
  190.4 3.7 fusion.67
  194.1 4.0 fusion.65
  202.3 21.6 %collective-permute-done.32 = bf16[256,2048]{1,0:T(8,128)(2,1)} collective-permute-done((bf16[256,2048]{1,0:T(8,128)(2,1)}, bf16[256,2048]{1,0:T(8,128)(2,1)}, u32[]{:S(2)}, u32[]{:S(2)}) %collective-permute-start.32) | collective-permute-done | bytes 1048608 | tf_op jit(solution)/shard_map/ppermute | solution.py:273
  225.7 2.3 constant_dynamic-update-slice_fusion.46
  228.0 2.0 slice.575
  233.2 2.3 constant_dynamic-update-slice_fusion.40
  235.5 2.3 constant_dynamic-update-slice_fusion.39
  238.7 13.4 %collective-permute-done.35 = bf16[128,2048]{1,0:T(8,128)(2,1)S(1)} collective-permute-done((bf16[128,2048]{1,0:T(8,128)(2,1)S(1)}, bf16[128,2048]{1,0:T(8,128)(2,1)S(1)}, u32[]{:S(2)}, u32[]{:S(2)}) %collective-permute-start.35) | collective-permute-done | bytes 524320 | tf_op jit(solution)/shard_map/ppermute | solution.py:273
  255.5 15.6 %multiply_convert_fusion = (bf16[1024,2048]{1,0:T(8,128)(2,1)S(1)}, f32[1024,2048]{1,0:T(8,128)}) fusion(f32[2048]{0:T(1024)S(1)} %bitcast.98, bf16[1024,2048]{1,0:T(8,128)(2,1)} %constant_dynamic-update-slice_fusion.37, bf16[2048,2048]{1,0:T(8,128)(2,1)} %all-gather.6.cloned.1.call-done), kind=kOutput, calls=%fused_computation.17 | convolution fusion | flops 8602517504 | bytes 25174016 | tf_op jit(solution)/shard_map/dot_general | solution.py:38
  271.1 2.1 constant_dynamic-update-slice_fusion.44
  274.4 1.9 copy-done.24
  276.4 11.4 %convolution_convert_fusion.2 = bf16[2048,2048]{1,0:T(8,128)(2,1)} fusion(bf16[1024,2048]{1,0:T(8,128)(2,1)S(1)} %get-tuple-element.123, bf16[1024,2048]{1,0:T(8,128)(2,1)S(1)} %constant_dynamic-update-slice_fusion.42), kind=kOutput, calls=%fused_computation.21 | convolution fusion | flops 8594128896 | bytes 16777216 | tf_op jit(solution)/shard_map/dot_general | solution.py:38
  287.9 17.5 %convert_reduce_fusion.1 = (f32[2048]{0:T(1024)S(1)}, bf16[1024,2048]{1,0:T(8,128)(2,1)S(1)}) fusion(f32[1024,2048]{1,0:T(8,128)} %get-tuple-element.269, f32[2048]{0:T(1024)S(1)} %bitcast.99, bf16[1024,2048]{1,0:T(8,128)(2,1)} %copy-done.24, bf16[2048,2048]{1,0:T(8,128)(2,1)} %all-gather.8.cloned.1.call-done), kind=kOutput, calls=%fused_computation.15 | convolution fusion | flops 8617195520 | bytes 25182208 | tf_op jit(solution)/shard_map/dot_general | solution.py:38
  305.4 5.8 convolution_convert_fusion.5
  312.9 9.2 %fusion.12 = f32[768,2048]{1,0:T(8,128)S(1)} fusion(bf16[2048,2048]{1,0:T(8,128)(2,1)} %all-gather.6.cloned.1.call-done, bf16[1024,2048]{1,0:T(8,128)(2,1)S(1)} %get-tuple-element.273), kind=kOutput, calls=%fused_computation.26 | convolution fusion | flops 6442450944 | bytes 17825792 | tf_op jit(solution)/shard_map/dot_general | solution.py:38
  322.1 3.2 copy-done.12
  329.6 11.3 %convolution_convert_fusion.1 = bf16[2048,2048]{1,0:T(8,128)(2,1)} fusion(bf16[1024,2048]{1,0:T(8,128)(2,1)S(1)} %copy-done.25, bf16[1024,2048]{1,0:T(8,128)(2,1)S(1)} %get-tuple-element.273), kind=kOutput, calls=%fused_computation.20 | convolution fusion | flops 8594128896 | bytes 16777216 | tf_op jit(solution)/shard_map/dot_general | solution.py:38
  340.9 6.5 %collective-permute-done.41 = bf16[256,2048]{1,0:T(8,128)(2,1)} collective-permute-done((bf16[256,2048]{1,0:T(8,128)(2,1)}, bf16[256,2048]{1,0:T(8,128)(2,1)}, u32[]{:S(2)}, u32[]{:S(2)}) %collective-permute-start.41) | collective-permute-done | bytes 1048608 | tf_op jit(solution)/shard_map/ppermute | solution.py:273
  348.8 4.1 fusion.41
  356.3 2.7 multiply_reduce_fusion
  359.1 2.7 convert_reduce_fusion.5
  361.7 3.8 fusion.68.own_ref
  365.6 3.6 fusion.69.other_ref
  374.2 3.3 convolution_convert_fusion.3
  381.0 15.2 %fusion.66 = (bf16[1024,2048]{1,0:T(8,128)(2,1)S(1)}, f32[1024,2048]{1,0:T(8,128)}) fusion(bf16[1024,2048]{1,0:T(8,128)(2,1)} %copy-done.35, bf16[2048,2048]{1,0:T(8,128)(2,1)} %all-gather.8.cloned.1.call-done), kind=kOutput, calls=%fused_computation.290 | convolution fusion | flops 8592031744 | bytes 25165824 | tf_op jit(solution)/shard_map/dot_general | solution.py:38
  398.3 22.0 %attend_backward.1 = (bf16[1024,512]{1,0:T(8,128)(2,1)S(1)}, bf16[1024,512]{1,0:T(8,128)(2,1)S(1)}, bf16[1024,512]{1,0:T(8,128)(2,1)S(1)}) custom-call(s32[1]{0:T(128)} %bitcast.2.me_ref, bf16[8,1024,1024]{2,1,0:T(8,128)(2,1)} %get-tuple-element.93.probs_ref, bf16[1024,1536]{1,0:T(8,128)(2,1)} %add_convert_fusion.q_ref.k_in.v_in, ...), custom_call_target="tpu_custom_call" | custom-call | flops 8589934592 | bytes 16777216 | tf_op jit(solution)/shard_map/attend_backward/pallas_call | solution.py:157
  420.6 4.9 fusion.34
  427.6 3.6 convert_add_fusion
  435.6 24.3 %collective-permute-done.52 = bf16[128,2048]{1,0:T(8,128)(2,1)S(1)} collective-permute-done((bf16[128,2048]{1,0:T(8,128)(2,1)S(1)}, bf16[128,2048]{1,0:T(8,128)(2,1)S(1)}, u32[]{:S(2)}, u32[]{:S(2)}) %collective-permute-start.52) | collective-permute-done | bytes 524320 | tf_op jit(solution)/shard_map/ppermute | solution.py:273
  464.3 12.8 %convolution_convert_fusion = bf16[2048,1536]{1,0:T(8,128)(2,1)} fusion(bf16[1024,1536]{1,0:T(8,128)(2,1)S(1)} %constant_dynamic-update-slice_fusion.47, bf16[1024,2048]{1,0:T(8,128)(2,1)} %constant_dynamic-update-slice_fusion, f32[2048]{0:T(1024)S(1)} %copy-done.31, f32[2048]{0:T(1024)S(1)} %copy-done.27, f32[1024]{0:T(1024)S(1)} %copy-done.33, ...), kind=kOutput, calls=%fused_computation.19 | convolution fusion | flops 6458179584 | bytes 13656064 | tf_op jit(solution)/shard_map/dot_general | solution.py:38
  477.2 4.0 fusion.46
  482.4 2.0 collective-permute-done.51
  484.5 3.2 fusion.45
  487.7 2.8 convert_element_type.214
  491.0 4.6 convolution_convert_fusion.4
  505.0 7.3 %fusion.21 = f32[768,2048]{1,0:T(8,128)S(1)} fusion(bf16[2048,1536]{1,0:T(8,128)(2,1)} %all-gather.4.cloned.1.call-done, bf16[1024,1536]{1,0:T(8,128)(2,1)S(1)} %copy-done.14), kind=kOutput, calls=%fused_computation.42 | convolution fusion | flops 4831838208 | bytes 14942208 | tf_op jit(solution)/shard_map/dot_general | solution.py:38
  512.4 5.2 collective-permute-done.66
  526.2 37.0 %collective-permute-done.63 = bf16[2,64,2048]{2,1,0:T(8,128)(2,1)S(1)} collective-permute-done((bf16[2,64,2048]{2,1,0:T(8,128)(2,1)S(1)}, bf16[2,64,2048]{2,1,0:T(8,128)(2,1)S(1)}, u32[]{:S(2)}, u32[]{:S(2)}) %collective-permute-start.63) | collective-permute-done | bytes 524320 | tf_op jit(solution)/shard_map/ppermute | solution.py:343
  564.1 2.6 fusion.28
  568.3 5.0 collective-permute-done.58
  573.4 7.7 %collective-permute-done.64 = bf16[1,64,2048]{2,1,0:T(8,128)(2,1)S(1)} collective-permute-done((bf16[1,64,2048]{2,1,0:T(8,128)(2,1)S(1)}, bf16[1,64,2048]{2,1,0:T(8,128)(2,1)S(1)}, u32[]{:S(2)}, u32[]{:S(2)}) %collective-permute-start.64) | collective-permute-done | bytes 262176 | tf_op jit(solution)/shard_map/ppermute | solution.py:343
  586.0 2.1 collective-permute-done.61
  598.4 4.9 collective-permute-done.69
  (383 shorter events, 139.8 us)
Async XLA Ops:
  7.2 107.4 %all-gather.4.cloned.1.call-start = ((), (), s32[]{:S(2)}) async-start(), calls=%async_computation.3 | async-start | bytes 7077888 | tf_op jit(solution)/shard_map/all_gather | solution.py:398
  7.2 13.9 %collective-permute-start.8 = (s32[256]{0:T(256)}, s32[256]{0:T(256)S(1)}, u32[]{:S(2)}, u32[]{:S(2)}) collective-permute-start(s32[256]{0:T(256)} %bitcast.104), channel_id=1, source_target_pairs={{0,3},{1,2},{2,1},{3,0},{4,7},{5,6},{6,5},{7,4},{8,11},{9,10},{10,... | collective-permute-start | bytes 3080 | tf_op jit(solution)/shard_map/ppermute | solution.py:273
  11.2 11.9 %collective-permute-start.7 = (s32[256]{0:T(256)}, s32[256]{0:T(256)S(1)}, u32[]{:S(2)}, u32[]{:S(2)}) collective-permute-start(s32[256]{0:T(256)} %bitcast.105), channel_id=1, source_target_pairs={{0,2},{1,3},{2,0},{3,1},{4,6},{5,7},{6,4},{7,5},{8,10},{9,11},{10,... | collective-permute-start | bytes 3080 | tf_op jit(solution)/shard_map/ppermute | solution.py:273
  11.7 12.8 %collective-permute-start.6 = (s32[256]{0:T(256)}, s32[256]{0:T(256)S(1)}, u32[]{:S(2)}, u32[]{:S(2)}) collective-permute-start(s32[256]{0:T(256)} %bitcast.106), channel_id=1, source_target_pairs={{0,1},{1,0},{2,3},{3,2},{4,5},{5,4},{6,7},{7,6},{8,9},{9,8},{10,11... | collective-permute-start | bytes 3080 | tf_op jit(solution)/shard_map/ppermute | solution.py:273
  13.2 18.5 %collective-permute-start = (bf16[64,1536]{1,0:T(8,128)(2,1)S(1)}, bf16[64,1536]{1,0:T(8,128)(2,1)S(1)}, u32[]{:S(2)}, u32[]{:S(2)}) collective-permute-start(bf16[64,1536]{1,0:T(8,128)(2,1)S(1)} %select_select_fusion.26), channel_id=1, source_target_pairs={{0,1},{1,0},{2,3},{3,2},{4,5},{5,4},{6,7},{7,6},{8,9},{9,8},{10,11... | collective-permute-start | bytes 589832 | tf_op jit(solution)/shard_map/ppermute | solution.py:273
  24.6 13.7 %collective-permute-start.3 = (bf16[64,2048]{1,0:T(8,128)(2,1)S(1)}, bf16[64,2048]{1,0:T(8,128)(2,1)S(1)}, u32[]{:S(2)}, u32[]{:S(2)}) collective-permute-start(bf16[64,2048]{1,0:T(8,128)(2,1)S(1)} %copy-done.22), channel_id=1, source_target_pairs={{0,8},{4,12},{8,16},{12,20},{16,24},{20,28},{24,0},{28,4},{1,9},{5... | collective-permute-start | bytes 786440 | tf_op jit(solution)/shard_map/ppermute | solution.py:449
  26.2 17.7 %collective-permute-start.4 = (bf16[64,2048]{1,0:T(8,128)(2,1)S(1)}, bf16[64,2048]{1,0:T(8,128)(2,1)S(1)}, u32[]{:S(2)}, u32[]{:S(2)}) collective-permute-start(bf16[64,2048]{1,0:T(8,128)(2,1)S(1)} %copy-done.22), channel_id=1, source_target_pairs={{0,16},{4,20},{8,24},{12,28},{16,0},{20,4},{24,8},{28,12},{1,17},{... | collective-permute-start | bytes 786440 | tf_op jit(solution)/shard_map/ppermute | solution.py:449
  28.8 15.0 %collective-permute-start.5 = (bf16[64,2048]{1,0:T(8,128)(2,1)S(1)}, bf16[64,2048]{1,0:T(8,128)(2,1)S(1)}, u32[]{:S(2)}, u32[]{:S(2)}) collective-permute-start(bf16[64,2048]{1,0:T(8,128)(2,1)S(1)} %copy-done.22), channel_id=1, source_target_pairs={{0,24},{4,28},{8,0},{12,4},{16,8},{20,12},{24,16},{28,20},{1,25},{... | collective-permute-start | bytes 786440 | tf_op jit(solution)/shard_map/ppermute | solution.py:449
  44.9 210.6 %all-gather.6.cloned.1.call-start = ((), (), s32[]{:S(2)}) async-start(), calls=%async_computation.4 | async-start | bytes 9437184 | tf_op jit(solution)/shard_map/all_gather | solution.py:398
  45.0 28.6 %collective-permute-start.12 = (bf16[256,2048]{1,0:T(8,128)(2,1)S(1)}, bf16[256,2048]{1,0:T(8,128)(2,1)S(1)}, u32[]{:S(2)}, u32[]{:S(2)}) collective-permute-start(bf16[256,2048]{1,0:T(8,128)(2,1)S(1)} %bitcast.82), channel_id=1, source_target_pairs={{0,1},{1,0},{2,3},{3,2},{4,5},{5,4},{6,7},{7,6},{8,9},{9,8},{10,11... | collective-permute-start | bytes 3145736 | tf_op jit(solution)/shard_map/ppermute | solution.py:273
  45.6 28.1 %collective-permute-start.13 = (bf16[256,2048]{1,0:T(8,128)(2,1)S(1)}, bf16[256,2048]{1,0:T(8,128)(2,1)S(1)}, u32[]{:S(2)}, u32[]{:S(2)}) collective-permute-start(bf16[256,2048]{1,0:T(8,128)(2,1)S(1)} %bitcast.83), channel_id=1, source_target_pairs={{0,2},{1,3},{2,0},{3,1},{4,6},{5,7},{6,4},{7,5},{8,10},{9,11},{10,... | collective-permute-start | bytes 3145736 | tf_op jit(solution)/shard_map/ppermute | solution.py:273
  47.1 8.8 %collective-permute-start.14 = (bf16[4,768]{1,0:T(4,128)(2,1)S(1)}, bf16[4,768]{1,0:T(4,128)(2,1)S(1)}, u32[]{:S(2)}, u32[]{:S(2)}) collective-permute-start(bf16[4,768]{1,0:T(4,128)(2,1)S(1)} %pad_maximum_fusion.10), channel_id=1, source_target_pairs={{0,4},{4,0},{8,12},{12,8},{16,20},{20,16},{24,28},{28,24},{1,5},{5... | collective-permute-start | bytes 18440 | tf_op jit(solution)/shard_map/ppermute | solution.py:326
  53.9 40.6 %collective-permute-start.19 = (bf16[64,2048]{1,0:T(8,128)(2,1)S(1)}, bf16[64,2048]{1,0:T(8,128)(2,1)S(1)}, u32[]{:S(2)}, u32[]{:S(2)}) collective-permute-start(bf16[64,2048]{1,0:T(8,128)(2,1)S(1)} %get-tuple-element.193), channel_id=1, source_target_pairs={{0,1},{1,0},{2,3},{3,2},{4,5},{5,4},{6,7},{7,6},{8,9},{9,8},{10,11... | collective-permute-start | bytes 786440 | tf_op jit(solution)/shard_map/ppermute | solution.py:273
  55.4 39.0 %collective-permute-start.20 = (bf16[64,2048]{1,0:T(8,128)(2,1)S(1)}, bf16[64,2048]{1,0:T(8,128)(2,1)S(1)}, u32[]{:S(2)}, u32[]{:S(2)}) collective-permute-start(bf16[64,2048]{1,0:T(8,128)(2,1)S(1)} %get-tuple-element.192), channel_id=1, source_target_pairs={{0,2},{1,3},{2,0},{3,1},{4,6},{5,7},{6,4},{7,5},{8,10},{9,11},{10,... | collective-permute-start | bytes 786440 | tf_op jit(solution)/shard_map/ppermute | solution.py:273
  56.0 10.4 %collective-permute-start.15 = (bf16[8,768]{1,0:T(8,128)(2,1)S(1)}, bf16[8,768]{1,0:T(8,128)(2,1)S(1)}, u32[]{:S(2)}, u32[]{:S(2)}) collective-permute-start(bf16[8,768]{1,0:T(8,128)(2,1)S(1)} %maximum_select_fusion.2), channel_id=1, source_target_pairs={{0,8},{4,12},{8,0},{12,4},{16,24},{20,28},{24,16},{28,20},{1,9},{5... | collective-permute-start | bytes 36872 | tf_op jit(solution)/shard_map/ppermute | solution.py:326
  73.6 20.8 %collective-permute-start.21 = (bf16[64,2048]{1,0:T(8,128)(2,1)S(1)}, bf16[64,2048]{1,0:T(8,128)(2,1)S(1)}, u32[]{:S(2)}, u32[]{:S(2)}) collective-permute-start(bf16[64,2048]{1,0:T(8,128)(2,1)S(1)} %get-tuple-element.191), channel_id=1, source_target_pairs={{0,3},{1,2},{2,1},{3,0},{4,7},{5,6},{6,5},{7,4},{8,11},{9,10},{10,... | collective-permute-start | bytes 786440 | tf_op jit(solution)/shard_map/ppermute | solution.py:273
  73.7 19.1 %collective-permute-start.17 = (bf16[128,2048]{1,0:T(8,128)(2,1)S(1)}, bf16[128,2048]{1,0:T(8,128)(2,1)S(1)}, u32[]{:S(2)}, u32[]{:S(2)}) collective-permute-start(bf16[128,2048]{1,0:T(8,128)(2,1)S(1)} %slice.524), channel_id=1, source_target_pairs={{0,2},{1,3},{2,0},{3,1},{4,6},{5,7},{6,4},{7,5},{8,10},{9,11},{10,... | collective-permute-start | bytes 1572872 | tf_op jit(solution)/shard_map/ppermute | solution.py:273
  76.4 17.2 %collective-permute-start.18 = (bf16[128,2048]{1,0:T(8,128)(2,1)S(1)}, bf16[128,2048]{1,0:T(8,128)(2,1)S(1)}, u32[]{:S(2)}, u32[]{:S(2)}) collective-permute-start(bf16[128,2048]{1,0:T(8,128)(2,1)S(1)} %slice.525), channel_id=1, source_target_pairs={{0,1},{1,0},{2,3},{3,2},{4,5},{5,4},{6,7},{7,6},{8,9},{9,8},{10,11... | collective-permute-start | bytes 1572872 | tf_op jit(solution)/shard_map/ppermute | solution.py:273
  95.7 192.1 %all-gather.8.cloned.1.call-start = ((), (), s32[]{:S(2)}) async-start(), calls=%async_computation.5 | async-start | bytes 9437184 | tf_op jit(solution)/shard_map/all_gather | solution.py:398
  96.0 30.5 %collective-permute-start.22 = (bf16[256,2048]{1,0:T(8,128)(2,1)S(1)}, bf16[256,2048]{1,0:T(8,128)(2,1)S(1)}, u32[]{:S(2)}, u32[]{:S(2)}) collective-permute-start(bf16[256,2048]{1,0:T(8,128)(2,1)S(1)} %pad_maximum_fusion.1), channel_id=1, source_target_pairs={{0,1},{1,0},{2,3},{3,2},{4,5},{5,4},{6,7},{7,6},{8,9},{9,8},{10,11... | collective-permute-start | bytes 3145736 | tf_op jit(solution)/shard_map/ppermute | solution.py:273
  97.6 28.9 %collective-permute-start.23 = (bf16[256,2048]{1,0:T(8,128)(2,1)S(1)}, bf16[256,2048]{1,0:T(8,128)(2,1)}, u32[]{:S(2)}, u32[]{:S(2)}) collective-permute-start(bf16[256,2048]{1,0:T(8,128)(2,1)S(1)} %pad_maximum_fusion.1), channel_id=1, source_target_pairs={{0,2},{1,3},{2,0},{3,1},{4,6},{5,7},{6,4},{7,5},{8,10},{9,11},{10,... | collective-permute-start | bytes 3145736 | tf_op jit(solution)/shard_map/ppermute | solution.py:273
  128.0 14.2 %collective-permute-start.30 = (bf16[128,2048]{1,0:T(8,128)(2,1)S(1)}, bf16[128,2048]{1,0:T(8,128)(2,1)}, u32[]{:S(2)}, u32[]{:S(2)}) collective-permute-start(bf16[128,2048]{1,0:T(8,128)(2,1)S(1)} %slice.568), channel_id=1, source_target_pairs={{0,1},{1,0},{2,3},{3,2},{4,5},{5,4},{6,7},{7,6},{8,9},{9,8},{10,11... | collective-permute-start | bytes 1572872 | tf_op jit(solution)/shard_map/ppermute | solution.py:273
  129.5 14.0 %collective-permute-start.29 = (bf16[128,2048]{1,0:T(8,128)(2,1)S(1)}, bf16[128,2048]{1,0:T(8,128)(2,1)}, u32[]{:S(2)}, u32[]{:S(2)}) collective-permute-start(bf16[128,2048]{1,0:T(8,128)(2,1)S(1)} %slice.567), channel_id=1, source_target_pairs={{0,2},{1,3},{2,0},{3,1},{4,6},{5,7},{6,4},{7,5},{8,10},{9,11},{10,... | collective-permute-start | bytes 1572872 | tf_op jit(solution)/shard_map/ppermute | solution.py:273
  131.1 356.6 %reduce-scatter.4.cloned.1.call-start = ((), (), s32[]{:S(2)}) async-start(), calls=%async_computation.6 | async-start | bytes 9437184 | tf_op jit(solution)/shard_map/reduce_scatter | solution.py:412
  148.3 42.0 %collective-permute-start.31 = (bf16[1024,2048]{1,0:T(8,128)(2,1)}, bf16[1024,2048]{1,0:T(8,128)(2,1)}, u32[]{:S(2)}, u32[]{:S(2)}) collective-permute-start(bf16[1024,2048]{1,0:T(8,128)(2,1)} %bitcast.14), channel_id=1, source_target_pairs={{0,4},{4,0},{8,12},{12,8},{16,20},{20,16},{24,28},{28,24},{1,5},{5... | collective-permute-start | bytes 12582920 | tf_op jit(solution)/shard_map/ppermute | solution.py:353
  148.3 25.6 %collective-permute-start.24 = (bf16[256,2048]{1,0:T(8,128)(2,1)S(1)}, bf16[256,2048]{1,0:T(8,128)(2,1)S(1)}, u32[]{:S(2)}, u32[]{:S(2)}) collective-permute-start(bf16[256,2048]{1,0:T(8,128)(2,1)S(1)} %bitcast.88), channel_id=1, source_target_pairs={{0,1},{1,0},{2,3},{3,2},{4,5},{5,4},{6,7},{7,6},{8,9},{9,8},{10,11... | collective-permute-start | bytes 3145736 | tf_op jit(solution)/shard_map/ppermute | solution.py:273
  149.0 25.3 %collective-permute-start.25 = (bf16[256,2048]{1,0:T(8,128)(2,1)S(1)}, bf16[256,2048]{1,0:T(8,128)(2,1)}, u32[]{:S(2)}, u32[]{:S(2)}) collective-permute-start(bf16[256,2048]{1,0:T(8,128)(2,1)S(1)} %bitcast.89), channel_id=1, source_target_pairs={{0,2},{1,3},{2,0},{3,1},{4,6},{5,7},{6,4},{7,5},{8,10},{9,11},{10,... | collective-permute-start | bytes 3145736 | tf_op jit(solution)/shard_map/ppermute | solution.py:273
  174.4 9.3 %collective-permute-start.26 = (bf16[256,512]{1,0:T(8,128)(2,1)S(1)}, bf16[256,512]{1,0:T(8,128)(2,1)S(1)}, u32[]{:S(2)}, u32[]{:S(2)}) collective-permute-start(bf16[256,512]{1,0:T(8,128)(2,1)S(1)} %get-tuple-element.185), channel_id=1, source_target_pairs={{0,1},{1,0},{2,3},{3,2},{4,5},{5,4},{6,7},{7,6},{8,9},{9,8},{10,11... | collective-permute-start | bytes 786440 | tf_op jit(solution)/shard_map/ppermute | solution.py:273
  175.9 12.9 %collective-permute-start.27 = (bf16[256,512]{1,0:T(8,128)(2,1)S(1)}, bf16[256,512]{1,0:T(8,128)(2,1)S(1)}, u32[]{:S(2)}, u32[]{:S(2)}) collective-permute-start(bf16[256,512]{1,0:T(8,128)(2,1)S(1)} %get-tuple-element.184), channel_id=1, source_target_pairs={{0,2},{1,3},{2,0},{3,1},{4,6},{5,7},{6,4},{7,5},{8,10},{9,11},{10,... | collective-permute-start | bytes 786440 | tf_op jit(solution)/shard_map/ppermute | solution.py:273
  177.4 11.4 %collective-permute-start.28 = (bf16[256,512]{1,0:T(8,128)(2,1)S(1)}, bf16[256,512]{1,0:T(8,128)(2,1)S(1)}, u32[]{:S(2)}, u32[]{:S(2)}) collective-permute-start(bf16[256,512]{1,0:T(8,128)(2,1)S(1)} %get-tuple-element.183), channel_id=1, source_target_pairs={{0,3},{1,2},{2,1},{3,0},{4,7},{5,6},{6,5},{7,4},{8,11},{9,10},{10,... | collective-permute-start | bytes 786440 | tf_op jit(solution)/shard_map/ppermute | solution.py:273
  200.3 23.7 %collective-permute-start.32 = (bf16[256,2048]{1,0:T(8,128)(2,1)}, bf16[256,2048]{1,0:T(8,128)(2,1)}, u32[]{:S(2)}, u32[]{:S(2)}) collective-permute-start(bf16[256,2048]{1,0:T(8,128)(2,1)} %get-tuple-element.147), channel_id=1, source_target_pairs={{0,1},{1,0},{2,3},{3,2},{4,5},{5,4},{6,7},{7,6},{8,9},{9,8},{10,11... | collective-permute-start | bytes 3145736 | tf_op jit(solution)/shard_map/ppermute | solution.py:273
  201.5 30.0 %collective-permute-start.33 = (bf16[256,2048]{1,0:T(8,128)(2,1)}, bf16[256,2048]{1,0:T(8,128)(2,1)}, u32[]{:S(2)}, u32[]{:S(2)}) collective-permute-start(bf16[256,2048]{1,0:T(8,128)(2,1)} %get-tuple-element.147), channel_id=1, source_target_pairs={{0,2},{1,3},{2,0},{3,1},{4,6},{5,7},{6,4},{7,5},{8,10},{9,11},{10,... | collective-permute-start | bytes 3145736 | tf_op jit(solution)/shard_map/ppermute | solution.py:273
  225.0 12.8 %collective-permute-start.34 = (bf16[128,2048]{1,0:T(8,128)(2,1)S(1)}, bf16[128,2048]{1,0:T(8,128)(2,1)S(1)}, u32[]{:S(2)}, u32[]{:S(2)}) collective-permute-start(bf16[128,2048]{1,0:T(8,128)(2,1)S(1)} %slice.680), channel_id=1, source_target_pairs={{0,2},{1,3},{2,0},{3,1},{4,6},{5,7},{6,4},{7,5},{8,10},{9,11},{10,... | collective-permute-start | bytes 1572872 | tf_op jit(solution)/shard_map/ppermute | solution.py:273
  230.0 44.3 %collective-permute-start.37 = (bf16[128,2048]{1,0:T(8,128)(2,1)}, bf16[128,2048]{1,0:T(8,128)(2,1)S(1)}, u32[]{:S(2)}, u32[]{:S(2)}) collective-permute-start(bf16[128,2048]{1,0:T(8,128)(2,1)} %slice.575), channel_id=1, source_target_pairs={{0,1},{1,0},{2,3},{3,2},{4,5},{5,4},{6,7},{7,6},{8,9},{9,8},{10,11... | collective-permute-start | bytes 1572872 | tf_op jit(solution)/shard_map/ppermute | solution.py:273
  232.5 19.5 %collective-permute-start.35 = (bf16[128,2048]{1,0:T(8,128)(2,1)S(1)}, bf16[128,2048]{1,0:T(8,128)(2,1)S(1)}, u32[]{:S(2)}, u32[]{:S(2)}) collective-permute-start(bf16[128,2048]{1,0:T(8,128)(2,1)S(1)} %slice.681), channel_id=1, source_target_pairs={{0,1},{1,0},{2,3},{3,2},{4,5},{5,4},{6,7},{7,6},{8,9},{9,8},{10,11... | collective-permute-start | bytes 1572872 | tf_op jit(solution)/shard_map/ppermute | solution.py:273
  253.7 19.5 %collective-permute-start.36 = (bf16[128,2048]{1,0:T(8,128)(2,1)}, bf16[128,2048]{1,0:T(8,128)(2,1)}, u32[]{:S(2)}, u32[]{:S(2)}) collective-permute-start(bf16[128,2048]{1,0:T(8,128)(2,1)} %slice.574), channel_id=1, source_target_pairs={{0,2},{1,3},{2,0},{3,1},{4,6},{5,7},{6,4},{7,5},{8,10},{9,11},{10,... | collective-permute-start | bytes 1572872 | tf_op jit(solution)/shard_map/ppermute | solution.py:273
  287.8 202.7 %reduce-scatter.6.cloned.1.call-start = ((), (), s32[]{:S(2)}) async-start(), calls=%async_computation.7 | async-start | bytes 9437184 | tf_op jit(solution)/shard_map/reduce_scatter | solution.py:412
  311.3 10.8 %collective-permute-start.38 = (bf16[128,2048]{1,0:T(8,128)(2,1)S(1)}, bf16[128,2048]{1,0:T(8,128)(2,1)S(1)}, u32[]{:S(2)}, u32[]{:S(2)}) collective-permute-start(bf16[128,2048]{1,0:T(8,128)(2,1)S(1)} %get-tuple-element.177), channel_id=1, source_target_pairs={{0,2},{1,3},{2,0},{3,1},{4,6},{5,7},{6,4},{7,5},{8,10},{9,11},{10,... | collective-permute-start | bytes 1572872 | tf_op jit(solution)/shard_map/ppermute | solution.py:273
  311.3 10.8 %collective-permute-start.40 = (bf16[128,2048]{1,0:T(8,128)(2,1)S(1)}, bf16[128,2048]{1,0:T(8,128)(2,1)S(1)}, u32[]{:S(2)}, u32[]{:S(2)}) collective-permute-start(bf16[128,2048]{1,0:T(8,128)(2,1)S(1)} %get-tuple-element.178), channel_id=1, source_target_pairs={{0,1},{1,0},{2,3},{3,2},{4,5},{5,4},{6,7},{7,6},{8,9},{9,8},{10,11... | collective-permute-start | bytes 1572872 | tf_op jit(solution)/shard_map/ppermute | solution.py:273
  327.1 20.4 %collective-permute-start.41 = (bf16[256,2048]{1,0:T(8,128)(2,1)}, bf16[256,2048]{1,0:T(8,128)(2,1)}, u32[]{:S(2)}, u32[]{:S(2)}) collective-permute-start(bf16[256,2048]{1,0:T(8,128)(2,1)} %get-tuple-element.156), channel_id=1, source_target_pairs={{0,2},{1,3},{2,0},{3,1},{4,6},{5,7},{6,4},{7,5},{8,10},{9,11},{10,... | collective-permute-start | bytes 3145736 | tf_op jit(solution)/shard_map/ppermute | solution.py:273
  329.0 19.8 %collective-permute-start.39 = (bf16[256,2048]{1,0:T(8,128)(2,1)}, bf16[256,2048]{1,0:T(8,128)(2,1)}, u32[]{:S(2)}, u32[]{:S(2)}) collective-permute-start(bf16[256,2048]{1,0:T(8,128)(2,1)} %get-tuple-element.155), channel_id=1, source_target_pairs={{0,1},{1,0},{2,3},{3,2},{4,5},{5,4},{6,7},{7,6},{8,9},{9,8},{10,11... | collective-permute-start | bytes 3145736 | tf_op jit(solution)/shard_map/ppermute | solution.py:273
  352.9 238.9 %reduce-scatter.8.cloned.1.call-start = ((), (), s32[]{:S(2)}) async-start(), calls=%async_computation.8 | async-start | bytes 7077888 | tf_op jit(solution)/shard_map/reduce_scatter | solution.py:412
  370.8 9.2 %collective-permute-start.43 = (bf16[256,512]{1,0:T(8,128)(2,1)S(1)}, bf16[256,512]{1,0:T(8,128)(2,1)S(1)}, u32[]{:S(2)}, u32[]{:S(2)}) collective-permute-start(bf16[256,512]{1,0:T(8,128)(2,1)S(1)} %get-tuple-element.114), channel_id=1, source_target_pairs={{0,2},{1,3},{2,0},{3,1},{4,6},{5,7},{6,4},{7,5},{8,10},{9,11},{10,... | collective-permute-start | bytes 786440 | tf_op jit(solution)/shard_map/ppermute | solution.py:273
  377.4 50.1 %collective-permute-start.49 = (bf16[1024,2048]{1,0:T(8,128)(2,1)}, bf16[1024,2048]{1,0:T(8,128)(2,1)}, u32[]{:S(2)}, u32[]{:S(2)}) collective-permute-start(bf16[1024,2048]{1,0:T(8,128)(2,1)} %convolution_convert_fusion.3), channel_id=1, source_target_pairs={{0,4},{4,0},{8,12},{12,8},{16,20},{20,16},{24,28},{28,24},{1,5},{5... | collective-permute-start | bytes 12582920 | tf_op jit(solution)/shard_map/ppermute | solution.py:353
  396.3 24.2 %collective-permute-start.45 = (bf16[128,2048]{1,0:T(8,128)(2,1)S(1)}, bf16[128,2048]{1,0:T(8,128)(2,1)S(1)}, u32[]{:S(2)}, u32[]{:S(2)}) collective-permute-start(bf16[128,2048]{1,0:T(8,128)(2,1)S(1)} %get-tuple-element.159), channel_id=1, source_target_pairs={{0,2},{1,3},{2,0},{3,1},{4,6},{5,7},{6,4},{7,5},{8,10},{9,11},{10,... | collective-permute-start | bytes 1572872 | tf_op jit(solution)/shard_map/ppermute | solution.py:273
  398.1 22.5 %collective-permute-start.47 = (bf16[128,2048]{1,0:T(8,128)(2,1)S(1)}, bf16[128,2048]{1,0:T(8,128)(2,1)S(1)}, u32[]{:S(2)}, u32[]{:S(2)}) collective-permute-start(bf16[128,2048]{1,0:T(8,128)(2,1)S(1)} %get-tuple-element.160), channel_id=1, source_target_pairs={{0,1},{1,0},{2,3},{3,2},{4,5},{5,4},{6,7},{7,6},{8,9},{9,8},{10,11... | collective-permute-start | bytes 1572872 | tf_op jit(solution)/shard_map/ppermute | solution.py:273
  425.5 51.7 %collective-permute-start.48 = (bf16[256,2048]{1,0:T(8,128)(2,1)}, bf16[256,2048]{1,0:T(8,128)(2,1)}, u32[]{:S(2)}, u32[]{:S(2)}) collective-permute-start(bf16[256,2048]{1,0:T(8,128)(2,1)} %get-tuple-element.152), channel_id=1, source_target_pairs={{0,2},{1,3},{2,0},{3,1},{4,6},{5,7},{6,4},{7,5},{8,10},{9,11},{10,... | collective-permute-start | bytes 3145736 | tf_op jit(solution)/shard_map/ppermute | solution.py:273
  426.9 50.3 %collective-permute-start.46 = (bf16[256,2048]{1,0:T(8,128)(2,1)S(1)}, bf16[256,2048]{1,0:T(8,128)(2,1)}, u32[]{:S(2)}, u32[]{:S(2)}) collective-permute-start(bf16[256,2048]{1,0:T(8,128)(2,1)S(1)} %get-tuple-element.151), channel_id=1, source_target_pairs={{0,1},{1,0},{2,3},{3,2},{4,5},{5,4},{6,7},{7,6},{8,9},{9,8},{10,11... | collective-permute-start | bytes 3145736 | tf_op jit(solution)/shard_map/ppermute | solution.py:273
  431.9 28.0 %collective-permute-start.52 = (bf16[128,2048]{1,0:T(8,128)(2,1)S(1)}, bf16[128,2048]{1,0:T(8,128)(2,1)S(1)}, u32[]{:S(2)}, u32[]{:S(2)}) collective-permute-start(bf16[128,2048]{1,0:T(8,128)(2,1)S(1)} %bitcast.95), channel_id=1, source_target_pairs={{0,1},{1,0},{2,3},{3,2},{4,5},{5,4},{6,7},{7,6},{8,9},{9,8},{10,11... | collective-permute-start | bytes 1572872 | tf_op jit(solution)/shard_map/ppermute | solution.py:273
  433.3 28.1 %collective-permute-start.50 = (bf16[128,2048]{1,0:T(8,128)(2,1)S(1)}, bf16[128,2048]{1,0:T(8,128)(2,1)S(1)}, u32[]{:S(2)}, u32[]{:S(2)}) collective-permute-start(bf16[128,2048]{1,0:T(8,128)(2,1)S(1)} %bitcast.94), channel_id=1, source_target_pairs={{0,2},{1,3},{2,0},{3,1},{4,6},{5,7},{6,4},{7,5},{8,10},{9,11},{10,... | collective-permute-start | bytes 1572872 | tf_op jit(solution)/shard_map/ppermute | solution.py:273
  461.0 21.4 %collective-permute-start.53 = (bf16[256,2048]{1,0:T(8,128)(2,1)}, bf16[256,2048]{1,0:T(8,128)(2,1)}, u32[]{:S(2)}, u32[]{:S(2)}) collective-permute-start(bf16[256,2048]{1,0:T(8,128)(2,1)} %fusion.42), channel_id=1, source_target_pairs={{0,2},{1,3},{2,0},{3,1},{4,6},{5,7},{6,4},{7,5},{8,10},{9,11},{10,... | collective-permute-start | bytes 3145736 | tf_op jit(solution)/shard_map/ppermute | solution.py:273
  462.6 21.9 %collective-permute-start.51 = (bf16[256,2048]{1,0:T(8,128)(2,1)}, bf16[256,2048]{1,0:T(8,128)(2,1)}, u32[]{:S(2)}, u32[]{:S(2)}) collective-permute-start(bf16[256,2048]{1,0:T(8,128)(2,1)} %fusion.43), channel_id=1, source_target_pairs={{0,1},{1,0},{2,3},{3,2},{4,5},{5,4},{6,7},{7,6},{8,9},{9,8},{10,11... | collective-permute-start | bytes 3145736 | tf_op jit(solution)/shard_map/ppermute | solution.py:273
  496.6 24.2 %collective-permute-start.54 = (bf16[128,2048]{1,0:T(8,128)(2,1)}, bf16[128,2048]{1,0:T(8,128)(2,1)}, u32[]{:S(2)}, u32[]{:S(2)}) collective-permute-start(bf16[128,2048]{1,0:T(8,128)(2,1)} %get-tuple-element.175), channel_id=1, source_target_pairs={{0,2},{1,3},{2,0},{3,1},{4,6},{5,7},{6,4},{7,5},{8,10},{9,11},{10,... | collective-permute-start | bytes 1572872 | tf_op jit(solution)/shard_map/ppermute | solution.py:273
  498.4 22.4 %collective-permute-start.56 = (bf16[128,2048]{1,0:T(8,128)(2,1)}, bf16[128,2048]{1,0:T(8,128)(2,1)}, u32[]{:S(2)}, u32[]{:S(2)}) collective-permute-start(bf16[128,2048]{1,0:T(8,128)(2,1)} %get-tuple-element.176), channel_id=1, source_target_pairs={{0,1},{1,0},{2,3},{3,2},{4,5},{5,4},{6,7},{7,6},{8,9},{9,8},{10,11... | collective-permute-start | bytes 1572872 | tf_op jit(solution)/shard_map/ppermute | solution.py:273
  501.4 16.2 %collective-permute-start.66 = (bf16[64,2048]{1,0:T(8,128)(2,1)S(1)}, bf16[64,2048]{1,0:T(8,128)(2,1)S(1)}, u32[]{:S(2)}, u32[]{:S(2)}) collective-permute-start(bf16[64,2048]{1,0:T(8,128)(2,1)S(1)} %get-tuple-element.171), channel_id=1, source_target_pairs={{0,2},{1,3},{2,0},{3,1},{4,6},{5,7},{6,4},{7,5},{8,10},{9,11},{10,... | collective-permute-start | bytes 786440 | tf_op jit(solution)/shard_map/ppermute | solution.py:273
  501.8 15.8 %collective-permute-start.67 = (bf16[64,2048]{1,0:T(8,128)(2,1)S(1)}, bf16[64,2048]{1,0:T(8,128)(2,1)S(1)}, u32[]{:S(2)}, u32[]{:S(2)}) collective-permute-start(bf16[64,2048]{1,0:T(8,128)(2,1)S(1)} %get-tuple-element.170), channel_id=1, source_target_pairs={{0,3},{1,2},{2,1},{3,0},{4,7},{5,6},{6,5},{7,4},{8,11},{9,10},{10,... | collective-permute-start | bytes 786440 | tf_op jit(solution)/shard_map/ppermute | solution.py:273
  503.3 15.9 %collective-permute-start.65 = (bf16[64,2048]{1,0:T(8,128)(2,1)S(1)}, bf16[64,2048]{1,0:T(8,128)(2,1)S(1)}, u32[]{:S(2)}, u32[]{:S(2)}) collective-permute-start(bf16[64,2048]{1,0:T(8,128)(2,1)S(1)} %get-tuple-element.169), channel_id=1, source_target_pairs={{0,1},{1,0},{2,3},{3,2},{4,5},{5,4},{6,7},{7,6},{8,9},{9,8},{10,11... | collective-permute-start | bytes 786440 | tf_op jit(solution)/shard_map/ppermute | solution.py:273
  517.6 45.6 %collective-permute-start.63 = (bf16[2,64,2048]{2,1,0:T(8,128)(2,1)S(1)}, bf16[2,64,2048]{2,1,0:T(8,128)(2,1)S(1)}, u32[]{:S(2)}, u32[]{:S(2)}) collective-permute-start(bf16[2,64,2048]{2,1,0:T(8,128)(2,1)S(1)} %bitcast.93), channel_id=1, source_target_pairs={{0,16},{4,20},{8,24},{12,28},{16,0},{20,4},{24,8},{28,12},{1,17},{... | collective-permute-start | bytes 1572872 | tf_op jit(solution)/shard_map/ppermute | solution.py:343
  522.6 41.5 %collective-permute-start.57 = (bf16[256,2048]{1,0:T(8,128)(2,1)S(1)}, bf16[256,2048]{1,0:T(8,128)(2,1)S(1)}, u32[]{:S(2)}, u32[]{:S(2)}) collective-permute-start(bf16[256,2048]{1,0:T(8,128)(2,1)S(1)} %get-tuple-element.154), channel_id=1, source_target_pairs={{0,2},{1,3},{2,0},{3,1},{4,6},{5,7},{6,4},{7,5},{8,10},{9,11},{10,... | collective-permute-start | bytes 3145736 | tf_op jit(solution)/shard_map/ppermute | solution.py:273
  522.9 41.2 %collective-permute-start.55 = (bf16[256,2048]{1,0:T(8,128)(2,1)S(1)}, bf16[256,2048]{1,0:T(8,128)(2,1)S(1)}, u32[]{:S(2)}, u32[]{:S(2)}) collective-permute-start(bf16[256,2048]{1,0:T(8,128)(2,1)S(1)} %get-tuple-element.153), channel_id=1, source_target_pairs={{0,1},{1,0},{2,3},{3,2},{4,5},{5,4},{6,7},{7,6},{8,9},{9,8},{10,11... | collective-permute-start | bytes 3145736 | tf_op jit(solution)/shard_map/ppermute | solution.py:273
  568.2 12.9 %collective-permute-start.64 = (bf16[1,64,2048]{2,1,0:T(8,128)(2,1)S(1)}, bf16[1,64,2048]{2,1,0:T(8,128)(2,1)S(1)}, u32[]{:S(2)}, u32[]{:S(2)}) collective-permute-start(bf16[1,64,2048]{2,1,0:T(8,128)(2,1)S(1)} %broadcast_select_fusion.2), channel_id=1, source_target_pairs={{0,8},{4,12},{8,0},{12,4},{16,24},{20,28},{24,16},{28,20},{1,9},{5... | collective-permute-start | bytes 786440 | tf_op jit(solution)/shard_map/ppermute | solution.py:343
  573.4 9.7 %collective-permute-start.59 = (f32[8,768]{1,0:T(8,128)S(1)}, f32[8,768]{1,0:T(8,128)S(1)}, u32[]{:S(2)}, u32[]{:S(2)}) collective-permute-start(f32[8,768]{1,0:T(8,128)S(1)} %slice_select_fusion.1), channel_id=1, source_target_pairs={{0,8},{4,12},{8,0},{12,4},{16,24},{20,28},{24,16},{28,20},{1,9},{5... | collective-permute-start | bytes 73736 | tf_op jit(solution)/shard_map/ppermute | solution.py:343
  594.1 9.2 %collective-permute-start.69 = (bf16[64,1536]{1,0:T(8,128)(2,1)S(1)}, bf16[64,1536]{1,0:T(8,128)(2,1)S(1)}, u32[]{:S(2)}, u32[]{:S(2)}) collective-permute-start(bf16[64,1536]{1,0:T(8,128)(2,1)S(1)} %get-tuple-element.229), channel_id=1, source_target_pairs={{0,2},{1,3},{2,0},{3,1},{4,6},{5,7},{6,4},{7,5},{8,10},{9,11},{10,... | collective-permute-start | bytes 589832 | tf_op jit(solution)/shard_map/ppermute | solution.py:273
  596.0 8.3 %collective-permute-start.70 = (bf16[64,1536]{1,0:T(8,128)(2,1)S(1)}, bf16[64,1536]{1,0:T(8,128)(2,1)S(1)}, u32[]{:S(2)}, u32[]{:S(2)}) collective-permute-start(bf16[64,1536]{1,0:T(8,128)(2,1)S(1)} %get-tuple-element.228), channel_id=1, source_target_pairs={{0,3},{1,2},{2,1},{3,0},{4,7},{5,6},{6,5},{7,4},{8,11},{9,10},{10,... | collective-permute-start | bytes 589832 | tf_op jit(solution)/shard_map/ppermute | solution.py:273
  (49 other events, 831.7 us)
Sparse Core Ops, SparseCore 0:
  45.0 69.5 all-gather.3
  116.8 80.6 all-gather.5
  199.1 80.5 all-gather.7
  288.0 87.3 reduce-scatter.3
  377.5 87.9 reduce-scatter.5
  500.4 86.0 reduce-scatter.7

commit v3 on v2

--- a/solution.py
+++ b/solution.py
@@ -265,6 +265,55 @@
     )(spot, own, other)
 
 
+def lay_kernel(count, spot_ref, *refs):
+    *part_refs, out_ref = refs
+    ways = len(part_refs)
+    size = part_refs[0].shape[1] // count
+    for way, ref in enumerate(part_refs):
+        for n in range(count):
+            place = pl.multiple_of((n * ways + (way ^ spot_ref[0])) * size, 128)
+            out_ref[:, pl.ds(place, size)] = ref[:, n * size : (n + 1) * size].astype(f32)
+
+
+def lay(count, spot, parts):
+    rows, width = parts[0].shape[0], parts[0].shape[1] * len(parts)
+    vmem = pl.BlockSpec(memory_space=pltpu.VMEM)
+    return pl.pallas_call(
+        functools.partial(lay_kernel, count),
+        in_specs=[pl.BlockSpec(memory_space=pltpu.SMEM)] + [vmem] * len(parts),
+        out_specs=vmem,
+        out_shape=jax.ShapeDtypeStruct((rows, width), f32),
+        compiler_params=pltpu.CompilerParams(vmem_limit_bytes=32 * 2**20),
+        cost_estimate=pl.CostEstimate(
+            flops=0, bytes_accessed=6 * rows * width, transcendentals=0
+        ),
+        name="lay",
+    )(spot, *parts)
+
+
+def pack_kernel(*refs):
+    *item_refs, out_ref = refs
+    width = out_ref.shape[1]
+    rows = []
+    for ref in item_refs:
+        row, rest = ref[...].astype(f32), width - ref.shape[1]
+        rows.append(jnp.concatenate([row, jnp.zeros((1, rest), f32)], axis=1) if rest else row)
+    rest = out_ref.shape[0] - len(rows)
+    rows.append(jnp.zeros((rest, width), f32))
+    out_ref[...] = jnp.concatenate(rows, axis=0).astype(bf16)
+
+
+def pack(items, width):
+    vmem = pl.BlockSpec(memory_space=pltpu.VMEM)
+    return pl.pallas_call(
+        pack_kernel,
+        in_specs=[vmem] * len(items),
+        out_specs=vmem,
+        out_shape=jax.ShapeDtypeStruct((16, width), bf16),
+        name="pack",
+    )(*[item[None] for item in items])
+
+
 ALL = ("dp", "ctx")
 
 
@@ -274,39 +323,61 @@
 
 
 def gather_near(value):
-    ways = lax.axis_size("ctx")
-    return [value] + [hop(value, way) for way in range(1, 3 if ways == 4 else ways)]
+    ways, half = lax.axis_size("ctx"), value.shape[0] // 2
+    halves = [value[:half], value[half:]]
+    return [halves] + [
+        [hop(item, way) for item in halves] for way in range(1, 3 if ways == 4 else ways)
+    ]
 
 
 def gather_far(parts):
-    if lax.axis_size("ctx") != 4:
-        return parts
-    half = parts[0].shape[0] // 2
-    far = [hop(parts[1][:half], 2), hop(parts[2][half:], 1)]
-    return parts + far
+    if lax.axis_size("ctx") == 4:
+        parts = parts + [[hop(parts[1][0], 2), hop(parts[2][1], 1)]]
+    return [item for halves in parts for item in halves]
 
 
 def gather_rows(value):
     return jnp.concatenate(gather_far(gather_near(value)), axis=0)
 
 
+def halves_of(near, ways):
+    half = near.shape[0] // (2 * ways - 2)
+    return [near[n * half : (n + 1) * half] for n in range(2 * ways - 2)]
+
+
+def scatter_far(far):
+    far, half = far.astype(bf16), far.shape[0] // 2
+    if lax.axis_size("ctx") != 4:
+        return [far[:half], far[half:]]
+    return [hop(far[:half], 1), hop(far[half:], 2)]
+
+
+def scatter_side(near):
+    ways = lax.axis_size("ctx")
+    near = halves_of(near, ways)
+    if ways != 4:
+        return [item.astype(bf16) for item in near[2:4]]
+    return [hop(near[2].astype(bf16), 1), hop(near[5].astype(bf16), 2)]
+
+
+def scatter_near(near, far, side):
+    ways = lax.axis_size("ctx")
+    near = halves_of(near, ways)
+    total = near[:2]
+    if ways != 4:
+        for n, part in enumerate(side + near[4:] + far):
+            total[n % 2] = total[n % 2] + hop(part.astype(bf16), 1 + n // 2).astype(f32)
+    else:
+        upper, lower = far
+        one = hop((near[3] + lower.astype(f32)).astype(bf16), 1)
+        two = hop((near[4] + upper.astype(f32)).astype(bf16), 2)
+        total[0] = total[0] + side[0].astype(f32) + two.astype(f32)
+        total[1] = total[1] + side[1].astype(f32) + one.astype(f32)
+    return jnp.concatenate(total, axis=0)
+
+
 def scatter_rows(far, near):
-    ways = lax.axis_size("ctx")
-    size = far.shape[0]
-    near = [near[way * size : (way + 1) * size] for way in range(ways - 1)]
-    far = far.astype(bf16)
-    if ways != 4:
-        total = near[0]
-        for way, part in enumerate(near[1:] + [far], 1):
-            total = total + hop(part.astype(bf16), way).astype(f32)
-        return total
-    half = size // 2
-    upper, lower = hop(far[:half], 1), hop(far[half:], 2)
-    nothing = jnp.zeros_like(upper)
-    one = near[1] + jnp.concatenate([nothing, lower], axis=0).astype(f32)
-    two = near[2] + jnp.concatenate([upper, nothing], axis=0).astype(f32)
-    one, two = hop(one.astype(bf16), 1), hop(two.astype(bf16), 2)
-    return near[0] + one.astype(f32) + two.astype(f32)
+    return scatter_near(near, scatter_far(far), scatter_side(near))
 
 
 def exchange(pieces):
@@ -426,8 +497,10 @@
             lax.dynamic_slice_in_dim(grad, (me ^ way) * slab, slab, 0) for way in range(ways)
         ]
         parts = exchange(pieces)
+        size = grad.shape[1] // count
+        if size % 128 == 0:
+            return lay(count, me.reshape(1), parts)
         parts = [lax.select_n(me ^ place, *parts) for place in range(ways)]
-        size = grad.shape[1] // count
         return jnp.concatenate(
             [part[:, n * size : (n + 1) * size] for n in range(count) for part in parts], axis=1
         ).astype(f32)
@@ -443,35 +516,51 @@
         expand_bias,
     )
     every = range(ways)
-    packed = jnp.concatenate(small)[None]
+    begin = (document_ids[0] - me_dp * length).reshape(-1, inner_slab)
+    kinds, lines = len(small), begin.shape[0]
+    begin = [*(begin >> 5).astype(bf16), *(begin & 31).astype(bf16)]
     qkv_parts = exchange(pieces_of(query_key_value, 3))
-    out_parts = [output_weight] + [
-        lax.ppermute(output_weight, "dp", [(d, (d + 2 * n) % groups) for d in range(groups)])
+    out_block = jnp.concatenate([output_weight, pack([*small, *begin], width)], axis=0)
+    out_parts = [out_block] + [
+        lax.ppermute(out_block, "dp", [(d, (d + 2 * n) % groups) for d in range(groups)])
         for n in range(1, line)
     ]
     block = residual_in[0]
-    docs_all = jnp.concatenate([hop(document_ids[0], way) if way else document_ids[0] for way in every])
-    packed = place_parts(
-        [hop(packed, way) if way else packed for way in every], 0
-    )
-    qkv_parts, out_parts, docs_all, expand_weight, block, packed = lax.optimization_barrier(
-        (qkv_parts, out_parts, docs_all, expand_weight, block, packed)
+    qkv_parts, out_parts, expand_weight, block = lax.optimization_barrier(
+        (qkv_parts, out_parts, expand_weight, block)
     )
     qkv_weight = gather_dp(place_parts(qkv_parts, 0))
-    exp_parts = exchange(pieces_of(expand_weight, groups))
-    packed = doubling(packed, "dp", bits_of(groups))
-    block_near = gather_near(block)
-    block_near, packed = lax.optimization_barrier((block_near, packed))
-    block_all = jnp.concatenate(gather_far(block_near), axis=0)
+    packs = [part[slab:, :inner_slab] for part in out_parts]
+    packs = [lax.select_n((spot - n + line) % line, *packs) for n in range(line)]
+    other = core_swap(jnp.concatenate(packs, axis=1))
+    packed = []
+    for n, mine in enumerate(packs):
+        theirs = other[:, n * inner_slab : (n + 1) * inner_slab]
+        packed += [jnp.where(core == 0, mine, theirs), jnp.where(core == 0, theirs, mine)]
+    packed = jnp.concatenate(packed, axis=1)
+    exp_parts = exchange(
+        [jnp.concatenate([piece, packed], axis=0) for piece in pieces_of(expand_weight, groups)]
+    )
+    block_all = gather_rows(block)
     out_mine = jnp.concatenate(
-        [lax.select_n((spot - n + line) % line, *out_parts) for n in range(line)], axis=0
+        [
+            lax.select_n((spot - n + line) % line, *[part[:slab] for part in out_parts])
+            for n in range(line)
+        ],
+        axis=0,
     )
     block_all, exp_parts, out_mine = lax.optimization_barrier((block_all, exp_parts, out_mine))
-    packed = packed.astype(f32)
-    whole, at = [], 0
-    for item in small:
-        whole.append(packed[:, at : at + item.shape[0]].reshape(-1))
-        at += item.shape[0]
+    packs = [part[slab:] for part in exp_parts]
+    exp_parts = [part[:slab] for part in exp_parts]
+    begin = [
+        lax.dynamic_slice_in_dim(part[kinds : kinds + 2 * lines], me_dp * inner_slab, inner_slab, 1)
+        for part in packs
+    ]
+    begin = [32.0 * item[:lines].astype(f32) + item[lines:].astype(f32) for item in begin]
+    starts = jnp.concatenate(begin, axis=0).astype(jnp.int32).reshape(length, 1)
+    packed = [part[:kinds].astype(f32).reshape(kinds, groups, inner_slab) for part in packs]
+    packed = jnp.stack([lax.select_n(me ^ place, *packed) for place in every], axis=2)
+    whole = [packed[n, :, :, : item.shape[0]].reshape(-1) for n, item in enumerate(small)]
     att_gain, att_shift, out_bias, ff_gain, ff_shift, con_bias, qv_bias, exp_bias = whole
     exp_bias = lax.dynamic_index_in_dim(
         exp_bias.reshape(groups, ways, inner_slab), me, 1, keepdims=False
@@ -481,7 +570,6 @@
     con_weight = gather_dp(contract_weight)
     out_near = gather_near(out_mine)
     grad_out = output_grad[0]
-    starts = (docs_all - me_dp * length)[:, None]
     slopes = jnp.exp2(
         -8.0 * ((me * heads + jnp.arange(heads, dtype=jnp.int32)).astype(f32) + 1.0) / HEADS
     )
@@ -492,15 +580,17 @@
     bias = jnp.concatenate([qv_bias[0], jnp.zeros((features,), f32), qv_bias[1]])
     projected = (dot(normed_low, qkv_weight) + bias).astype(bf16)
     projected, out_near = lax.optimization_barrier((projected, out_near))
-    out_own = [item.reshape(-1, slab, width) for item in gather_far(out_near)]
-    if ways == 4:
-        out_own[3:] = [jnp.concatenate(out_own[3:], axis=0)]
-    out_own = jnp.stack(out_own, axis=1).reshape(width // 2, width)
-    out_other = core_swap(out_own)
+    out_all = gather_far(out_near)
     grad_near = gather_near(grad_out)
     me_array = me.reshape(1)
     attended, probs = attend_forward(stretch, me_array, slopes, starts, projected)
-    attended, grad_near = lax.optimization_barrier((attended, grad_near))
+    attended, grad_near, out_all = lax.optimization_barrier((attended, grad_near, out_all))
+    out_own = [
+        jnp.concatenate([item.reshape(-1, slab, width) for item in out_all[2 * way : 2 * way + 2]])
+        for way in every
+    ]
+    out_own = jnp.stack(out_own, axis=1).reshape(width // 2, width)
+    out_other = core_swap(out_own)
     device = jnp.stack([me, core])
     rows_own, rows_other = arrange(
         slab, device, exchange([rows_of(attended, way) for way in every])
@@ -509,7 +599,7 @@
 
     unit_mid, scale_mid = unit_rows(middle)
     normed_mid = gather_rows((unit_mid * ff_gain + ff_shift).astype(bf16))
-    normed_mid, grad_near[1] = lax.optimization_barrier((normed_mid, grad_near[1]))
+    normed_mid, grad_near = lax.optimization_barrier((normed_mid, grad_near))
     grad_out_all = jnp.concatenate(gather_far(grad_near), axis=0)
     inner = dot(normed_mid, exp_weight) + exp_bias
     cumulative = (1.0 + lax.erf(inner * 0.7071067811865476)) * 0.5
@@ -533,35 +623,43 @@
     grad_middle = grad_out_full + grad_mid_norm
     grad_branch = grad_middle.astype(bf16)
 
-    grad_heads = disarrange(
-        slab,
-        device,
-        dot(grad_branch, out_own, ((1,), (1,))),
-        dot(grad_branch, out_other, ((1,), (1,))),
-        ways,
-    )
+    grad_own = dot(grad_branch, out_own, ((1,), (1,)))
+    grad_other = dot(grad_branch, out_other, ((1,), (1,)))
+    grad_heads = disarrange(slab, device, grad_own, grad_other, ways)
+    grad_heads, active, grad_branch = lax.optimization_barrier((grad_heads, active, grad_branch))
     grad_heads = jnp.concatenate(exchange(grad_heads), axis=0)
-    grad_heads, active = lax.optimization_barrier((grad_heads, active))
+    give = dot(rows_other, grad_branch, ((0,), (0,))).astype(bf16)
     result = dot(active, con_weight)
-    result = scatter_rows(result[(ways - 1) * stretch :], result)
-    layer_output = (middle + result + con_bias).astype(bf16)[None]
+    out_term = dot(rows_own, grad_branch, ((0,), (0,))) + core_swap(give).astype(f32)
+    grad_heads, out_term, result = lax.optimization_barrier((grad_heads, out_term, result))
+    last = (ways - 1) * stretch
+    result_first = (scatter_far(result[last:]), scatter_side(result[:last]))
+    out_term = out_term.reshape(line, ways, slab, width)
+    out_term = [out_term[:, way].reshape(line * slab, width) for way in every]
+    out_near = jnp.concatenate(out_term[:-1], axis=0)
+    out_first = (scatter_far(out_term[-1]), scatter_side(out_near))
     grad_projected = jnp.concatenate(
         attend_backward(stretch, me_array, probs, projected, grad_heads), axis=1
     )
     qkv_term = dot(normed_low, grad_projected, ((0,), (0,))).astype(bf16)
-    qkv_term, con_sum = lax.optimization_barrier((qkv_term, con_sum))
-    give = dot(rows_other, grad_branch, ((0,), (0,))).astype(bf16)
-    out_term = dot(rows_own, grad_branch, ((0,), (0,))) + core_swap(give).astype(f32)
-    out_term = out_term.reshape(line, ways, slab, width)
-    out_term = [out_term[:, way].reshape(line * slab, width) for way in every]
-    out_term = scatter_rows(out_term[-1], jnp.concatenate(out_term[:-1], axis=0)).astype(bf16)
-    qkv_term, grad_projected, exp_sum, layer_output, out_term = lax.optimization_barrier(
-        (qkv_term, grad_projected, exp_sum, layer_output, out_term)
-    )
-    far, near = split_rows(grad_projected, qkv_weight, ((1,), (1,)))
-    grad_normed_in = scatter_rows(far, near)
+    qkv_term, con_sum, grad_projected, out_first = lax.optimization_barrier(
+        (qkv_term, con_sum, grad_projected, out_first)
+    )
+    far = dot(grad_projected[last:], qkv_weight, ((1,), (1,))).astype(bf16)
+    far, grad_projected = lax.optimization_barrier((far, grad_projected))
+    near = dot(grad_projected[:last], qkv_weight, ((1,), (1,)))
+    first = (scatter_far(far), scatter_side(near))
+    near, out_first, result_first, exp_sum = lax.optimization_barrier(
+        (near, out_first, result_first, exp_sum)
+    )
     exp_grad = own_rows(exp_sum, groups)
+    grad_normed_in = scatter_near(near, *first)
+    out_term = scatter_near(out_near, *out_first).astype(bf16)
+    result = scatter_near(result[:last], *result_first)
+    layer_output = (middle + result + con_bias).astype(bf16)[None]
+    grad_normed_in, exp_grad = lax.optimization_barrier((grad_normed_in, exp_grad))
     qkv_sum = scatter_dp(qkv_term)
+    grad_normed_in, qkv_sum = lax.optimization_barrier((grad_normed_in, qkv_sum))
     grad_in_norm, att_gain_term, att_shift_term = norm_backward(
         grad_normed_in, unit_in, scale_in, att_gain
     )
@@ -594,9 +692,6 @@
     out_grad = out_grad[0].astype(f32)
     sums = halving(sums, "dp", bits_of(groups)[::-1])
     sums = halving(sums, "ctx", bits_of(ways)[::-1]).reshape(-1)
-    sums, qkv_sum, out_grad, exp_grad = lax.optimization_barrier(
-        (sums, qkv_sum, out_grad, exp_grad)
-    )
     qkv_grad = own_rows(qkv_sum, 3)
     own, at = [], 0
     for item in small:

time: 623 us -> 599 us (0.961)
  waiting for transfers between devices: 209 us -> 173 us
  matrix products: 145 us -> 137 us
  other arithmetic: 65.5 us -> 72.3 us
  local copies, waits for them, and re-layouts: 50.9 us -> 57.5 us
    ppermute x7, waiting for transfers between devices: 53 us -> 7.59 us  [halving(): value = keep + lax.ppermute(give, axis, [(d, d ^ bit) for d in range(size)])]
    ppermute x56 -> x66, waiting for transfers between devices: 130 us -> 157 us  [hop(): return lax.ppermute(value, 'ctx', [(c, c ^ way) for c in range(ways)])]
    ppermute x6 -> x3, waiting for transfers between devices: 16.8 us -> 5.04 us  [shards(): lax.ppermute(out_block, 'dp', [(d, (d + 2 * n) % groups) for d in range(g...]
    dot_general x17, matrix products: 145 us -> 137 us  [dot(): lax.dot_general(left, right, (contract, ((), ())), preferred_element_type...]
    ppermute x56 -> x66, starting transfers between devices: 66.9 us -> 74.2 us  [hop(): return lax.ppermute(value, 'ctx', [(c, c ^ way) for c in range(ways)])]
    convert_element_type x8 -> x7, other arithmetic: 16.7 us -> 9.58 us  [the longest x4 4.44 us: scatter_near(): two = hop((near[4] + upper.astype(f32)).astype(bf16), 2)]
    concatenate x4 -> x0, local copies, waits for them, and re-layouts: 6.26 us -> none  [the longest x1 5.41 us: shards(): packed = jnp.concatenate(small)[None]]
    slice x16 -> x18, local copies, waits for them, and re-layouts: 9.61 us -> 12.5 us  [the longest x5 10.2 us: halves_of(): return [near[n * half:(n + 1) * half] for n in range(2 * ways - 2)]]
  transfers between devices with their start and end apart: 77 -> 85, of which waited for: 32 -> 32; matrix products, arithmetic and copies ran while one was open for 40% -> 43% of each run, Pallas kernels for 8% -> 8%
where the time goes in v3:
time: 599 us; the launch traced here: 594 us
  waiting for transfers between devices  173 us (29%)
  matrix products  137 us (23%)
  starting transfers between devices  87.7 us (15%)
  other arithmetic  72.3 us (12%)
  local copies, waits for them, and re-layouts  57.5 us (10%)
  Pallas kernels  50.6 us (8%)
  between operations  15.9 us (3%)
    ppermute x66, waiting for transfers between devices, hop(): return lax.ppermute(value, 'ctx', [(c, c ^ way) for c in range(ways)])  157 us
    dot_general x17, matrix products, dot(): lax.dot_general(left, right, (contract, ((), ())), preferred_element_type...  137 us
    ppermute x66, starting transfers between devices, hop(): return lax.ppermute(value, 'ctx', [(c, c ^ way) for c in range(ways)])  74.2 us
    unnamed x145, local copies, waits for them, and re-layouts  29.1 us
    pallas_call x1, Pallas kernels, attend_backward(): pl.pallas_call(functools.partial(attend_backward_kernel, block), grid=(pa...  22 us
    pallas_call x1, Pallas kernels, attend_forward(): pl.pallas_call(functools.partial(attend_forward_kernel, block), grid=(pai...  21.4 us
  transfers between devices with their start and end apart: 85, of which 32 were waited for; matrix products, arithmetic and copies ran while one was open for 43% of the time, Pallas kernels for 8%

profile of v3, /device:TPU:0, one launch (start us, length us, event | category | flops | bytes accessed | tf_op | source)
XLA Modules:
  0.0 593.8 jit_solution(15974961283492536675)
XLA Ops:
  12.2 3.1 collective-permute-start.3
  15.2 2.6 collective-permute-start.4
  21.2 2.4 collective-permute-start.2
  25.7 2.5 collective-permute-done.2
  29.8 2.5 collective-permute-done.1
  34.1 5.0 collective-permute-done.4
  57.7 8.9 %collective-permute-done.7 = bf16[128,2048]{1,0:T(8,128)(2,1)S(1)} collective-permute-done((bf16[128,2048]{1,0:T(8,128)(2,1)S(1)}, bf16[128,2048]{1,0:T(8,128)(2,1)S(1)}, u32[]{:S(2)}, u32[]{:S(2)}) %collective-permute-start.7) | collective-permute-done | bytes 524320 | tf_op jit(solution)/shard_map/ppermute | solution.py:322
  72.6 19.4 %collective-permute-done.10 = bf16[128,2048]{1,0:T(8,128)(2,1)S(1)} collective-permute-done((bf16[128,2048]{1,0:T(8,128)(2,1)S(1)}, bf16[128,2048]{1,0:T(8,128)(2,1)S(1)}, u32[]{:S(2)}, u32[]{:S(2)}) %collective-permute-start.10) | collective-permute-done | bytes 524320 | tf_op jit(solution)/shard_map/ppermute | solution.py:322
  104.0 2.8 convert_reduce_fusion
  106.8 3.4 fusion.2
  111.3 11.8 %add_convert_fusion.q_ref.k_in.v_in = bf16[1024,1536]{1,0:T(8,128)(2,1)} fusion(bf16[2048,1536]{1,0:T(8,128)(2,1)} %all-gather.4.cloned.1.call-done, f32[1536]{0:T(1024)S(1)} %pad_maximum_fusion.26, bf16[1024,2048]{1,0:T(8,128)(2,1)} %constant_dynamic-update-slice_fusion, f32[2048]{0:T(1024)S(1)} %add.322, f32[2048]{0:T(1024)S(1)} %mul.194, ...), kind=kOutput, calls=%fused_computation.23 | convolution fusion | flops 6458179584 | bytes 13662208 | tf_op jit(solution)/shard_map/dot_general | solution.py:38
  124.6 6.6 %collective-permute-done.17 = bf16[128,2048]{1,0:T(8,128)(2,1)S(1)} collective-permute-done((bf16[128,2048]{1,0:T(8,128)(2,1)S(1)}, bf16[128,2048]{1,0:T(8,128)(2,1)S(1)}, u32[]{:S(2)}, u32[]{:S(2)}) %collective-permute-start.17) | collective-permute-done | bytes 524320 | tf_op jit(solution)/shard_map/ppermute | solution.py:322
  135.8 21.4 %attend_forward.1 = (bf16[1024,512]{1,0:T(8,128)(2,1)S(1)}, bf16[8,1024,1024]{2,1,0:T(8,128)(2,1)}) custom-call(s32[1]{0:T(128)} %bitcast.8.me_ref.spot_ref, f32[8]{0:T(128)S(1)} %multiply_exponential_fusion.slope_ref, s32[1024,1]{1,0:T(8,128)S(1)} %bitcast.130, bf16[1024,1536]{1,0:T(8,128)(2,1)} %add_convert_fusion.q_ref.k_in.v_in, ...), custom_call_target="tpu_custom_call" | custom-call | flops 4294967296 | bytes 16777216 | tf_op jit(solution)/shard_map/attend_forward/pallas_call | solution.py:124
  157.2 2.6 collective-permute-done.24
  164.6 2.3 pad_maximum_fusion
  171.8 4.6 collective-permute-done.26.refs_1_
  176.4 6.4 %collective-permute-done.27.refs_2_ = bf16[256,512]{1,0:T(8,128)(2,1)S(1)} collective-permute-done((bf16[256,512]{1,0:T(8,128)(2,1)S(1)}, bf16[256,512]{1,0:T(8,128)(2,1)S(1)}, u32[]{:S(2)}, u32[]{:S(2)}) %collective-permute-start.27) | collective-permute-done | bytes 262176 | tf_op jit(solution)/shard_map/ppermute | solution.py:322
  184.4 3.4 fusion.90
  187.9 4.1 fusion.87
  197.1 10.7 %collective-permute-done.30 = bf16[128,2048]{1,0:T(8,128)(2,1)S(1)} collective-permute-done((bf16[128,2048]{1,0:T(8,128)(2,1)S(1)}, bf16[128,2048]{1,0:T(8,128)(2,1)S(1)}, u32[]{:S(2)}, u32[]{:S(2)}) %collective-permute-start.30) | collective-permute-done | bytes 524320 | tf_op jit(solution)/shard_map/ppermute | solution.py:322
  209.9 9.1 %collective-permute-done.31 = bf16[128,2048]{1,0:T(8,128)(2,1)S(1)} collective-permute-done((bf16[128,2048]{1,0:T(8,128)(2,1)S(1)}, bf16[128,2048]{1,0:T(8,128)(2,1)S(1)}, u32[]{:S(2)}, u32[]{:S(2)}) %collective-permute-start.31) | collective-permute-done | bytes 524320 | tf_op jit(solution)/shard_map/ppermute | solution.py:322
  220.4 9.6 %collective-permute-done.34 = bf16[128,2048]{1,0:T(8,128)(2,1)S(1)} collective-permute-done((bf16[128,2048]{1,0:T(8,128)(2,1)S(1)}, bf16[128,2048]{1,0:T(8,128)(2,1)S(1)}, u32[]{:S(2)}, u32[]{:S(2)}) %collective-permute-start.34) | collective-permute-done | bytes 524320 | tf_op jit(solution)/shard_map/ppermute | solution.py:322
  233.9 1.9 constant_dynamic-update-slice_fusion.59
  235.7 15.1 %multiply_convert_fusion = (bf16[1024,2048]{1,0:T(8,128)(2,1)S(1)}, f32[1024,2048]{1,0:T(8,128)}) fusion(f32[2048]{0:T(1024)S(1)} %bitcast.150, bf16[1024,2048]{1,0:T(8,128)(2,1)} %copy-done.39, bf16[2048,2048]{1,0:T(8,128)(2,1)} %all-gather.6.cloned.1.call-done), kind=kOutput, calls=%fused_computation.17 | convolution fusion | flops 8602517504 | bytes 25174016 | tf_op jit(solution)/shard_map/dot_general | solution.py:38
  250.8 2.3 constant_dynamic-update-slice_fusion.58
  253.1 1.9 constant_dynamic-update-slice_fusion.57
  255.0 1.9 constant_dynamic-update-slice_fusion.56
  256.9 1.9 constant_dynamic-update-slice_fusion.55
  258.8 1.9 constant_dynamic-update-slice_fusion.54
  260.7 13.4 %convolution_convert_fusion.2 = bf16[2048,2048]{1,0:T(8,128)(2,1)} fusion(bf16[1024,2048]{1,0:T(8,128)(2,1)S(1)} %get-tuple-element.165, bf16[1024,2048]{1,0:T(8,128)(2,1)} %constant_dynamic-update-slice_fusion.54), kind=kOutput, calls=%fused_computation.21 | convolution fusion | flops 8594128896 | bytes 16777216 | tf_op jit(solution)/shard_map/dot_general | solution.py:38
  274.1 2.3 all-gather.8.cloned.1.call-done
  276.5 16.7 %convert_reduce_fusion.1 = (f32[2048]{0:T(1024)S(1)}, bf16[1024,2048]{1,0:T(8,128)(2,1)S(1)}) fusion(f32[1024,2048]{1,0:T(8,128)} %get-tuple-element.352, f32[2048]{0:T(1024)S(1)} %bitcast.151, bf16[1024,2048]{1,0:T(8,128)(2,1)} %constant_dynamic-update-slice_fusion.54, bf16[2048,2048]{1,0:T(8,128)(2,1)} %all-gather.8.cloned.1.call-done), kind=kOutput, calls=%fused_computation.15 | convolution fusion | flops 8617195520 | bytes 25182208 | tf_op jit(solution)/shard_map/dot_general | solution.py:38
  293.2 7.5 %convolution_convert_fusion.5 = bf16[256,2048]{1,0:T(8,128)(2,1)S(1)} fusion(bf16[2048,2048]{1,0:T(8,128)(2,1)} %all-gather.6.cloned.1.call-done, bf16[1024,2048]{1,0:T(8,128)(2,1)S(1)} %get-tuple-element.358), kind=kOutput, calls=%fused_computation.36 | convolution fusion | flops 2148007936 | bytes 10485760 | tf_op jit(solution)/shard_map/dot_general | solution.py:38
  303.9 10.2 %fusion.88 = (bf16[768,2048]{1,0:T(8,128)(2,1)S(1)}, f32[768,2048]{1,0:T(8,128)S(1)}) fusion(bf16[2048,2048]{1,0:T(8,128)(2,1)} %all-gather.6.cloned.1.call-done, bf16[1024,2048]{1,0:T(8,128)(2,1)} %copy-done.50), kind=kOutput, calls=%fused_computation.317 | convolution fusion | flops 6444023808 | bytes 20971520 | tf_op jit(solution)/shard_map/dot_general | solution.py:38
  317.7 10.6 %collective-permute-done.38 = bf16[128,2048]{1,0:T(8,128)(2,1)S(1)} collective-permute-done((bf16[128,2048]{1,0:T(8,128)(2,1)S(1)}, bf16[128,2048]{1,0:T(8,128)(2,1)S(1)}, u32[]{:S(2)}, u32[]{:S(2)}) %collective-permute-start.38) | collective-permute-done | bytes 524320 | tf_op jit(solution)/shard_map/ppermute | solution.py:322
  328.4 2.2 collective-permute-done.40
  333.5 11.6 %convolution_convert_fusion.1 = bf16[2048,2048]{1,0:T(8,128)(2,1)} fusion(bf16[1024,2048]{1,0:T(8,128)(2,1)S(1)} %copy-done.40, bf16[1024,2048]{1,0:T(8,128)(2,1)S(1)} %copy-done.51), kind=kOutput, calls=%fused_computation.20 | convolution fusion | flops 8594128896 | bytes 16777216 | tf_op jit(solution)/shard_map/dot_general | solution.py:38
  346.9 2.7 pad_maximum_fusion.1
  349.7 2.7 multiply_reduce_fusion
  352.4 2.3 fusion.72
  354.7 3.8 fusion.91.own_ref
  358.5 3.6 fusion.92.other_ref
  366.7 1.9 collective-permute-start.46
  368.6 11.2 %fusion.93 = f32[1024,2048]{1,0:T(8,128)} fusion(bf16[1024,2048]{1,0:T(8,128)(2,1)S(1)} %copy-done.53, bf16[2048,2048]{1,0:T(8,128)(2,1)S(1)} %bitcast.166), kind=kOutput, calls=%fused_computation.322 | convolution fusion | flops 8589934592 | bytes 20971520 | tf_op jit(solution)/shard_map/dot_general | solution.py:38
  382.9 2.6 copy-done
  390.9 22.0 %attend_backward.1 = (bf16[1024,512]{1,0:T(8,128)(2,1)S(1)}, bf16[1024,512]{1,0:T(8,128)(2,1)S(1)}, bf16[1024,512]{1,0:T(8,128)(2,1)S(1)}) custom-call(s32[1]{0:T(128)} %bitcast.8.me_ref.spot_ref, bf16[8,1024,1024]{2,1,0:T(8,128)(2,1)} %get-tuple-element.167.probs_ref, bf16[1024,1536]{1,0:T(8,128)(2,1)} %add_convert_fusion.q_ref.k_in.v_in, ...), custom_call_target="tpu_custom_call" | custom-call | flops 8589934592 | bytes 16777216 | tf_op jit(solution)/shard_map/attend_backward/pallas_call | solution.py:157
  414.8 12.8 %convolution_convert_fusion = bf16[2048,1536]{1,0:T(8,128)(2,1)} fusion(bf16[1024,1536]{1,0:T(8,128)(2,1)S(1)} %constant_dynamic-update-slice_fusion.62, bf16[1024,2048]{1,0:T(8,128)(2,1)} %constant_dynamic-update-slice_fusion, f32[2048]{0:T(1024)S(1)} %copy-done.47, f32[2048]{0:T(1024)S(1)} %copy-done.42, f32[1024]{0:T(1024)S(1)} %copy-done.49, ...), kind=kOutput, calls=%fused_computation.19 | convolution fusion | flops 6458179584 | bytes 13656064 | tf_op jit(solution)/shard_map/dot_general | solution.py:38
  434.2 4.2 convert.23
  443.9 4.3 fusion.74
  452.9 7.5 %fusion.89 = (bf16[768,2048]{1,0:T(8,128)(2,1)}, f32[768,2048]{1,0:T(8,128)}) fusion(bf16[2048,1536]{1,0:T(8,128)(2,1)S(1)} %bitcast.168, bf16[1024,1536]{1,0:T(8,128)(2,1)S(1)} %copy-done.10), kind=kOutput, calls=%fused_computation.318 | convolution fusion | flops 4833411072 | bytes 18087936 | tf_op jit(solution)/shard_map/dot_general | solution.py:38
  461.3 2.8 convert_element_type.322
  464.0 2.3 fusion.77
  475.6 1.9 collective-permute-done.59
  480.3 13.9 %collective-permute-done.64.refs_1_ = bf16[64,2048]{1,0:T(8,128)(2,1)S(1)} collective-permute-done((bf16[64,2048]{1,0:T(8,128)(2,1)S(1)}, bf16[64,2048]{1,0:T(8,128)(2,1)S(1)}, u32[]{:S(2)}, u32[]{:S(2)}) %collective-permute-start.64) | collective-permute-done | bytes 262176 | tf_op jit(solution)/shard_map/ppermute | solution.py:322
  496.5 3.8 collective-permute-done.66.refs_3_
  506.5 2.1 collective-permute-done.58
  511.0 22.5 %collective-permute-done.60 = bf16[128,2048]{1,0:T(8,128)(2,1)S(1)} collective-permute-done((bf16[128,2048]{1,0:T(8,128)(2,1)S(1)}, bf16[128,2048]{1,0:T(8,128)(2,1)S(1)}, u32[]{:S(2)}, u32[]{:S(2)}) %collective-permute-start.60) | collective-permute-done | bytes 524320 | tf_op jit(solution)/shard_map/ppermute | solution.py:322
  534.9 6.7 %collective-permute-done.56 = bf16[128,2048]{1,0:T(8,128)(2,1)S(1)} collective-permute-done((bf16[128,2048]{1,0:T(8,128)(2,1)S(1)}, bf16[128,2048]{1,0:T(8,128)(2,1)S(1)}, u32[]{:S(2)}, u32[]{:S(2)}) %collective-permute-start.56) | collective-permute-done | bytes 524320 | tf_op jit(solution)/shard_map/ppermute | solution.py:322
  541.6 2.2 convert_add_fusion.5
  544.9 1.9 collective-permute-done.77
  550.1 4.6 collective-permute-done.57
  557.7 3.3 fusion.28
  566.3 2.0 collective-permute-done.67
  577.5 2.6 collective-permute-done.70
  (443 shorter events, 176.9 us)
Async XLA Ops:
  7.2 104.1 %all-gather.4.cloned.1.call-start = ((), (), s32[]{:S(2)}) async-start(), calls=%async_computation.3 | async-start | bytes 7077888 | tf_op jit(solution)/shard_map/all_gather | solution.py:469
  12.2 22.0 %collective-permute-start.3 = (bf16[80,2048]{1,0:T(8,128)(2,1)S(1)}, bf16[80,2048]{1,0:T(8,128)(2,1)S(1)}, u32[]{:S(2)}, u32[]{:S(2)}) collective-permute-start(bf16[80,2048]{1,0:T(8,128)(2,1)S(1)} %pad_maximum_fusion.11), channel_id=1, source_target_pairs={{0,8},{4,12},{8,16},{12,20},{16,24},{20,28},{24,0},{28,4},{1,9},{5... | collective-permute-start | bytes 983048 | tf_op jit(solution)/shard_map/ppermute | solution.py:525
  15.2 23.9 %collective-permute-start.4 = (bf16[80,2048]{1,0:T(8,128)(2,1)S(1)}, bf16[80,2048]{1,0:T(8,128)(2,1)S(1)}, u32[]{:S(2)}, u32[]{:S(2)}) collective-permute-start(bf16[80,2048]{1,0:T(8,128)(2,1)S(1)} %pad_maximum_fusion.11), channel_id=1, source_target_pairs={{0,16},{4,20},{8,24},{12,28},{16,0},{20,4},{24,8},{28,12},{1,17},{... | collective-permute-start | bytes 983048 | tf_op jit(solution)/shard_map/ppermute | solution.py:525
  17.8 21.3 %collective-permute-start.5 = (bf16[80,2048]{1,0:T(8,128)(2,1)S(1)}, bf16[80,2048]{1,0:T(8,128)(2,1)S(1)}, u32[]{:S(2)}, u32[]{:S(2)}) collective-permute-start(bf16[80,2048]{1,0:T(8,128)(2,1)S(1)} %pad_maximum_fusion.11), channel_id=1, source_target_pairs={{0,24},{4,28},{8,0},{12,4},{16,8},{20,12},{24,16},{28,20},{1,25},{... | collective-permute-start | bytes 983048 | tf_op jit(solution)/shard_map/ppermute | solution.py:525
  40.2 195.5 %all-gather.6.cloned.1.call-start = ((), (), s32[]{:S(2)}) async-start(), calls=%async_computation.4 | async-start | bytes 9437184 | tf_op jit(solution)/shard_map/all_gather | solution.py:469
  40.5 14.9 %collective-permute-start.6 = (bf16[128,2048]{1,0:T(8,128)(2,1)S(1)}, bf16[128,2048]{1,0:T(8,128)(2,1)S(1)}, u32[]{:S(2)}, u32[]{:S(2)}) collective-permute-start(bf16[128,2048]{1,0:T(8,128)(2,1)S(1)} %get-tuple-element.306), channel_id=1, source_target_pairs={{0,1},{1,0},{2,3},{3,2},{4,5},{5,4},{6,7},{7,6},{8,9},{9,8},{10,11... | collective-permute-start | bytes 1572872 | tf_op jit(solution)/shard_map/ppermute | solution.py:322
  42.0 26.9 %collective-permute-start.8 = (bf16[128,2048]{1,0:T(8,128)(2,1)S(1)}, bf16[128,2048]{1,0:T(8,128)(2,1)S(1)}, u32[]{:S(2)}, u32[]{:S(2)}) collective-permute-start(bf16[128,2048]{1,0:T(8,128)(2,1)S(1)} %get-tuple-element.306), channel_id=1, source_target_pairs={{0,2},{1,3},{2,0},{3,1},{4,6},{5,7},{6,4},{7,5},{8,10},{9,11},{10,... | collective-permute-start | bytes 1572872 | tf_op jit(solution)/shard_map/ppermute | solution.py:322
  43.5 23.0 %collective-permute-start.7 = (bf16[128,2048]{1,0:T(8,128)(2,1)S(1)}, bf16[128,2048]{1,0:T(8,128)(2,1)S(1)}, u32[]{:S(2)}, u32[]{:S(2)}) collective-permute-start(bf16[128,2048]{1,0:T(8,128)(2,1)S(1)} %get-tuple-element.305), channel_id=1, source_target_pairs={{0,1},{1,0},{2,3},{3,2},{4,5},{5,4},{6,7},{7,6},{8,9},{9,8},{10,11... | collective-permute-start | bytes 1572872 | tf_op jit(solution)/shard_map/ppermute | solution.py:322
  44.1 26.3 %collective-permute-start.9 = (bf16[128,2048]{1,0:T(8,128)(2,1)S(1)}, bf16[128,2048]{1,0:T(8,128)(2,1)S(1)}, u32[]{:S(2)}, u32[]{:S(2)}) collective-permute-start(bf16[128,2048]{1,0:T(8,128)(2,1)S(1)} %get-tuple-element.305), channel_id=1, source_target_pairs={{0,2},{1,3},{2,0},{3,1},{4,6},{5,7},{6,4},{7,5},{8,10},{9,11},{10,... | collective-permute-start | bytes 1572872 | tf_op jit(solution)/shard_map/ppermute | solution.py:322
  53.1 40.6 %collective-permute-start.13 = (bf16[80,2048]{1,0:T(8,128)(2,1)S(1)}, bf16[80,2048]{1,0:T(8,128)(2,1)S(1)}, u32[]{:S(2)}, u32[]{:S(2)}) collective-permute-start(bf16[80,2048]{1,0:T(8,128)(2,1)S(1)} %get-tuple-element.334), channel_id=1, source_target_pairs={{0,1},{1,0},{2,3},{3,2},{4,5},{5,4},{6,7},{7,6},{8,9},{9,8},{10,11... | collective-permute-start | bytes 983048 | tf_op jit(solution)/shard_map/ppermute | solution.py:322
  55.3 38.4 %collective-permute-start.14 = (bf16[80,2048]{1,0:T(8,128)(2,1)S(1)}, bf16[80,2048]{1,0:T(8,128)(2,1)S(1)}, u32[]{:S(2)}, u32[]{:S(2)}) collective-permute-start(bf16[80,2048]{1,0:T(8,128)(2,1)S(1)} %get-tuple-element.335), channel_id=1, source_target_pairs={{0,2},{1,3},{2,0},{3,1},{4,6},{5,7},{6,4},{7,5},{8,10},{9,11},{10,... | collective-permute-start | bytes 983048 | tf_op jit(solution)/shard_map/ppermute | solution.py:322
  66.6 25.4 %collective-permute-start.10 = (bf16[128,2048]{1,0:T(8,128)(2,1)S(1)}, bf16[128,2048]{1,0:T(8,128)(2,1)S(1)}, u32[]{:S(2)}, u32[]{:S(2)}) collective-permute-start(bf16[128,2048]{1,0:T(8,128)(2,1)S(1)} %collective-permute-done.6), channel_id=1, source_target_pairs={{0,2},{1,3},{2,0},{3,1},{4,6},{5,7},{6,4},{7,5},{8,10},{9,11},{10,... | collective-permute-start | bytes 1572872 | tf_op jit(solution)/shard_map/ppermute | solution.py:322
  68.9 24.8 %collective-permute-start.15 = (bf16[80,2048]{1,0:T(8,128)(2,1)S(1)}, bf16[80,2048]{1,0:T(8,128)(2,1)S(1)}, u32[]{:S(2)}, u32[]{:S(2)}) collective-permute-start(bf16[80,2048]{1,0:T(8,128)(2,1)S(1)} %get-tuple-element.333), channel_id=1, source_target_pairs={{0,3},{1,2},{2,1},{3,0},{4,7},{5,6},{6,5},{7,4},{8,11},{9,10},{10,... | collective-permute-start | bytes 983048 | tf_op jit(solution)/shard_map/ppermute | solution.py:322
  70.4 22.5 %collective-permute-start.11 = (bf16[128,2048]{1,0:T(8,128)(2,1)S(1)}, bf16[128,2048]{1,0:T(8,128)(2,1)S(1)}, u32[]{:S(2)}, u32[]{:S(2)}) collective-permute-start(bf16[128,2048]{1,0:T(8,128)(2,1)S(1)} %collective-permute-done.9), channel_id=1, source_target_pairs={{0,1},{1,0},{2,3},{3,2},{4,5},{5,4},{6,7},{7,6},{8,9},{9,8},{10,11... | collective-permute-start | bytes 1572872 | tf_op jit(solution)/shard_map/ppermute | solution.py:322
  95.7 180.8 %all-gather.8.cloned.1.call-start = ((), (), s32[]{:S(2)}) async-start(), calls=%async_computation.5 | async-start | bytes 9437184 | tf_op jit(solution)/shard_map/all_gather | solution.py:469
  96.0 37.9 %collective-permute-start.20 = (bf16[128,2048]{1,0:T(8,128)(2,1)S(1)}, bf16[128,2048]{1,0:T(8,128)(2,1)}, u32[]{:S(2)}, u32[]{:S(2)}) collective-permute-start(bf16[128,2048]{1,0:T(8,128)(2,1)S(1)} %get-tuple-element.148), channel_id=1, source_target_pairs={{0,1},{1,0},{2,3},{3,2},{4,5},{5,4},{6,7},{7,6},{8,9},{9,8},{10,11... | collective-permute-start | bytes 1572872 | tf_op jit(solution)/shard_map/ppermute | solution.py:322
  97.5 25.5 %collective-permute-start.16 = (bf16[128,2048]{1,0:T(8,128)(2,1)}, bf16[128,2048]{1,0:T(8,128)(2,1)}, u32[]{:S(2)}, u32[]{:S(2)}) collective-permute-start(bf16[128,2048]{1,0:T(8,128)(2,1)} %get-tuple-element.132), channel_id=1, source_target_pairs={{0,1},{1,0},{2,3},{3,2},{4,5},{5,4},{6,7},{7,6},{8,9},{9,8},{10,11... | collective-permute-start | bytes 1572872 | tf_op jit(solution)/shard_map/ppermute | solution.py:322
  99.0 32.8 %collective-permute-start.18 = (bf16[128,2048]{1,0:T(8,128)(2,1)}, bf16[128,2048]{1,0:T(8,128)(2,1)S(1)}, u32[]{:S(2)}, u32[]{:S(2)}) collective-permute-start(bf16[128,2048]{1,0:T(8,128)(2,1)} %get-tuple-element.132), channel_id=1, source_target_pairs={{0,2},{1,3},{2,0},{3,1},{4,6},{5,7},{6,4},{7,5},{8,10},{9,11},{10,... | collective-permute-start | bytes 1572872 | tf_op jit(solution)/shard_map/ppermute | solution.py:322
  100.6 30.7 %collective-permute-start.17 = (bf16[128,2048]{1,0:T(8,128)(2,1)S(1)}, bf16[128,2048]{1,0:T(8,128)(2,1)S(1)}, u32[]{:S(2)}, u32[]{:S(2)}) collective-permute-start(bf16[128,2048]{1,0:T(8,128)(2,1)S(1)} %get-tuple-element.133), channel_id=1, source_target_pairs={{0,1},{1,0},{2,3},{3,2},{4,5},{5,4},{6,7},{7,6},{8,9},{9,8},{10,11... | collective-permute-start | bytes 1572872 | tf_op jit(solution)/shard_map/ppermute | solution.py:322
  101.1 32.3 %collective-permute-start.19 = (bf16[128,2048]{1,0:T(8,128)(2,1)S(1)}, bf16[128,2048]{1,0:T(8,128)(2,1)}, u32[]{:S(2)}, u32[]{:S(2)}) collective-permute-start(bf16[128,2048]{1,0:T(8,128)(2,1)S(1)} %get-tuple-element.133), channel_id=1, source_target_pairs={{0,2},{1,3},{2,0},{3,1},{4,6},{5,7},{6,4},{7,5},{8,10},{9,11},{10,... | collective-permute-start | bytes 1572872 | tf_op jit(solution)/shard_map/ppermute | solution.py:322
  123.1 34.1 %collective-permute-start.22 = (bf16[128,2048]{1,0:T(8,128)(2,1)S(1)}, bf16[128,2048]{1,0:T(8,128)(2,1)}, u32[]{:S(2)}, u32[]{:S(2)}) collective-permute-start(bf16[128,2048]{1,0:T(8,128)(2,1)S(1)} %get-tuple-element.148), channel_id=1, source_target_pairs={{0,2},{1,3},{2,0},{3,1},{4,6},{5,7},{6,4},{7,5},{8,10},{9,11},{10,... | collective-permute-start | bytes 1572872 | tf_op jit(solution)/shard_map/ppermute | solution.py:322
  131.3 25.9 %collective-permute-start.21 = (bf16[128,2048]{1,0:T(8,128)(2,1)S(1)}, bf16[128,2048]{1,0:T(8,128)(2,1)}, u32[]{:S(2)}, u32[]{:S(2)}) collective-permute-start(bf16[128,2048]{1,0:T(8,128)(2,1)S(1)} %get-tuple-element.149), channel_id=1, source_target_pairs={{0,1},{1,0},{2,3},{3,2},{4,5},{5,4},{6,7},{7,6},{8,9},{9,8},{10,11... | collective-permute-start | bytes 1572872 | tf_op jit(solution)/shard_map/ppermute | solution.py:322
  131.8 25.4 %collective-permute-start.23 = (bf16[128,2048]{1,0:T(8,128)(2,1)S(1)}, bf16[128,2048]{1,0:T(8,128)(2,1)}, u32[]{:S(2)}, u32[]{:S(2)}) collective-permute-start(bf16[128,2048]{1,0:T(8,128)(2,1)S(1)} %get-tuple-element.149), channel_id=1, source_target_pairs={{0,2},{1,3},{2,0},{3,1},{4,6},{5,7},{6,4},{7,5},{8,10},{9,11},{10,... | collective-permute-start | bytes 1572872 | tf_op jit(solution)/shard_map/ppermute | solution.py:322
  133.4 26.4 %collective-permute-start.24 = (bf16[128,2048]{1,0:T(8,128)(2,1)}, bf16[128,2048]{1,0:T(8,128)(2,1)}, u32[]{:S(2)}, u32[]{:S(2)}) collective-permute-start(bf16[128,2048]{1,0:T(8,128)(2,1)} %collective-permute-done.16), channel_id=1, source_target_pairs={{0,2},{1,3},{2,0},{3,1},{4,6},{5,7},{6,4},{7,5},{8,10},{9,11},{10,... | collective-permute-start | bytes 1572872 | tf_op jit(solution)/shard_map/ppermute | solution.py:322
  133.9 25.9 %collective-permute-start.25 = (bf16[128,2048]{1,0:T(8,128)(2,1)}, bf16[128,2048]{1,0:T(8,128)(2,1)}, u32[]{:S(2)}, u32[]{:S(2)}) collective-permute-start(bf16[128,2048]{1,0:T(8,128)(2,1)} %collective-permute-done.19), channel_id=1, source_target_pairs={{0,1},{1,0},{2,3},{3,2},{4,5},{5,4},{6,7},{7,6},{8,9},{9,8},{10,11... | collective-permute-start | bytes 1572872 | tf_op jit(solution)/shard_map/ppermute | solution.py:322
  166.9 17.5 %collective-permute-start.29 = (bf16[1024,2048]{1,0:T(8,128)(2,1)}, bf16[1024,2048]{1,0:T(8,128)(2,1)}, u32[]{:S(2)}, u32[]{:S(2)}) collective-permute-start(bf16[1024,2048]{1,0:T(8,128)(2,1)} %bitcast.30), channel_id=1, source_target_pairs={{0,4},{4,0},{8,12},{12,8},{16,20},{20,16},{24,28},{28,24},{1,5},{5... | collective-permute-start | bytes 12582920 | tf_op jit(solution)/shard_map/ppermute | solution.py:424
  166.9 260.8 %reduce-scatter.4.cloned.1.call-start = ((), (), s32[]{:S(2)}) async-start(), calls=%async_computation.6 | async-start | bytes 9437184 | tf_op jit(solution)/shard_map/reduce_scatter | solution.py:483
  192.9 14.9 %collective-permute-start.30 = (bf16[128,2048]{1,0:T(8,128)(2,1)S(1)}, bf16[128,2048]{1,0:T(8,128)(2,1)S(1)}, u32[]{:S(2)}, u32[]{:S(2)}) collective-permute-start(bf16[128,2048]{1,0:T(8,128)(2,1)S(1)} %get-tuple-element.260), channel_id=1, source_target_pairs={{0,1},{1,0},{2,3},{3,2},{4,5},{5,4},{6,7},{7,6},{8,9},{9,8},{10,11... | collective-permute-start | bytes 1572872 | tf_op jit(solution)/shard_map/ppermute | solution.py:322
  194.2 15.1 %collective-permute-start.33 = (bf16[128,2048]{1,0:T(8,128)(2,1)S(1)}, bf16[128,2048]{1,0:T(8,128)(2,1)S(1)}, u32[]{:S(2)}, u32[]{:S(2)}) collective-permute-start(bf16[128,2048]{1,0:T(8,128)(2,1)S(1)} %get-tuple-element.259), channel_id=1, source_target_pairs={{0,2},{1,3},{2,0},{3,1},{4,6},{5,7},{6,4},{7,5},{8,10},{9,11},{10,... | collective-permute-start | bytes 1572872 | tf_op jit(solution)/shard_map/ppermute | solution.py:322
  195.0 24.0 %collective-permute-start.31 = (bf16[128,2048]{1,0:T(8,128)(2,1)S(1)}, bf16[128,2048]{1,0:T(8,128)(2,1)S(1)}, u32[]{:S(2)}, u32[]{:S(2)}) collective-permute-start(bf16[128,2048]{1,0:T(8,128)(2,1)S(1)} %get-tuple-element.259), channel_id=1, source_target_pairs={{0,1},{1,0},{2,3},{3,2},{4,5},{5,4},{6,7},{7,6},{8,9},{9,8},{10,11... | collective-permute-start | bytes 1572872 | tf_op jit(solution)/shard_map/ppermute | solution.py:322
  196.5 23.8 %collective-permute-start.32 = (bf16[128,2048]{1,0:T(8,128)(2,1)S(1)}, bf16[128,2048]{1,0:T(8,128)(2,1)S(1)}, u32[]{:S(2)}, u32[]{:S(2)}) collective-permute-start(bf16[128,2048]{1,0:T(8,128)(2,1)S(1)} %get-tuple-element.260), channel_id=1, source_target_pairs={{0,2},{1,3},{2,0},{3,1},{4,6},{5,7},{6,4},{7,5},{8,10},{9,11},{10,... | collective-permute-start | bytes 1572872 | tf_op jit(solution)/shard_map/ppermute | solution.py:322
  207.8 22.2 %collective-permute-start.34 = (bf16[128,2048]{1,0:T(8,128)(2,1)S(1)}, bf16[128,2048]{1,0:T(8,128)(2,1)S(1)}, u32[]{:S(2)}, u32[]{:S(2)}) collective-permute-start(bf16[128,2048]{1,0:T(8,128)(2,1)S(1)} %collective-permute-done.30), channel_id=1, source_target_pairs={{0,2},{1,3},{2,0},{3,1},{4,6},{5,7},{6,4},{7,5},{8,10},{9,11},{10,... | collective-permute-start | bytes 1572872 | tf_op jit(solution)/shard_map/ppermute | solution.py:322
  209.3 20.7 %collective-permute-start.35 = (bf16[128,2048]{1,0:T(8,128)(2,1)S(1)}, bf16[128,2048]{1,0:T(8,128)(2,1)S(1)}, u32[]{:S(2)}, u32[]{:S(2)}) collective-permute-start(bf16[128,2048]{1,0:T(8,128)(2,1)S(1)} %collective-permute-done.33), channel_id=1, source_target_pairs={{0,1},{1,0},{2,3},{3,2},{4,5},{5,4},{6,7},{7,6},{8,9},{9,8},{10,11... | collective-permute-start | bytes 1572872 | tf_op jit(solution)/shard_map/ppermute | solution.py:322
  230.1 26.8 %collective-permute-start.36 = (bf16[128,2048]{1,0:T(8,128)(2,1)}, bf16[128,2048]{1,0:T(8,128)(2,1)}, u32[]{:S(2)}, u32[]{:S(2)}) collective-permute-start(bf16[128,2048]{1,0:T(8,128)(2,1)} %collective-permute-done.20), channel_id=1, source_target_pairs={{0,2},{1,3},{2,0},{3,1},{4,6},{5,7},{6,4},{7,5},{8,10},{9,11},{10,... | collective-permute-start | bytes 1572872 | tf_op jit(solution)/shard_map/ppermute | solution.py:322
  230.8 28.0 %collective-permute-start.37 = (bf16[128,2048]{1,0:T(8,128)(2,1)}, bf16[128,2048]{1,0:T(8,128)(2,1)}, u32[]{:S(2)}, u32[]{:S(2)}) collective-permute-start(bf16[128,2048]{1,0:T(8,128)(2,1)} %collective-permute-done.23), channel_id=1, source_target_pairs={{0,1},{1,0},{2,3},{3,2},{4,5},{5,4},{6,7},{7,6},{8,9},{9,8},{10,11... | collective-permute-start | bytes 1572872 | tf_op jit(solution)/shard_map/ppermute | solution.py:322
  276.5 189.9 %reduce-scatter.6.cloned.1.call-start = ((), (), s32[]{:S(2)}) async-start(), calls=%async_computation.7 | async-start | bytes 9437184 | tf_op jit(solution)/shard_map/reduce_scatter | solution.py:483
  300.8 14.7 %collective-permute-start.39 = (bf16[128,2048]{1,0:T(8,128)(2,1)S(1)}, bf16[128,2048]{1,0:T(8,128)(2,1)S(1)}, u32[]{:S(2)}, u32[]{:S(2)}) collective-permute-start(bf16[128,2048]{1,0:T(8,128)(2,1)S(1)} %get-tuple-element.257), channel_id=1, source_target_pairs={{0,1},{1,0},{2,3},{3,2},{4,5},{5,4},{6,7},{7,6},{8,9},{9,8},{10,11... | collective-permute-start | bytes 1572872 | tf_op jit(solution)/shard_map/ppermute | solution.py:322
  302.4 15.3 %collective-permute-start.42 = (bf16[128,2048]{1,0:T(8,128)(2,1)S(1)}, bf16[128,2048]{1,0:T(8,128)(2,1)S(1)}, u32[]{:S(2)}, u32[]{:S(2)}) collective-permute-start(bf16[128,2048]{1,0:T(8,128)(2,1)S(1)} %get-tuple-element.258), channel_id=1, source_target_pairs={{0,2},{1,3},{2,0},{3,1},{4,6},{5,7},{6,4},{7,5},{8,10},{9,11},{10,... | collective-permute-start | bytes 1572872 | tf_op jit(solution)/shard_map/ppermute | solution.py:322
  315.6 14.9 %collective-permute-start.40 = (bf16[128,2048]{1,0:T(8,128)(2,1)S(1)}, bf16[128,2048]{1,0:T(8,128)(2,1)S(1)}, u32[]{:S(2)}, u32[]{:S(2)}) collective-permute-start(bf16[128,2048]{1,0:T(8,128)(2,1)S(1)} %fusion.38), channel_id=1, source_target_pairs={{0,2},{1,3},{2,0},{3,1},{4,6},{5,7},{6,4},{7,5},{8,10},{9,11},{10,... | collective-permute-start | bytes 1572872 | tf_op jit(solution)/shard_map/ppermute | solution.py:322
  316.6 28.6 %collective-permute-start.41 = (bf16[128,2048]{1,0:T(8,128)(2,1)}, bf16[128,2048]{1,0:T(8,128)(2,1)}, u32[]{:S(2)}, u32[]{:S(2)}) collective-permute-start(bf16[128,2048]{1,0:T(8,128)(2,1)} %get-tuple-element.234), channel_id=1, source_target_pairs={{0,2},{1,3},{2,0},{3,1},{4,6},{5,7},{6,4},{7,5},{8,10},{9,11},{10,... | collective-permute-start | bytes 1572872 | tf_op jit(solution)/shard_map/ppermute | solution.py:322
  349.6 208.1 %reduce-scatter.8.cloned.1.call-start = ((), (), s32[]{:S(2)}) async-start(), calls=%async_computation.8 | async-start | bytes 7077888 | tf_op jit(solution)/shard_map/reduce_scatter | solution.py:483
  365.0 15.9 %collective-permute-start.47 = (bf16[1024,2048]{1,0:T(8,128)(2,1)S(1)}, bf16[1024,2048]{1,0:T(8,128)(2,1)S(1)}, u32[]{:S(2)}, u32[]{:S(2)}) collective-permute-start(bf16[1024,2048]{1,0:T(8,128)(2,1)S(1)} %convolution_convert_fusion.3), channel_id=1, source_target_pairs={{0,4},{4,0},{8,12},{12,8},{16,20},{20,16},{24,28},{28,24},{1,5},{5... | collective-permute-start | bytes 12582920 | tf_op jit(solution)/shard_map/ppermute | solution.py:424
  365.1 14.7 %collective-permute-start.44 = (bf16[256,512]{1,0:T(8,128)(2,1)S(1)}, bf16[256,512]{1,0:T(8,128)(2,1)S(1)}, u32[]{:S(2)}, u32[]{:S(2)}) collective-permute-start(bf16[256,512]{1,0:T(8,128)(2,1)S(1)} %get-tuple-element.161), channel_id=1, source_target_pairs={{0,1},{1,0},{2,3},{3,2},{4,5},{5,4},{6,7},{7,6},{8,9},{9,8},{10,11... | collective-permute-start | bytes 786440 | tf_op jit(solution)/shard_map/ppermute | solution.py:322
  386.8 40.8 %collective-permute-start.48 = (bf16[128,2048]{1,0:T(8,128)(2,1)}, bf16[128,2048]{1,0:T(8,128)(2,1)}, u32[]{:S(2)}, u32[]{:S(2)}) collective-permute-start(bf16[128,2048]{1,0:T(8,128)(2,1)} %bitcast.34), channel_id=1, source_target_pairs={{0,1},{1,0},{2,3},{3,2},{4,5},{5,4},{6,7},{7,6},{8,9},{9,8},{10,11... | collective-permute-start | bytes 1572872 | tf_op jit(solution)/shard_map/ppermute | solution.py:322
  388.2 39.5 %collective-permute-start.49 = (bf16[128,2048]{1,0:T(8,128)(2,1)}, bf16[128,2048]{1,0:T(8,128)(2,1)}, u32[]{:S(2)}, u32[]{:S(2)}) collective-permute-start(bf16[128,2048]{1,0:T(8,128)(2,1)} %bitcast.35), channel_id=1, source_target_pairs={{0,2},{1,3},{2,0},{3,1},{4,6},{5,7},{6,4},{7,5},{8,10},{9,11},{10,... | collective-permute-start | bytes 1572872 | tf_op jit(solution)/shard_map/ppermute | solution.py:322
  389.1 38.5 %collective-permute-start.50 = (bf16[128,2048]{1,0:T(8,128)(2,1)}, bf16[128,2048]{1,0:T(8,128)(2,1)}, u32[]{:S(2)}, u32[]{:S(2)}) collective-permute-start(bf16[128,2048]{1,0:T(8,128)(2,1)} %bitcast.36), channel_id=1, source_target_pairs={{0,1},{1,0},{2,3},{3,2},{4,5},{5,4},{6,7},{7,6},{8,9},{9,8},{10,11... | collective-permute-start | bytes 1572872 | tf_op jit(solution)/shard_map/ppermute | solution.py:322
  389.9 37.7 %collective-permute-start.51 = (bf16[128,2048]{1,0:T(8,128)(2,1)}, bf16[128,2048]{1,0:T(8,128)(2,1)}, u32[]{:S(2)}, u32[]{:S(2)}) collective-permute-start(bf16[128,2048]{1,0:T(8,128)(2,1)} %bitcast.37), channel_id=1, source_target_pairs={{0,2},{1,3},{2,0},{3,1},{4,6},{5,7},{6,4},{7,5},{8,10},{9,11},{10,... | collective-permute-start | bytes 1572872 | tf_op jit(solution)/shard_map/ppermute | solution.py:322
  439.8 26.5 %collective-permute-start.52 = (bf16[128,2048]{1,0:T(8,128)(2,1)}, bf16[128,2048]{1,0:T(8,128)(2,1)}, u32[]{:S(2)}, u32[]{:S(2)}) collective-permute-start(bf16[128,2048]{1,0:T(8,128)(2,1)} %get-tuple-element.226), channel_id=1, source_target_pairs={{0,1},{1,0},{2,3},{3,2},{4,5},{5,4},{6,7},{7,6},{8,9},{9,8},{10,11... | collective-permute-start | bytes 1572872 | tf_op jit(solution)/shard_map/ppermute | solution.py:322
  441.1 25.2 %collective-permute-start.53 = (bf16[128,2048]{1,0:T(8,128)(2,1)}, bf16[128,2048]{1,0:T(8,128)(2,1)}, u32[]{:S(2)}, u32[]{:S(2)}) collective-permute-start(bf16[128,2048]{1,0:T(8,128)(2,1)} %get-tuple-element.225), channel_id=1, source_target_pairs={{0,2},{1,3},{2,0},{3,1},{4,6},{5,7},{6,4},{7,5},{8,10},{9,11},{10,... | collective-permute-start | bytes 1572872 | tf_op jit(solution)/shard_map/ppermute | solution.py:322
  442.0 24.3 %collective-permute-start.54 = (bf16[128,2048]{1,0:T(8,128)(2,1)}, bf16[128,2048]{1,0:T(8,128)(2,1)}, u32[]{:S(2)}, u32[]{:S(2)}) collective-permute-start(bf16[128,2048]{1,0:T(8,128)(2,1)} %get-tuple-element.224), channel_id=1, source_target_pairs={{0,1},{1,0},{2,3},{3,2},{4,5},{5,4},{6,7},{7,6},{8,9},{9,8},{10,11... | collective-permute-start | bytes 1572872 | tf_op jit(solution)/shard_map/ppermute | solution.py:322
  442.8 23.5 %collective-permute-start.55 = (bf16[128,2048]{1,0:T(8,128)(2,1)}, bf16[128,2048]{1,0:T(8,128)(2,1)}, u32[]{:S(2)}, u32[]{:S(2)}) collective-permute-start(bf16[128,2048]{1,0:T(8,128)(2,1)} %get-tuple-element.223), channel_id=1, source_target_pairs={{0,2},{1,3},{2,0},{3,1},{4,6},{5,7},{6,4},{7,5},{8,10},{9,11},{10,... | collective-permute-start | bytes 1572872 | tf_op jit(solution)/shard_map/ppermute | solution.py:322
  451.0 26.4 %collective-permute-start.59 = (bf16[128,2048]{1,0:T(8,128)(2,1)}, bf16[128,2048]{1,0:T(8,128)(2,1)}, u32[]{:S(2)}, u32[]{:S(2)}) collective-permute-start(bf16[128,2048]{1,0:T(8,128)(2,1)} %get-tuple-element.255), channel_id=1, source_target_pairs={{0,1},{1,0},{2,3},{3,2},{4,5},{5,4},{6,7},{7,6},{8,9},{9,8},{10,11... | collective-permute-start | bytes 1572872 | tf_op jit(solution)/shard_map/ppermute | solution.py:322
  468.0 34.7 %collective-permute-start.75 = (bf16[128,2048]{1,0:T(8,128)(2,1)S(1)}, bf16[128,2048]{1,0:T(8,128)(2,1)S(1)}, u32[]{:S(2)}, u32[]{:S(2)}) collective-permute-start(bf16[128,2048]{1,0:T(8,128)(2,1)S(1)} %fusion.43), channel_id=1, source_target_pairs={{0,1},{1,0},{2,3},{3,2},{4,5},{5,4},{6,7},{7,6},{8,9},{9,8},{10,11... | collective-permute-start | bytes 1572872 | tf_op jit(solution)/shard_map/ppermute | solution.py:322
  470.9 32.9 %collective-permute-start.76 = (bf16[128,2048]{1,0:T(8,128)(2,1)S(1)}, bf16[128,2048]{1,0:T(8,128)(2,1)S(1)}, u32[]{:S(2)}, u32[]{:S(2)}) collective-permute-start(bf16[128,2048]{1,0:T(8,128)(2,1)S(1)} %fusion.40), channel_id=1, source_target_pairs={{0,2},{1,3},{2,0},{3,1},{4,6},{5,7},{6,4},{7,5},{8,10},{9,11},{10,... | collective-permute-start | bytes 1572872 | tf_op jit(solution)/shard_map/ppermute | solution.py:322
  472.0 22.2 %collective-permute-start.64 = (bf16[64,2048]{1,0:T(8,128)(2,1)S(1)}, bf16[64,2048]{1,0:T(8,128)(2,1)S(1)}, u32[]{:S(2)}, u32[]{:S(2)}) collective-permute-start(bf16[64,2048]{1,0:T(8,128)(2,1)S(1)} %get-tuple-element.253), channel_id=1, source_target_pairs={{0,1},{1,0},{2,3},{3,2},{4,5},{5,4},{6,7},{7,6},{8,9},{9,8},{10,11... | collective-permute-start | bytes 786440 | tf_op jit(solution)/shard_map/ppermute | solution.py:322
  473.1 22.4 %collective-permute-start.65 = (bf16[64,2048]{1,0:T(8,128)(2,1)S(1)}, bf16[64,2048]{1,0:T(8,128)(2,1)S(1)}, u32[]{:S(2)}, u32[]{:S(2)}) collective-permute-start(bf16[64,2048]{1,0:T(8,128)(2,1)S(1)} %get-tuple-element.252), channel_id=1, source_target_pairs={{0,2},{1,3},{2,0},{3,1},{4,6},{5,7},{6,4},{7,5},{8,10},{9,11},{10,... | collective-permute-start | bytes 786440 | tf_op jit(solution)/shard_map/ppermute | solution.py:322
  477.5 22.8 %collective-permute-start.66 = (bf16[64,2048]{1,0:T(8,128)(2,1)S(1)}, bf16[64,2048]{1,0:T(8,128)(2,1)S(1)}, u32[]{:S(2)}, u32[]{:S(2)}) collective-permute-start(bf16[64,2048]{1,0:T(8,128)(2,1)S(1)} %get-tuple-element.251), channel_id=1, source_target_pairs={{0,3},{1,2},{2,1},{3,0},{4,7},{5,6},{6,5},{7,4},{8,11},{9,10},{10,... | collective-permute-start | bytes 786440 | tf_op jit(solution)/shard_map/ppermute | solution.py:322
  495.5 15.4 %collective-permute-start.62 = (bf16[128,2048]{1,0:T(8,128)(2,1)S(1)}, bf16[128,2048]{1,0:T(8,128)(2,1)S(1)}, u32[]{:S(2)}, u32[]{:S(2)}) collective-permute-start(bf16[128,2048]{1,0:T(8,128)(2,1)S(1)} %copy-done.35), channel_id=1, source_target_pairs={{0,2},{1,3},{2,0},{3,1},{4,6},{5,7},{6,4},{7,5},{8,10},{9,11},{10,... | collective-permute-start | bytes 1572872 | tf_op jit(solution)/shard_map/ppermute | solution.py:322
  500.2 48.2 %collective-permute-start.61 = (bf16[128,2048]{1,0:T(8,128)(2,1)S(1)}, bf16[128,2048]{1,0:T(8,128)(2,1)S(1)}, u32[]{:S(2)}, u32[]{:S(2)}) collective-permute-start(bf16[128,2048]{1,0:T(8,128)(2,1)S(1)} %copy-done.32), channel_id=1, source_target_pairs={{0,2},{1,3},{2,0},{3,1},{4,6},{5,7},{6,4},{7,5},{8,10},{9,11},{10,... | collective-permute-start | bytes 1572872 | tf_op jit(solution)/shard_map/ppermute | solution.py:322
  502.8 30.7 %collective-permute-start.60 = (bf16[128,2048]{1,0:T(8,128)(2,1)S(1)}, bf16[128,2048]{1,0:T(8,128)(2,1)S(1)}, u32[]{:S(2)}, u32[]{:S(2)}) collective-permute-start(bf16[128,2048]{1,0:T(8,128)(2,1)S(1)} %add_convert_fusion.3), channel_id=1, source_target_pairs={{0,2},{1,3},{2,0},{3,1},{4,6},{5,7},{6,4},{7,5},{8,10},{9,11},{10,... | collective-permute-start | bytes 1572872 | tf_op jit(solution)/shard_map/ppermute | solution.py:322
  503.7 37.9 %collective-permute-start.56 = (bf16[128,2048]{1,0:T(8,128)(2,1)S(1)}, bf16[128,2048]{1,0:T(8,128)(2,1)S(1)}, u32[]{:S(2)}, u32[]{:S(2)}) collective-permute-start(bf16[128,2048]{1,0:T(8,128)(2,1)S(1)} %add_convert_fusion.5), channel_id=1, source_target_pairs={{0,2},{1,3},{2,0},{3,1},{4,6},{5,7},{6,4},{7,5},{8,10},{9,11},{10,... | collective-permute-start | bytes 1572872 | tf_op jit(solution)/shard_map/ppermute | solution.py:322
  508.6 38.1 %collective-permute-start.77 = (bf16[2,64,2048]{2,1,0:T(8,128)(2,1)S(1)}, bf16[2,64,2048]{2,1,0:T(8,128)(2,1)S(1)}, u32[]{:S(2)}, u32[]{:S(2)}) collective-permute-start(bf16[2,64,2048]{2,1,0:T(8,128)(2,1)S(1)} %bitcast.142), channel_id=1, source_target_pairs={{0,16},{4,20},{8,24},{12,28},{16,0},{20,4},{24,8},{28,12},{1,17},{... | collective-permute-start | bytes 1572872 | tf_op jit(solution)/shard_map/ppermute | solution.py:414
  533.8 14.6 %collective-permute-start.63 = (bf16[128,2048]{1,0:T(8,128)(2,1)S(1)}, bf16[128,2048]{1,0:T(8,128)(2,1)S(1)}, u32[]{:S(2)}, u32[]{:S(2)}) collective-permute-start(bf16[128,2048]{1,0:T(8,128)(2,1)S(1)} %get-tuple-element.220), channel_id=1, source_target_pairs={{0,1},{1,0},{2,3},{3,2},{4,5},{5,4},{6,7},{7,6},{8,9},{9,8},{10,11... | collective-permute-start | bytes 1572872 | tf_op jit(solution)/shard_map/ppermute | solution.py:322
  548.4 16.1 %collective-permute-start.78 = (bf16[1,64,2048]{2,1,0:T(8,128)(2,1)}, bf16[1,64,2048]{2,1,0:T(8,128)(2,1)S(1)}, u32[]{:S(2)}, u32[]{:S(2)}) collective-permute-start(bf16[1,64,2048]{2,1,0:T(8,128)(2,1)} %broadcast_select_fusion.2), channel_id=1, source_target_pairs={{0,8},{4,12},{8,0},{12,4},{16,24},{20,28},{24,16},{28,20},{1,9},{5... | collective-permute-start | bytes 786440 | tf_op jit(solution)/shard_map/ppermute | solution.py:414
  (82 other events, 1115.3 us)
Sparse Core Ops, SparseCore 0:
  40.3 70.9 all-gather.3
  113.5 80.6 all-gather.5
  195.8 80.5 all-gather.7
  278.6 88.1 reduce-scatter.3
  368.9 87.9 reduce-scatter.5
  459.0 79.3 reduce-scatter.7

commit v4 on v3

--- a/solution.py
+++ b/solution.py
@@ -649,8 +649,8 @@
     far, grad_projected = lax.optimization_barrier((far, grad_projected))
     near = dot(grad_projected[:last], qkv_weight, ((1,), (1,)))
     first = (scatter_far(far), scatter_side(near))
-    near, out_first, result_first, exp_sum = lax.optimization_barrier(
-        (near, out_first, result_first, exp_sum)
+    first, out_first, result_first, exp_sum = lax.optimization_barrier(
+        (first, out_first, result_first, exp_sum)
     )
     exp_grad = own_rows(exp_sum, groups)
     grad_normed_in = scatter_near(near, *first)

time: 599 us -> 599 us (level)
    ppermute x66, waiting for transfers between devices: 157 us -> 147 us  [hop(): return lax.ppermute(value, 'ctx', [(c, c ^ way) for c in range(ways)])]
    ppermute x7, waiting for transfers between devices: 7.59 us -> 16.2 us  [halving(): value = keep + lax.ppermute(give, axis, [(d, d ^ bit) for d in range(size)])]
    unnamed x145 -> x153, local copies, waits for them, and re-layouts: 29.1 us -> 29.1 us
  transfers between devices with their start and end apart: 85 -> 85, of which waited for: 32 -> 33; matrix products, arithmetic and copies ran while one was open for 43% -> 43% of each run, Pallas kernels for 8% -> 8%
where the time goes in v4:
time: 599 us; the launch traced here: 593 us
  waiting for transfers between devices  172 us (29%)
  matrix products  137 us (23%)
  starting transfers between devices  87.8 us (15%)
  other arithmetic  74.5 us (12%)
  local copies, waits for them, and re-layouts  56 us (9%)
  Pallas kernels  50.6 us (8%)
  between operations  15.9 us (3%)
    ppermute x66, waiting for transfers between devices, hop(): return lax.ppermute(value, 'ctx', [(c, c ^ way) for c in range(ways)])  147 us
    dot_general x17, matrix products, dot(): lax.dot_general(left, right, (contract, ((), ())), preferred_element_type...  137 us
    ppermute x66, starting transfers between devices, hop(): return lax.ppermute(value, 'ctx', [(c, c ^ way) for c in range(ways)])  73 us
    unnamed x153, local copies, waits for them, and re-layouts  29.1 us
    pallas_call x1, Pallas kernels, attend_backward(): pl.pallas_call(functools.partial(attend_backward_kernel, block), grid=(pa...  22 us
    pallas_call x1, Pallas kernels, attend_forward(): pl.pallas_call(functools.partial(attend_forward_kernel, block), grid=(pai...  21.4 us
    ppermute x7, waiting for transfers between devices, halving(): value = keep + lax.ppermute(give, axis, [(d, d ^ bit) for d in range(size)])  16.2 us
  transfers between devices with their start and end apart: 85, of which 33 were waited for; matrix products, arithmetic and copies ran while one was open for 43% of the time, Pallas kernels for 8%

profile of v4, /device:TPU:0, one launch (start us, length us, event | category | flops | bytes accessed | tf_op | source)
XLA Modules:
  0.0 593.0 jit_solution(11135859463926720060)
XLA Ops:
  12.2 3.1 collective-permute-start.3
  15.2 2.6 collective-permute-start.4
  21.2 2.4 collective-permute-start.2
  25.7 2.5 collective-permute-done.2
  29.8 2.5 collective-permute-done.1
  34.1 5.0 collective-permute-done.4
  57.7 8.9 %collective-permute-done.7 = bf16[128,2048]{1,0:T(8,128)(2,1)S(1)} collective-permute-done((bf16[128,2048]{1,0:T(8,128)(2,1)S(1)}, bf16[128,2048]{1,0:T(8,128)(2,1)S(1)}, u32[]{:S(2)}, u32[]{:S(2)}) %collective-permute-start.7) | collective-permute-done | bytes 524320 | tf_op jit(solution)/shard_map/ppermute | solution.py:322
  72.6 19.4 %collective-permute-done.10 = bf16[128,2048]{1,0:T(8,128)(2,1)S(1)} collective-permute-done((bf16[128,2048]{1,0:T(8,128)(2,1)S(1)}, bf16[128,2048]{1,0:T(8,128)(2,1)S(1)}, u32[]{:S(2)}, u32[]{:S(2)}) %collective-permute-start.10) | collective-permute-done | bytes 524320 | tf_op jit(solution)/shard_map/ppermute | solution.py:322
  104.0 2.8 convert_reduce_fusion
  106.9 3.4 fusion.2
  111.3 11.8 %add_convert_fusion.q_ref.k_in.v_in = bf16[1024,1536]{1,0:T(8,128)(2,1)} fusion(bf16[2048,1536]{1,0:T(8,128)(2,1)} %all-gather.4.cloned.1.call-done, f32[1536]{0:T(1024)S(1)} %pad_maximum_fusion.26, bf16[1024,2048]{1,0:T(8,128)(2,1)} %constant_dynamic-update-slice_fusion, f32[2048]{0:T(1024)S(1)} %add.322, f32[2048]{0:T(1024)S(1)} %mul.194, ...), kind=kOutput, calls=%fused_computation.23 | convolution fusion | flops 6458179584 | bytes 13662208 | tf_op jit(solution)/shard_map/dot_general | solution.py:38
  124.6 6.7 %collective-permute-done.17 = bf16[128,2048]{1,0:T(8,128)(2,1)S(1)} collective-permute-done((bf16[128,2048]{1,0:T(8,128)(2,1)S(1)}, bf16[128,2048]{1,0:T(8,128)(2,1)S(1)}, u32[]{:S(2)}, u32[]{:S(2)}) %collective-permute-start.17) | collective-permute-done | bytes 524320 | tf_op jit(solution)/shard_map/ppermute | solution.py:322
  135.8 21.4 %attend_forward.1 = (bf16[1024,512]{1,0:T(8,128)(2,1)S(1)}, bf16[8,1024,1024]{2,1,0:T(8,128)(2,1)}) custom-call(s32[1]{0:T(128)} %bitcast.8.me_ref.spot_ref, f32[8]{0:T(128)S(1)} %multiply_exponential_fusion.slope_ref, s32[1024,1]{1,0:T(8,128)S(1)} %bitcast.130, bf16[1024,1536]{1,0:T(8,128)(2,1)} %add_convert_fusion.q_ref.k_in.v_in, ...), custom_call_target="tpu_custom_call" | custom-call | flops 4294967296 | bytes 16777216 | tf_op jit(solution)/shard_map/attend_forward/pallas_call | solution.py:124
  157.3 2.5 collective-permute-done.24
  164.6 2.3 pad_maximum_fusion
  171.8 4.6 collective-permute-done.26.refs_1_
  176.4 6.4 %collective-permute-done.27.refs_2_ = bf16[256,512]{1,0:T(8,128)(2,1)S(1)} collective-permute-done((bf16[256,512]{1,0:T(8,128)(2,1)S(1)}, bf16[256,512]{1,0:T(8,128)(2,1)S(1)}, u32[]{:S(2)}, u32[]{:S(2)}) %collective-permute-start.27) | collective-permute-done | bytes 262176 | tf_op jit(solution)/shard_map/ppermute | solution.py:322
  184.4 3.4 fusion.94
  187.9 4.1 fusion.91
  197.1 10.7 %collective-permute-done.30 = bf16[128,2048]{1,0:T(8,128)(2,1)S(1)} collective-permute-done((bf16[128,2048]{1,0:T(8,128)(2,1)S(1)}, bf16[128,2048]{1,0:T(8,128)(2,1)S(1)}, u32[]{:S(2)}, u32[]{:S(2)}) %collective-permute-start.30) | collective-permute-done | bytes 524320 | tf_op jit(solution)/shard_map/ppermute | solution.py:322
  209.9 9.1 %collective-permute-done.31 = bf16[128,2048]{1,0:T(8,128)(2,1)S(1)} collective-permute-done((bf16[128,2048]{1,0:T(8,128)(2,1)S(1)}, bf16[128,2048]{1,0:T(8,128)(2,1)S(1)}, u32[]{:S(2)}, u32[]{:S(2)}) %collective-permute-start.31) | collective-permute-done | bytes 524320 | tf_op jit(solution)/shard_map/ppermute | solution.py:322
  220.4 9.6 %collective-permute-done.34 = bf16[128,2048]{1,0:T(8,128)(2,1)S(1)} collective-permute-done((bf16[128,2048]{1,0:T(8,128)(2,1)S(1)}, bf16[128,2048]{1,0:T(8,128)(2,1)S(1)}, u32[]{:S(2)}, u32[]{:S(2)}) %collective-permute-start.34) | collective-permute-done | bytes 524320 | tf_op jit(solution)/shard_map/ppermute | solution.py:322
  235.7 15.2 %multiply_convert_fusion = (bf16[1024,2048]{1,0:T(8,128)(2,1)S(1)}, f32[1024,2048]{1,0:T(8,128)}) fusion(f32[2048]{0:T(1024)S(1)} %bitcast.152, bf16[1024,2048]{1,0:T(8,128)(2,1)} %copy-done.41, bf16[2048,2048]{1,0:T(8,128)(2,1)} %all-gather.6.cloned.1.call-done), kind=kOutput, calls=%fused_computation.17 | convolution fusion | flops 8602517504 | bytes 25174016 | tf_op jit(solution)/shard_map/dot_general | solution.py:38
  250.9 2.2 constant_dynamic-update-slice_fusion.58
  253.2 1.9 constant_dynamic-update-slice_fusion.57
  255.1 1.9 constant_dynamic-update-slice_fusion.56
  257.0 1.9 constant_dynamic-update-slice_fusion.55
  258.9 1.9 constant_dynamic-update-slice_fusion.54
  260.8 13.4 %convolution_convert_fusion.2 = bf16[2048,2048]{1,0:T(8,128)(2,1)} fusion(bf16[1024,2048]{1,0:T(8,128)(2,1)S(1)} %get-tuple-element.168, bf16[1024,2048]{1,0:T(8,128)(2,1)} %constant_dynamic-update-slice_fusion.54), kind=kOutput, calls=%fused_computation.21 | convolution fusion | flops 8594128896 | bytes 16777216 | tf_op jit(solution)/shard_map/dot_general | solution.py:38
  274.2 2.3 all-gather.8.cloned.1.call-done
  276.5 16.7 %convert_reduce_fusion.1 = (f32[2048]{0:T(1024)S(1)}, bf16[1024,2048]{1,0:T(8,128)(2,1)S(1)}) fusion(f32[1024,2048]{1,0:T(8,128)} %get-tuple-element.358, f32[2048]{0:T(1024)S(1)} %bitcast.153, bf16[1024,2048]{1,0:T(8,128)(2,1)} %constant_dynamic-update-slice_fusion.54, bf16[2048,2048]{1,0:T(8,128)(2,1)} %all-gather.8.cloned.1.call-done), kind=kOutput, calls=%fused_computation.15 | convolution fusion | flops 8617195520 | bytes 25182208 | tf_op jit(solution)/shard_map/dot_general | solution.py:38
  293.2 7.5 %convolution_convert_fusion.5 = bf16[256,2048]{1,0:T(8,128)(2,1)S(1)} fusion(bf16[2048,2048]{1,0:T(8,128)(2,1)} %all-gather.6.cloned.1.call-done, bf16[1024,2048]{1,0:T(8,128)(2,1)S(1)} %get-tuple-element.364), kind=kOutput, calls=%fused_computation.36 | convolution fusion | flops 2148007936 | bytes 10485760 | tf_op jit(solution)/shard_map/dot_general | solution.py:38
  303.9 10.2 %fusion.92 = (bf16[768,2048]{1,0:T(8,128)(2,1)S(1)}, f32[768,2048]{1,0:T(8,128)S(1)}) fusion(bf16[2048,2048]{1,0:T(8,128)(2,1)} %all-gather.6.cloned.1.call-done, bf16[1024,2048]{1,0:T(8,128)(2,1)} %copy-done.52), kind=kOutput, calls=%fused_computation.321 | convolution fusion | flops 6444023808 | bytes 20971520 | tf_op jit(solution)/shard_map/dot_general | solution.py:38
  317.8 10.6 %collective-permute-done.38 = bf16[128,2048]{1,0:T(8,128)(2,1)S(1)} collective-permute-done((bf16[128,2048]{1,0:T(8,128)(2,1)S(1)}, bf16[128,2048]{1,0:T(8,128)(2,1)S(1)}, u32[]{:S(2)}, u32[]{:S(2)}) %collective-permute-start.38) | collective-permute-done | bytes 524320 | tf_op jit(solution)/shard_map/ppermute | solution.py:322
  328.4 2.2 collective-permute-done.40
  333.6 11.6 %convolution_convert_fusion.1 = bf16[2048,2048]{1,0:T(8,128)(2,1)} fusion(bf16[1024,2048]{1,0:T(8,128)(2,1)S(1)} %copy-done.42, bf16[1024,2048]{1,0:T(8,128)(2,1)S(1)} %copy-done.53), kind=kOutput, calls=%fused_computation.20 | convolution fusion | flops 8594128896 | bytes 16777216 | tf_op jit(solution)/shard_map/dot_general | solution.py:38
  346.9 2.7 pad_maximum_fusion.1
  349.7 2.7 multiply_reduce_fusion
  352.4 2.3 fusion.76
  354.7 3.8 fusion.95.own_ref
  358.6 3.6 fusion.96.other_ref
  366.7 1.9 collective-permute-start.46
  368.7 11.3 %fusion.97 = f32[1024,2048]{1,0:T(8,128)} fusion(bf16[1024,2048]{1,0:T(8,128)(2,1)S(1)} %copy-done.55, bf16[2048,2048]{1,0:T(8,128)(2,1)S(1)} %bitcast.168), kind=kOutput, calls=%fused_computation.326 | convolution fusion | flops 8589934592 | bytes 20971520 | tf_op jit(solution)/shard_map/dot_general | solution.py:38
  383.0 2.6 copy-done
  391.0 22.0 %attend_backward.1 = (bf16[1024,512]{1,0:T(8,128)(2,1)S(1)}, bf16[1024,512]{1,0:T(8,128)(2,1)S(1)}, bf16[1024,512]{1,0:T(8,128)(2,1)S(1)}) custom-call(s32[1]{0:T(128)} %bitcast.8.me_ref.spot_ref, bf16[8,1024,1024]{2,1,0:T(8,128)(2,1)} %get-tuple-element.170.probs_ref, bf16[1024,1536]{1,0:T(8,128)(2,1)} %add_convert_fusion.q_ref.k_in.v_in, ...), custom_call_target="tpu_custom_call" | custom-call | flops 8589934592 | bytes 16777216 | tf_op jit(solution)/shard_map/attend_backward/pallas_call | solution.py:157
  414.9 12.8 %convolution_convert_fusion = bf16[2048,1536]{1,0:T(8,128)(2,1)} fusion(bf16[1024,1536]{1,0:T(8,128)(2,1)S(1)} %constant_dynamic-update-slice_fusion.62, bf16[1024,2048]{1,0:T(8,128)(2,1)} %constant_dynamic-update-slice_fusion, f32[2048]{0:T(1024)S(1)} %copy-done.49, f32[2048]{0:T(1024)S(1)} %copy-done.44, f32[1024]{0:T(1024)S(1)} %copy-done.51, ...), kind=kOutput, calls=%fused_computation.19 | convolution fusion | flops 6458179584 | bytes 13656064 | tf_op jit(solution)/shard_map/dot_general | solution.py:38
  434.3 4.2 convert.24
  443.5 4.3 fusion.78
  449.7 6.9 %fusion.93 = (bf16[768,2048]{1,0:T(8,128)(2,1)S(1)}, f32[768,2048]{1,0:T(8,128)}) fusion(bf16[2048,1536]{1,0:T(8,128)(2,1)S(1)} %bitcast.170, bf16[1024,1536]{1,0:T(8,128)(2,1)S(1)} %copy-done.10), kind=kOutput, calls=%fused_computation.322 | convolution fusion | flops 4833411072 | bytes 18087936 | tf_op jit(solution)/shard_map/dot_general | solution.py:38
  461.9 3.7 collective-permute-done.58
  467.9 2.8 convert_element_type.322
  470.7 6.2 %collective-permute-done.54 = bf16[128,2048]{1,0:T(8,128)(2,1)} collective-permute-done((bf16[128,2048]{1,0:T(8,128)(2,1)}, bf16[128,2048]{1,0:T(8,128)(2,1)}, u32[]{:S(2)}, u32[]{:S(2)}) %collective-permute-start.54) | collective-permute-done | bytes 524320 | tf_op jit(solution)/shard_map/ppermute | solution.py:322
  478.1 7.5 %collective-permute-done.52 = bf16[128,2048]{1,0:T(8,128)(2,1)} collective-permute-done((bf16[128,2048]{1,0:T(8,128)(2,1)}, bf16[128,2048]{1,0:T(8,128)(2,1)}, u32[]{:S(2)}, u32[]{:S(2)}) %collective-permute-start.52) | collective-permute-done | bytes 524320 | tf_op jit(solution)/shard_map/ppermute | solution.py:322
  493.6 1.9 collective-permute-start.66
  498.4 8.8 %collective-permute-done.64.refs_1_ = bf16[64,2048]{1,0:T(8,128)(2,1)S(1)} collective-permute-done((bf16[64,2048]{1,0:T(8,128)(2,1)S(1)}, bf16[64,2048]{1,0:T(8,128)(2,1)S(1)}, u32[]{:S(2)}, u32[]{:S(2)}) %collective-permute-start.64) | collective-permute-done | bytes 262176 | tf_op jit(solution)/shard_map/ppermute | solution.py:322
  508.3 8.5 %collective-permute-done.65.refs_2_ = bf16[64,2048]{1,0:T(8,128)(2,1)S(1)} collective-permute-done((bf16[64,2048]{1,0:T(8,128)(2,1)S(1)}, bf16[64,2048]{1,0:T(8,128)(2,1)S(1)}, u32[]{:S(2)}, u32[]{:S(2)}) %collective-permute-start.65) | collective-permute-done | bytes 262176 | tf_op jit(solution)/shard_map/ppermute | solution.py:322
  522.3 5.8 collective-permute-done.62
  530.2 5.2 collective-permute-done.60
  535.3 1.9 convert_add_fusion.3
  538.0 10.3 %collective-permute-done.77 = bf16[2,64,2048]{2,1,0:T(8,128)(2,1)S(1)} collective-permute-done((bf16[2,64,2048]{2,1,0:T(8,128)(2,1)S(1)}, bf16[2,64,2048]{2,1,0:T(8,128)(2,1)S(1)}, u32[]{:S(2)}, u32[]{:S(2)}) %collective-permute-start.77) | collective-permute-done | bytes 524320 | tf_op jit(solution)/shard_map/ppermute | solution.py:414
  555.6 3.3 fusion.28
  562.8 1.9 bitcast_convert_fusion
  566.3 2.0 collective-permute-start.68
  576.6 2.7 collective-permute-done.70
  (452 shorter events, 178.4 us)
Async XLA Ops:
  7.2 104.1 %all-gather.4.cloned.1.call-start = ((), (), s32[]{:S(2)}) async-start(), calls=%async_computation.3 | async-start | bytes 7077888 | tf_op jit(solution)/shard_map/all_gather | solution.py:469
  12.2 22.0 %collective-permute-start.3 = (bf16[80,2048]{1,0:T(8,128)(2,1)S(1)}, bf16[80,2048]{1,0:T(8,128)(2,1)S(1)}, u32[]{:S(2)}, u32[]{:S(2)}) collective-permute-start(bf16[80,2048]{1,0:T(8,128)(2,1)S(1)} %pad_maximum_fusion.11), channel_id=1, source_target_pairs={{0,8},{4,12},{8,16},{12,20},{16,24},{20,28},{24,0},{28,4},{1,9},{5... | collective-permute-start | bytes 983048 | tf_op jit(solution)/shard_map/ppermute | solution.py:525
  15.2 23.9 %collective-permute-start.4 = (bf16[80,2048]{1,0:T(8,128)(2,1)S(1)}, bf16[80,2048]{1,0:T(8,128)(2,1)S(1)}, u32[]{:S(2)}, u32[]{:S(2)}) collective-permute-start(bf16[80,2048]{1,0:T(8,128)(2,1)S(1)} %pad_maximum_fusion.11), channel_id=1, source_target_pairs={{0,16},{4,20},{8,24},{12,28},{16,0},{20,4},{24,8},{28,12},{1,17},{... | collective-permute-start | bytes 983048 | tf_op jit(solution)/shard_map/ppermute | solution.py:525
  17.8 21.3 %collective-permute-start.5 = (bf16[80,2048]{1,0:T(8,128)(2,1)S(1)}, bf16[80,2048]{1,0:T(8,128)(2,1)S(1)}, u32[]{:S(2)}, u32[]{:S(2)}) collective-permute-start(bf16[80,2048]{1,0:T(8,128)(2,1)S(1)} %pad_maximum_fusion.11), channel_id=1, source_target_pairs={{0,24},{4,28},{8,0},{12,4},{16,8},{20,12},{24,16},{28,20},{1,25},{... | collective-permute-start | bytes 983048 | tf_op jit(solution)/shard_map/ppermute | solution.py:525
  40.2 195.5 %all-gather.6.cloned.1.call-start = ((), (), s32[]{:S(2)}) async-start(), calls=%async_computation.4 | async-start | bytes 9437184 | tf_op jit(solution)/shard_map/all_gather | solution.py:469
  40.5 14.9 %collective-permute-start.6 = (bf16[128,2048]{1,0:T(8,128)(2,1)S(1)}, bf16[128,2048]{1,0:T(8,128)(2,1)S(1)}, u32[]{:S(2)}, u32[]{:S(2)}) collective-permute-start(bf16[128,2048]{1,0:T(8,128)(2,1)S(1)} %get-tuple-element.312), channel_id=1, source_target_pairs={{0,1},{1,0},{2,3},{3,2},{4,5},{5,4},{6,7},{7,6},{8,9},{9,8},{10,11... | collective-permute-start | bytes 1572872 | tf_op jit(solution)/shard_map/ppermute | solution.py:322
  42.0 26.9 %collective-permute-start.8 = (bf16[128,2048]{1,0:T(8,128)(2,1)S(1)}, bf16[128,2048]{1,0:T(8,128)(2,1)S(1)}, u32[]{:S(2)}, u32[]{:S(2)}) collective-permute-start(bf16[128,2048]{1,0:T(8,128)(2,1)S(1)} %get-tuple-element.312), channel_id=1, source_target_pairs={{0,2},{1,3},{2,0},{3,1},{4,6},{5,7},{6,4},{7,5},{8,10},{9,11},{10,... | collective-permute-start | bytes 1572872 | tf_op jit(solution)/shard_map/ppermute | solution.py:322
  43.5 23.0 %collective-permute-start.7 = (bf16[128,2048]{1,0:T(8,128)(2,1)S(1)}, bf16[128,2048]{1,0:T(8,128)(2,1)S(1)}, u32[]{:S(2)}, u32[]{:S(2)}) collective-permute-start(bf16[128,2048]{1,0:T(8,128)(2,1)S(1)} %get-tuple-element.311), channel_id=1, source_target_pairs={{0,1},{1,0},{2,3},{3,2},{4,5},{5,4},{6,7},{7,6},{8,9},{9,8},{10,11... | collective-permute-start | bytes 1572872 | tf_op jit(solution)/shard_map/ppermute | solution.py:322
  44.1 26.3 %collective-permute-start.9 = (bf16[128,2048]{1,0:T(8,128)(2,1)S(1)}, bf16[128,2048]{1,0:T(8,128)(2,1)S(1)}, u32[]{:S(2)}, u32[]{:S(2)}) collective-permute-start(bf16[128,2048]{1,0:T(8,128)(2,1)S(1)} %get-tuple-element.311), channel_id=1, source_target_pairs={{0,2},{1,3},{2,0},{3,1},{4,6},{5,7},{6,4},{7,5},{8,10},{9,11},{10,... | collective-permute-start | bytes 1572872 | tf_op jit(solution)/shard_map/ppermute | solution.py:322
  53.0 40.7 %collective-permute-start.13 = (bf16[80,2048]{1,0:T(8,128)(2,1)S(1)}, bf16[80,2048]{1,0:T(8,128)(2,1)S(1)}, u32[]{:S(2)}, u32[]{:S(2)}) collective-permute-start(bf16[80,2048]{1,0:T(8,128)(2,1)S(1)} %get-tuple-element.340), channel_id=1, source_target_pairs={{0,1},{1,0},{2,3},{3,2},{4,5},{5,4},{6,7},{7,6},{8,9},{9,8},{10,11... | collective-permute-start | bytes 983048 | tf_op jit(solution)/shard_map/ppermute | solution.py:322
  55.3 38.4 %collective-permute-start.14 = (bf16[80,2048]{1,0:T(8,128)(2,1)S(1)}, bf16[80,2048]{1,0:T(8,128)(2,1)S(1)}, u32[]{:S(2)}, u32[]{:S(2)}) collective-permute-start(bf16[80,2048]{1,0:T(8,128)(2,1)S(1)} %get-tuple-element.341), channel_id=1, source_target_pairs={{0,2},{1,3},{2,0},{3,1},{4,6},{5,7},{6,4},{7,5},{8,10},{9,11},{10,... | collective-permute-start | bytes 983048 | tf_op jit(solution)/shard_map/ppermute | solution.py:322
  66.6 25.4 %collective-permute-start.10 = (bf16[128,2048]{1,0:T(8,128)(2,1)S(1)}, bf16[128,2048]{1,0:T(8,128)(2,1)S(1)}, u32[]{:S(2)}, u32[]{:S(2)}) collective-permute-start(bf16[128,2048]{1,0:T(8,128)(2,1)S(1)} %collective-permute-done.6), channel_id=1, source_target_pairs={{0,2},{1,3},{2,0},{3,1},{4,6},{5,7},{6,4},{7,5},{8,10},{9,11},{10,... | collective-permute-start | bytes 1572872 | tf_op jit(solution)/shard_map/ppermute | solution.py:322
  68.9 24.8 %collective-permute-start.15 = (bf16[80,2048]{1,0:T(8,128)(2,1)S(1)}, bf16[80,2048]{1,0:T(8,128)(2,1)S(1)}, u32[]{:S(2)}, u32[]{:S(2)}) collective-permute-start(bf16[80,2048]{1,0:T(8,128)(2,1)S(1)} %get-tuple-element.339), channel_id=1, source_target_pairs={{0,3},{1,2},{2,1},{3,0},{4,7},{5,6},{6,5},{7,4},{8,11},{9,10},{10,... | collective-permute-start | bytes 983048 | tf_op jit(solution)/shard_map/ppermute | solution.py:322
  70.4 22.5 %collective-permute-start.11 = (bf16[128,2048]{1,0:T(8,128)(2,1)S(1)}, bf16[128,2048]{1,0:T(8,128)(2,1)S(1)}, u32[]{:S(2)}, u32[]{:S(2)}) collective-permute-start(bf16[128,2048]{1,0:T(8,128)(2,1)S(1)} %collective-permute-done.9), channel_id=1, source_target_pairs={{0,1},{1,0},{2,3},{3,2},{4,5},{5,4},{6,7},{7,6},{8,9},{9,8},{10,11... | collective-permute-start | bytes 1572872 | tf_op jit(solution)/shard_map/ppermute | solution.py:322
  95.7 180.8 %all-gather.8.cloned.1.call-start = ((), (), s32[]{:S(2)}) async-start(), calls=%async_computation.5 | async-start | bytes 9437184 | tf_op jit(solution)/shard_map/all_gather | solution.py:469
  96.1 37.9 %collective-permute-start.20 = (bf16[128,2048]{1,0:T(8,128)(2,1)S(1)}, bf16[128,2048]{1,0:T(8,128)(2,1)}, u32[]{:S(2)}, u32[]{:S(2)}) collective-permute-start(bf16[128,2048]{1,0:T(8,128)(2,1)S(1)} %get-tuple-element.151), channel_id=1, source_target_pairs={{0,1},{1,0},{2,3},{3,2},{4,5},{5,4},{6,7},{7,6},{8,9},{9,8},{10,11... | collective-permute-start | bytes 1572872 | tf_op jit(solution)/shard_map/ppermute | solution.py:322
  97.6 25.5 %collective-permute-start.16 = (bf16[128,2048]{1,0:T(8,128)(2,1)}, bf16[128,2048]{1,0:T(8,128)(2,1)}, u32[]{:S(2)}, u32[]{:S(2)}) collective-permute-start(bf16[128,2048]{1,0:T(8,128)(2,1)} %get-tuple-element.135), channel_id=1, source_target_pairs={{0,1},{1,0},{2,3},{3,2},{4,5},{5,4},{6,7},{7,6},{8,9},{9,8},{10,11... | collective-permute-start | bytes 1572872 | tf_op jit(solution)/shard_map/ppermute | solution.py:322
  99.1 32.8 %collective-permute-start.18 = (bf16[128,2048]{1,0:T(8,128)(2,1)}, bf16[128,2048]{1,0:T(8,128)(2,1)S(1)}, u32[]{:S(2)}, u32[]{:S(2)}) collective-permute-start(bf16[128,2048]{1,0:T(8,128)(2,1)} %get-tuple-element.135), channel_id=1, source_target_pairs={{0,2},{1,3},{2,0},{3,1},{4,6},{5,7},{6,4},{7,5},{8,10},{9,11},{10,... | collective-permute-start | bytes 1572872 | tf_op jit(solution)/shard_map/ppermute | solution.py:322
  100.6 30.7 %collective-permute-start.17 = (bf16[128,2048]{1,0:T(8,128)(2,1)S(1)}, bf16[128,2048]{1,0:T(8,128)(2,1)S(1)}, u32[]{:S(2)}, u32[]{:S(2)}) collective-permute-start(bf16[128,2048]{1,0:T(8,128)(2,1)S(1)} %get-tuple-element.136), channel_id=1, source_target_pairs={{0,1},{1,0},{2,3},{3,2},{4,5},{5,4},{6,7},{7,6},{8,9},{9,8},{10,11... | collective-permute-start | bytes 1572872 | tf_op jit(solution)/shard_map/ppermute | solution.py:322
  101.1 32.3 %collective-permute-start.19 = (bf16[128,2048]{1,0:T(8,128)(2,1)S(1)}, bf16[128,2048]{1,0:T(8,128)(2,1)}, u32[]{:S(2)}, u32[]{:S(2)}) collective-permute-start(bf16[128,2048]{1,0:T(8,128)(2,1)S(1)} %get-tuple-element.136), channel_id=1, source_target_pairs={{0,2},{1,3},{2,0},{3,1},{4,6},{5,7},{6,4},{7,5},{8,10},{9,11},{10,... | collective-permute-start | bytes 1572872 | tf_op jit(solution)/shard_map/ppermute | solution.py:322
  123.1 34.2 %collective-permute-start.22 = (bf16[128,2048]{1,0:T(8,128)(2,1)S(1)}, bf16[128,2048]{1,0:T(8,128)(2,1)}, u32[]{:S(2)}, u32[]{:S(2)}) collective-permute-start(bf16[128,2048]{1,0:T(8,128)(2,1)S(1)} %get-tuple-element.151), channel_id=1, source_target_pairs={{0,2},{1,3},{2,0},{3,1},{4,6},{5,7},{6,4},{7,5},{8,10},{9,11},{10,... | collective-permute-start | bytes 1572872 | tf_op jit(solution)/shard_map/ppermute | solution.py:322
  131.3 26.0 %collective-permute-start.21 = (bf16[128,2048]{1,0:T(8,128)(2,1)S(1)}, bf16[128,2048]{1,0:T(8,128)(2,1)}, u32[]{:S(2)}, u32[]{:S(2)}) collective-permute-start(bf16[128,2048]{1,0:T(8,128)(2,1)S(1)} %get-tuple-element.152), channel_id=1, source_target_pairs={{0,1},{1,0},{2,3},{3,2},{4,5},{5,4},{6,7},{7,6},{8,9},{9,8},{10,11... | collective-permute-start | bytes 1572872 | tf_op jit(solution)/shard_map/ppermute | solution.py:322
  131.8 25.4 %collective-permute-start.23 = (bf16[128,2048]{1,0:T(8,128)(2,1)S(1)}, bf16[128,2048]{1,0:T(8,128)(2,1)}, u32[]{:S(2)}, u32[]{:S(2)}) collective-permute-start(bf16[128,2048]{1,0:T(8,128)(2,1)S(1)} %get-tuple-element.152), channel_id=1, source_target_pairs={{0,2},{1,3},{2,0},{3,1},{4,6},{5,7},{6,4},{7,5},{8,10},{9,11},{10,... | collective-permute-start | bytes 1572872 | tf_op jit(solution)/shard_map/ppermute | solution.py:322
  133.4 26.4 %collective-permute-start.24 = (bf16[128,2048]{1,0:T(8,128)(2,1)}, bf16[128,2048]{1,0:T(8,128)(2,1)}, u32[]{:S(2)}, u32[]{:S(2)}) collective-permute-start(bf16[128,2048]{1,0:T(8,128)(2,1)} %collective-permute-done.16), channel_id=1, source_target_pairs={{0,2},{1,3},{2,0},{3,1},{4,6},{5,7},{6,4},{7,5},{8,10},{9,11},{10,... | collective-permute-start | bytes 1572872 | tf_op jit(solution)/shard_map/ppermute | solution.py:322
  133.9 25.9 %collective-permute-start.25 = (bf16[128,2048]{1,0:T(8,128)(2,1)}, bf16[128,2048]{1,0:T(8,128)(2,1)}, u32[]{:S(2)}, u32[]{:S(2)}) collective-permute-start(bf16[128,2048]{1,0:T(8,128)(2,1)} %collective-permute-done.19), channel_id=1, source_target_pairs={{0,1},{1,0},{2,3},{3,2},{4,5},{5,4},{6,7},{7,6},{8,9},{9,8},{10,11... | collective-permute-start | bytes 1572872 | tf_op jit(solution)/shard_map/ppermute | solution.py:322
  166.9 17.5 %collective-permute-start.29 = (bf16[1024,2048]{1,0:T(8,128)(2,1)}, bf16[1024,2048]{1,0:T(8,128)(2,1)}, u32[]{:S(2)}, u32[]{:S(2)}) collective-permute-start(bf16[1024,2048]{1,0:T(8,128)(2,1)} %bitcast.30), channel_id=1, source_target_pairs={{0,4},{4,0},{8,12},{12,8},{16,20},{20,16},{24,28},{28,24},{1,5},{5... | collective-permute-start | bytes 12582920 | tf_op jit(solution)/shard_map/ppermute | solution.py:424
  166.9 260.9 %reduce-scatter.4.cloned.1.call-start = ((), (), s32[]{:S(2)}) async-start(), calls=%async_computation.6 | async-start | bytes 9437184 | tf_op jit(solution)/shard_map/reduce_scatter | solution.py:483
  192.9 14.9 %collective-permute-start.30 = (bf16[128,2048]{1,0:T(8,128)(2,1)S(1)}, bf16[128,2048]{1,0:T(8,128)(2,1)S(1)}, u32[]{:S(2)}, u32[]{:S(2)}) collective-permute-start(bf16[128,2048]{1,0:T(8,128)(2,1)S(1)} %get-tuple-element.266), channel_id=1, source_target_pairs={{0,1},{1,0},{2,3},{3,2},{4,5},{5,4},{6,7},{7,6},{8,9},{9,8},{10,11... | collective-permute-start | bytes 1572872 | tf_op jit(solution)/shard_map/ppermute | solution.py:322
  194.2 15.1 %collective-permute-start.33 = (bf16[128,2048]{1,0:T(8,128)(2,1)S(1)}, bf16[128,2048]{1,0:T(8,128)(2,1)S(1)}, u32[]{:S(2)}, u32[]{:S(2)}) collective-permute-start(bf16[128,2048]{1,0:T(8,128)(2,1)S(1)} %get-tuple-element.265), channel_id=1, source_target_pairs={{0,2},{1,3},{2,0},{3,1},{4,6},{5,7},{6,4},{7,5},{8,10},{9,11},{10,... | collective-permute-start | bytes 1572872 | tf_op jit(solution)/shard_map/ppermute | solution.py:322
  195.0 24.0 %collective-permute-start.31 = (bf16[128,2048]{1,0:T(8,128)(2,1)S(1)}, bf16[128,2048]{1,0:T(8,128)(2,1)S(1)}, u32[]{:S(2)}, u32[]{:S(2)}) collective-permute-start(bf16[128,2048]{1,0:T(8,128)(2,1)S(1)} %get-tuple-element.265), channel_id=1, source_target_pairs={{0,1},{1,0},{2,3},{3,2},{4,5},{5,4},{6,7},{7,6},{8,9},{9,8},{10,11... | collective-permute-start | bytes 1572872 | tf_op jit(solution)/shard_map/ppermute | solution.py:322
  196.5 23.8 %collective-permute-start.32 = (bf16[128,2048]{1,0:T(8,128)(2,1)S(1)}, bf16[128,2048]{1,0:T(8,128)(2,1)S(1)}, u32[]{:S(2)}, u32[]{:S(2)}) collective-permute-start(bf16[128,2048]{1,0:T(8,128)(2,1)S(1)} %get-tuple-element.266), channel_id=1, source_target_pairs={{0,2},{1,3},{2,0},{3,1},{4,6},{5,7},{6,4},{7,5},{8,10},{9,11},{10,... | collective-permute-start | bytes 1572872 | tf_op jit(solution)/shard_map/ppermute | solution.py:322
  207.8 22.2 %collective-permute-start.34 = (bf16[128,2048]{1,0:T(8,128)(2,1)S(1)}, bf16[128,2048]{1,0:T(8,128)(2,1)S(1)}, u32[]{:S(2)}, u32[]{:S(2)}) collective-permute-start(bf16[128,2048]{1,0:T(8,128)(2,1)S(1)} %collective-permute-done.30), channel_id=1, source_target_pairs={{0,2},{1,3},{2,0},{3,1},{4,6},{5,7},{6,4},{7,5},{8,10},{9,11},{10,... | collective-permute-start | bytes 1572872 | tf_op jit(solution)/shard_map/ppermute | solution.py:322
  209.3 20.7 %collective-permute-start.35 = (bf16[128,2048]{1,0:T(8,128)(2,1)S(1)}, bf16[128,2048]{1,0:T(8,128)(2,1)S(1)}, u32[]{:S(2)}, u32[]{:S(2)}) collective-permute-start(bf16[128,2048]{1,0:T(8,128)(2,1)S(1)} %collective-permute-done.33), channel_id=1, source_target_pairs={{0,1},{1,0},{2,3},{3,2},{4,5},{5,4},{6,7},{7,6},{8,9},{9,8},{10,11... | collective-permute-start | bytes 1572872 | tf_op jit(solution)/shard_map/ppermute | solution.py:322
  230.1 26.8 %collective-permute-start.36 = (bf16[128,2048]{1,0:T(8,128)(2,1)}, bf16[128,2048]{1,0:T(8,128)(2,1)}, u32[]{:S(2)}, u32[]{:S(2)}) collective-permute-start(bf16[128,2048]{1,0:T(8,128)(2,1)} %collective-permute-done.20), channel_id=1, source_target_pairs={{0,2},{1,3},{2,0},{3,1},{4,6},{5,7},{6,4},{7,5},{8,10},{9,11},{10,... | collective-permute-start | bytes 1572872 | tf_op jit(solution)/shard_map/ppermute | solution.py:322
  230.8 28.1 %collective-permute-start.37 = (bf16[128,2048]{1,0:T(8,128)(2,1)}, bf16[128,2048]{1,0:T(8,128)(2,1)}, u32[]{:S(2)}, u32[]{:S(2)}) collective-permute-start(bf16[128,2048]{1,0:T(8,128)(2,1)} %collective-permute-done.23), channel_id=1, source_target_pairs={{0,1},{1,0},{2,3},{3,2},{4,5},{5,4},{6,7},{7,6},{8,9},{9,8},{10,11... | collective-permute-start | bytes 1572872 | tf_op jit(solution)/shard_map/ppermute | solution.py:322
  276.5 209.5 %reduce-scatter.6.cloned.1.call-start = ((), (), s32[]{:S(2)}) async-start(), calls=%async_computation.7 | async-start | bytes 9437184 | tf_op jit(solution)/shard_map/reduce_scatter | solution.py:483
  302.4 15.3 %collective-permute-start.42 = (bf16[128,2048]{1,0:T(8,128)(2,1)S(1)}, bf16[128,2048]{1,0:T(8,128)(2,1)S(1)}, u32[]{:S(2)}, u32[]{:S(2)}) collective-permute-start(bf16[128,2048]{1,0:T(8,128)(2,1)S(1)} %get-tuple-element.264), channel_id=1, source_target_pairs={{0,2},{1,3},{2,0},{3,1},{4,6},{5,7},{6,4},{7,5},{8,10},{9,11},{10,... | collective-permute-start | bytes 1572872 | tf_op jit(solution)/shard_map/ppermute | solution.py:322
  315.7 14.9 %collective-permute-start.40 = (bf16[128,2048]{1,0:T(8,128)(2,1)S(1)}, bf16[128,2048]{1,0:T(8,128)(2,1)S(1)}, u32[]{:S(2)}, u32[]{:S(2)}) collective-permute-start(bf16[128,2048]{1,0:T(8,128)(2,1)S(1)} %fusion.42), channel_id=1, source_target_pairs={{0,2},{1,3},{2,0},{3,1},{4,6},{5,7},{6,4},{7,5},{8,10},{9,11},{10,... | collective-permute-start | bytes 1572872 | tf_op jit(solution)/shard_map/ppermute | solution.py:322
  316.6 28.6 %collective-permute-start.41 = (bf16[128,2048]{1,0:T(8,128)(2,1)}, bf16[128,2048]{1,0:T(8,128)(2,1)}, u32[]{:S(2)}, u32[]{:S(2)}) collective-permute-start(bf16[128,2048]{1,0:T(8,128)(2,1)} %get-tuple-element.240), channel_id=1, source_target_pairs={{0,2},{1,3},{2,0},{3,1},{4,6},{5,7},{6,4},{7,5},{8,10},{9,11},{10,... | collective-permute-start | bytes 1572872 | tf_op jit(solution)/shard_map/ppermute | solution.py:322
  349.6 206.0 %reduce-scatter.8.cloned.1.call-start = ((), (), s32[]{:S(2)}) async-start(), calls=%async_computation.8 | async-start | bytes 7077888 | tf_op jit(solution)/shard_map/reduce_scatter | solution.py:483
  365.0 16.0 %collective-permute-start.47 = (bf16[1024,2048]{1,0:T(8,128)(2,1)S(1)}, bf16[1024,2048]{1,0:T(8,128)(2,1)S(1)}, u32[]{:S(2)}, u32[]{:S(2)}) collective-permute-start(bf16[1024,2048]{1,0:T(8,128)(2,1)S(1)} %convolution_convert_fusion.3), channel_id=1, source_target_pairs={{0,4},{4,0},{8,12},{12,8},{16,20},{20,16},{24,28},{28,24},{1,5},{5... | collective-permute-start | bytes 12582920 | tf_op jit(solution)/shard_map/ppermute | solution.py:424
  386.9 40.8 %collective-permute-start.48 = (bf16[128,2048]{1,0:T(8,128)(2,1)}, bf16[128,2048]{1,0:T(8,128)(2,1)}, u32[]{:S(2)}, u32[]{:S(2)}) collective-permute-start(bf16[128,2048]{1,0:T(8,128)(2,1)} %bitcast.34), channel_id=1, source_target_pairs={{0,1},{1,0},{2,3},{3,2},{4,5},{5,4},{6,7},{7,6},{8,9},{9,8},{10,11... | collective-permute-start | bytes 1572872 | tf_op jit(solution)/shard_map/ppermute | solution.py:322
  388.2 39.5 %collective-permute-start.49 = (bf16[128,2048]{1,0:T(8,128)(2,1)}, bf16[128,2048]{1,0:T(8,128)(2,1)}, u32[]{:S(2)}, u32[]{:S(2)}) collective-permute-start(bf16[128,2048]{1,0:T(8,128)(2,1)} %bitcast.35), channel_id=1, source_target_pairs={{0,2},{1,3},{2,0},{3,1},{4,6},{5,7},{6,4},{7,5},{8,10},{9,11},{10,... | collective-permute-start | bytes 1572872 | tf_op jit(solution)/shard_map/ppermute | solution.py:322
  389.1 38.6 %collective-permute-start.50 = (bf16[128,2048]{1,0:T(8,128)(2,1)}, bf16[128,2048]{1,0:T(8,128)(2,1)}, u32[]{:S(2)}, u32[]{:S(2)}) collective-permute-start(bf16[128,2048]{1,0:T(8,128)(2,1)} %bitcast.36), channel_id=1, source_target_pairs={{0,1},{1,0},{2,3},{3,2},{4,5},{5,4},{6,7},{7,6},{8,9},{9,8},{10,11... | collective-permute-start | bytes 1572872 | tf_op jit(solution)/shard_map/ppermute | solution.py:322
  389.9 37.8 %collective-permute-start.51 = (bf16[128,2048]{1,0:T(8,128)(2,1)}, bf16[128,2048]{1,0:T(8,128)(2,1)}, u32[]{:S(2)}, u32[]{:S(2)}) collective-permute-start(bf16[128,2048]{1,0:T(8,128)(2,1)} %bitcast.37), channel_id=1, source_target_pairs={{0,2},{1,3},{2,0},{3,1},{4,6},{5,7},{6,4},{7,5},{8,10},{9,11},{10,... | collective-permute-start | bytes 1572872 | tf_op jit(solution)/shard_map/ppermute | solution.py:322
  439.5 20.6 %collective-permute-start.56 = (bf16[128,2048]{1,0:T(8,128)(2,1)S(1)}, bf16[128,2048]{1,0:T(8,128)(2,1)S(1)}, u32[]{:S(2)}, u32[]{:S(2)}) collective-permute-start(bf16[128,2048]{1,0:T(8,128)(2,1)S(1)} %get-tuple-element.232), channel_id=1, source_target_pairs={{0,1},{1,0},{2,3},{3,2},{4,5},{5,4},{6,7},{7,6},{8,9},{9,8},{10,11... | collective-permute-start | bytes 1572872 | tf_op jit(solution)/shard_map/ppermute | solution.py:322
  440.7 20.4 %collective-permute-start.57 = (bf16[128,2048]{1,0:T(8,128)(2,1)S(1)}, bf16[128,2048]{1,0:T(8,128)(2,1)S(1)}, u32[]{:S(2)}, u32[]{:S(2)}) collective-permute-start(bf16[128,2048]{1,0:T(8,128)(2,1)S(1)} %get-tuple-element.231), channel_id=1, source_target_pairs={{0,2},{1,3},{2,0},{3,1},{4,6},{5,7},{6,4},{7,5},{8,10},{9,11},{10,... | collective-permute-start | bytes 1572872 | tf_op jit(solution)/shard_map/ppermute | solution.py:322
  441.6 24.0 %collective-permute-start.58 = (bf16[128,2048]{1,0:T(8,128)(2,1)S(1)}, bf16[128,2048]{1,0:T(8,128)(2,1)S(1)}, u32[]{:S(2)}, u32[]{:S(2)}) collective-permute-start(bf16[128,2048]{1,0:T(8,128)(2,1)S(1)} %get-tuple-element.230), channel_id=1, source_target_pairs={{0,1},{1,0},{2,3},{3,2},{4,5},{5,4},{6,7},{7,6},{8,9},{9,8},{10,11... | collective-permute-start | bytes 1572872 | tf_op jit(solution)/shard_map/ppermute | solution.py:322
  442.4 28.3 %collective-permute-start.59 = (bf16[128,2048]{1,0:T(8,128)(2,1)}, bf16[128,2048]{1,0:T(8,128)(2,1)}, u32[]{:S(2)}, u32[]{:S(2)}) collective-permute-start(bf16[128,2048]{1,0:T(8,128)(2,1)} %get-tuple-element.229), channel_id=1, source_target_pairs={{0,2},{1,3},{2,0},{3,1},{4,6},{5,7},{6,4},{7,5},{8,10},{9,11},{10,... | collective-permute-start | bytes 1572872 | tf_op jit(solution)/shard_map/ppermute | solution.py:322
  457.7 19.2 %collective-permute-start.54 = (bf16[128,2048]{1,0:T(8,128)(2,1)}, bf16[128,2048]{1,0:T(8,128)(2,1)}, u32[]{:S(2)}, u32[]{:S(2)}) collective-permute-start(bf16[128,2048]{1,0:T(8,128)(2,1)} %get-tuple-element.238), channel_id=1, source_target_pairs={{0,1},{1,0},{2,3},{3,2},{4,5},{5,4},{6,7},{7,6},{8,9},{9,8},{10,11... | collective-permute-start | bytes 1572872 | tf_op jit(solution)/shard_map/ppermute | solution.py:322
  460.1 18.1 %collective-permute-start.55 = (bf16[128,2048]{1,0:T(8,128)(2,1)}, bf16[128,2048]{1,0:T(8,128)(2,1)}, u32[]{:S(2)}, u32[]{:S(2)}) collective-permute-start(bf16[128,2048]{1,0:T(8,128)(2,1)} %get-tuple-element.237), channel_id=1, source_target_pairs={{0,2},{1,3},{2,0},{3,1},{4,6},{5,7},{6,4},{7,5},{8,10},{9,11},{10,... | collective-permute-start | bytes 1572872 | tf_op jit(solution)/shard_map/ppermute | solution.py:322
  461.1 24.5 %collective-permute-start.52 = (bf16[128,2048]{1,0:T(8,128)(2,1)}, bf16[128,2048]{1,0:T(8,128)(2,1)}, u32[]{:S(2)}, u32[]{:S(2)}) collective-permute-start(bf16[128,2048]{1,0:T(8,128)(2,1)} %get-tuple-element.262), channel_id=1, source_target_pairs={{0,1},{1,0},{2,3},{3,2},{4,5},{5,4},{6,7},{7,6},{8,9},{9,8},{10,11... | collective-permute-start | bytes 1572872 | tf_op jit(solution)/shard_map/ppermute | solution.py:322
  465.6 20.4 %collective-permute-start.53 = (bf16[128,2048]{1,0:T(8,128)(2,1)}, bf16[128,2048]{1,0:T(8,128)(2,1)}, u32[]{:S(2)}, u32[]{:S(2)}) collective-permute-start(bf16[128,2048]{1,0:T(8,128)(2,1)} %get-tuple-element.261), channel_id=1, source_target_pairs={{0,2},{1,3},{2,0},{3,1},{4,6},{5,7},{6,4},{7,5},{8,10},{9,11},{10,... | collective-permute-start | bytes 1572872 | tf_op jit(solution)/shard_map/ppermute | solution.py:322
  487.6 31.8 %collective-permute-start.75 = (bf16[128,2048]{1,0:T(8,128)(2,1)S(1)}, bf16[128,2048]{1,0:T(8,128)(2,1)S(1)}, u32[]{:S(2)}, u32[]{:S(2)}) collective-permute-start(bf16[128,2048]{1,0:T(8,128)(2,1)S(1)} %fusion.47), channel_id=1, source_target_pairs={{0,1},{1,0},{2,3},{3,2},{4,5},{5,4},{6,7},{7,6},{8,9},{9,8},{10,11... | collective-permute-start | bytes 1572872 | tf_op jit(solution)/shard_map/ppermute | solution.py:322
  490.7 28.7 %collective-permute-start.76 = (bf16[128,2048]{1,0:T(8,128)(2,1)S(1)}, bf16[128,2048]{1,0:T(8,128)(2,1)S(1)}, u32[]{:S(2)}, u32[]{:S(2)}) collective-permute-start(bf16[128,2048]{1,0:T(8,128)(2,1)S(1)} %fusion.44), channel_id=1, source_target_pairs={{0,2},{1,3},{2,0},{3,1},{4,6},{5,7},{6,4},{7,5},{8,10},{9,11},{10,... | collective-permute-start | bytes 1572872 | tf_op jit(solution)/shard_map/ppermute | solution.py:322
  492.0 15.2 %collective-permute-start.64 = (bf16[64,2048]{1,0:T(8,128)(2,1)S(1)}, bf16[64,2048]{1,0:T(8,128)(2,1)S(1)}, u32[]{:S(2)}, u32[]{:S(2)}) collective-permute-start(bf16[64,2048]{1,0:T(8,128)(2,1)S(1)} %get-tuple-element.259), channel_id=1, source_target_pairs={{0,1},{1,0},{2,3},{3,2},{4,5},{5,4},{6,7},{7,6},{8,9},{9,8},{10,11... | collective-permute-start | bytes 786440 | tf_op jit(solution)/shard_map/ppermute | solution.py:322
  492.7 24.2 %collective-permute-start.65 = (bf16[64,2048]{1,0:T(8,128)(2,1)S(1)}, bf16[64,2048]{1,0:T(8,128)(2,1)S(1)}, u32[]{:S(2)}, u32[]{:S(2)}) collective-permute-start(bf16[64,2048]{1,0:T(8,128)(2,1)S(1)} %get-tuple-element.258), channel_id=1, source_target_pairs={{0,2},{1,3},{2,0},{3,1},{4,6},{5,7},{6,4},{7,5},{8,10},{9,11},{10,... | collective-permute-start | bytes 786440 | tf_op jit(solution)/shard_map/ppermute | solution.py:322
  493.6 24.3 %collective-permute-start.66 = (bf16[64,2048]{1,0:T(8,128)(2,1)S(1)}, bf16[64,2048]{1,0:T(8,128)(2,1)S(1)}, u32[]{:S(2)}, u32[]{:S(2)}) collective-permute-start(bf16[64,2048]{1,0:T(8,128)(2,1)S(1)} %get-tuple-element.257), channel_id=1, source_target_pairs={{0,3},{1,2},{2,1},{3,0},{4,7},{5,6},{6,5},{7,4},{8,11},{9,10},{10,... | collective-permute-start | bytes 786440 | tf_op jit(solution)/shard_map/ppermute | solution.py:322
  507.2 21.0 %collective-permute-start.62 = (bf16[128,2048]{1,0:T(8,128)(2,1)S(1)}, bf16[128,2048]{1,0:T(8,128)(2,1)S(1)}, u32[]{:S(2)}, u32[]{:S(2)}) collective-permute-start(bf16[128,2048]{1,0:T(8,128)(2,1)S(1)} %fusion.37), channel_id=1, source_target_pairs={{0,2},{1,3},{2,0},{3,1},{4,6},{5,7},{6,4},{7,5},{8,10},{9,11},{10,... | collective-permute-start | bytes 1572872 | tf_op jit(solution)/shard_map/ppermute | solution.py:322
  516.9 18.4 %collective-permute-start.60 = (bf16[128,2048]{1,0:T(8,128)(2,1)S(1)}, bf16[128,2048]{1,0:T(8,128)(2,1)S(1)}, u32[]{:S(2)}, u32[]{:S(2)}) collective-permute-start(bf16[128,2048]{1,0:T(8,128)(2,1)S(1)} %add_convert_fusion.3), channel_id=1, source_target_pairs={{0,2},{1,3},{2,0},{3,1},{4,6},{5,7},{6,4},{7,5},{8,10},{9,11},{10,... | collective-permute-start | bytes 1572872 | tf_op jit(solution)/shard_map/ppermute | solution.py:322
  521.3 27.0 %collective-permute-start.77 = (bf16[2,64,2048]{2,1,0:T(8,128)(2,1)S(1)}, bf16[2,64,2048]{2,1,0:T(8,128)(2,1)S(1)}, u32[]{:S(2)}, u32[]{:S(2)}) collective-permute-start(bf16[2,64,2048]{2,1,0:T(8,128)(2,1)S(1)} %bitcast.144), channel_id=1, source_target_pairs={{0,16},{4,20},{8,24},{12,28},{16,0},{20,4},{24,8},{28,12},{1,17},{... | collective-permute-start | bytes 1572872 | tf_op jit(solution)/shard_map/ppermute | solution.py:414
  529.7 20.2 %collective-permute-start.63 = (bf16[128,2048]{1,0:T(8,128)(2,1)S(1)}, bf16[128,2048]{1,0:T(8,128)(2,1)S(1)}, u32[]{:S(2)}, u32[]{:S(2)}) collective-permute-start(bf16[128,2048]{1,0:T(8,128)(2,1)S(1)} %get-tuple-element.226), channel_id=1, source_target_pairs={{0,1},{1,0},{2,3},{3,2},{4,5},{5,4},{6,7},{7,6},{8,9},{9,8},{10,11... | collective-permute-start | bytes 1572872 | tf_op jit(solution)/shard_map/ppermute | solution.py:322
  537.3 15.4 %collective-permute-start.61 = (bf16[128,2048]{1,0:T(8,128)(2,1)S(1)}, bf16[128,2048]{1,0:T(8,128)(2,1)S(1)}, u32[]{:S(2)}, u32[]{:S(2)}) collective-permute-start(bf16[128,2048]{1,0:T(8,128)(2,1)S(1)} %get-tuple-element.224), channel_id=1, source_target_pairs={{0,1},{1,0},{2,3},{3,2},{4,5},{5,4},{6,7},{7,6},{8,9},{9,8},{10,11... | collective-permute-start | bytes 1572872 | tf_op jit(solution)/shard_map/ppermute | solution.py:322
  569.6 15.1 %collective-permute-start.72 = (bf16[64,1536]{1,0:T(8,128)(2,1)S(1)}, bf16[64,1536]{1,0:T(8,128)(2,1)S(1)}, u32[]{:S(2)}, u32[]{:S(2)}) collective-permute-start(bf16[64,1536]{1,0:T(8,128)(2,1)S(1)} %get-tuple-element.315), channel_id=1, source_target_pairs={{0,1},{1,0},{2,3},{3,2},{4,5},{5,4},{6,7},{7,6},{8,9},{9,8},{10,11... | collective-permute-start | bytes 589832 | tf_op jit(solution)/shard_map/ppermute | solution.py:322
  (86 other events, 1119.7 us)
Sparse Core Ops, SparseCore 0:
  40.3 70.9 all-gather.3
  113.5 80.6 all-gather.5
  195.8 80.6 all-gather.7
  278.6 88.1 reduce-scatter.3
  368.9 87.9 reduce-scatter.5
  459.1 75.3 reduce-scatter.7

commit v5 on v4

--- a/solution.py
+++ b/solution.py
@@ -657,7 +657,6 @@
     out_term = scatter_near(out_near, *out_first).astype(bf16)
     result = scatter_near(result[:last], *result_first)
     layer_output = (middle + result + con_bias).astype(bf16)[None]
-    grad_normed_in, exp_grad = lax.optimization_barrier((grad_normed_in, exp_grad))
     qkv_sum = scatter_dp(qkv_term)
     grad_normed_in, qkv_sum = lax.optimization_barrier((grad_normed_in, qkv_sum))
     grad_in_norm, att_gain_term, att_shift_term = norm_backward(

time: 599 us -> 599 us (level)
    unnamed x153 -> x149, local copies, waits for them, and re-layouts: 29.1 us -> 29.1 us
  transfers between devices with their start and end apart: 85 -> 85, of which waited for: 33 -> 35; matrix products, arithmetic and copies ran while one was open for 43% -> 43% of each run, Pallas kernels for 8% -> 8%
where the time goes in v5:
time: 599 us; the launch traced here: 593 us
  waiting for transfers between devices  170 us (28%)
  matrix products  137 us (23%)
  starting transfers between devices  88.9 us (15%)
  other arithmetic  73.8 us (12%)
  local copies, waits for them, and re-layouts  57.3 us (10%)
  Pallas kernels  50.6 us (8%)
  between operations  15.9 us (3%)
    ppermute x66, waiting for transfers between devices, hop(): return lax.ppermute(value, 'ctx', [(c, c ^ way) for c in range(ways)])  144 us
    dot_general x17, matrix products, dot(): lax.dot_general(left, right, (contract, ((), ())), preferred_element_type...  137 us
    ppermute x66, starting transfers between devices, hop(): return lax.ppermute(value, 'ctx', [(c, c ^ way) for c in range(ways)])  74 us
    unnamed x149, local copies, waits for them, and re-layouts  29.1 us
    pallas_call x1, Pallas kernels, attend_backward(): pl.pallas_call(functools.partial(attend_backward_kernel, block), grid=(pa...  22 us
    pallas_call x1, Pallas kernels, attend_forward(): pl.pallas_call(functools.partial(attend_forward_kernel, block), grid=(pai...  21.4 us
    ppermute x7, waiting for transfers between devices, halving(): value = keep + lax.ppermute(give, axis, [(d, d ^ bit) for d in range(size)])  17.6 us
  transfers between devices with their start and end apart: 85, of which 35 were waited for; matrix products, arithmetic and copies ran while one was open for 43% of the time, Pallas kernels for 8%

profile of v5, /device:TPU:0, one launch (start us, length us, event | category | flops | bytes accessed | tf_op | source)
XLA Modules:
  0.0 593.3 jit_solution(2442786836060418757)
XLA Ops:
  12.2 3.1 collective-permute-start.3
  15.2 2.6 collective-permute-start.4
  21.2 2.4 collective-permute-start.2
  25.7 2.5 collective-permute-done.2
  29.8 2.5 collective-permute-done.1
  34.1 5.0 collective-permute-done.4
  57.7 8.9 %collective-permute-done.7 = bf16[128,2048]{1,0:T(8,128)(2,1)S(1)} collective-permute-done((bf16[128,2048]{1,0:T(8,128)(2,1)S(1)}, bf16[128,2048]{1,0:T(8,128)(2,1)S(1)}, u32[]{:S(2)}, u32[]{:S(2)}) %collective-permute-start.7) | collective-permute-done | bytes 524320 | tf_op jit(solution)/shard_map/ppermute | solution.py:322
  72.6 19.4 %collective-permute-done.10 = bf16[128,2048]{1,0:T(8,128)(2,1)S(1)} collective-permute-done((bf16[128,2048]{1,0:T(8,128)(2,1)S(1)}, bf16[128,2048]{1,0:T(8,128)(2,1)S(1)}, u32[]{:S(2)}, u32[]{:S(2)}) %collective-permute-start.10) | collective-permute-done | bytes 524320 | tf_op jit(solution)/shard_map/ppermute | solution.py:322
  104.0 2.8 convert_reduce_fusion
  106.9 3.4 fusion.2
  111.3 11.8 %add_convert_fusion.q_ref.k_in.v_in = bf16[1024,1536]{1,0:T(8,128)(2,1)} fusion(bf16[2048,1536]{1,0:T(8,128)(2,1)} %all-gather.4.cloned.1.call-done, f32[1536]{0:T(1024)S(1)} %pad_maximum_fusion.26, bf16[1024,2048]{1,0:T(8,128)(2,1)} %constant_dynamic-update-slice_fusion, f32[2048]{0:T(1024)S(1)} %add.322, f32[2048]{0:T(1024)S(1)} %mul.194, ...), kind=kOutput, calls=%fused_computation.23 | convolution fusion | flops 6458179584 | bytes 13662208 | tf_op jit(solution)/shard_map/dot_general | solution.py:38
  124.6 6.7 %collective-permute-done.17 = bf16[128,2048]{1,0:T(8,128)(2,1)S(1)} collective-permute-done((bf16[128,2048]{1,0:T(8,128)(2,1)S(1)}, bf16[128,2048]{1,0:T(8,128)(2,1)S(1)}, u32[]{:S(2)}, u32[]{:S(2)}) %collective-permute-start.17) | collective-permute-done | bytes 524320 | tf_op jit(solution)/shard_map/ppermute | solution.py:322
  135.8 21.4 %attend_forward.1 = (bf16[1024,512]{1,0:T(8,128)(2,1)S(1)}, bf16[8,1024,1024]{2,1,0:T(8,128)(2,1)}) custom-call(s32[1]{0:T(128)} %bitcast.8.me_ref.spot_ref, f32[8]{0:T(128)S(1)} %multiply_exponential_fusion.slope_ref, s32[1024,1]{1,0:T(8,128)S(1)} %bitcast.130, bf16[1024,1536]{1,0:T(8,128)(2,1)} %add_convert_fusion.q_ref.k_in.v_in, ...), custom_call_target="tpu_custom_call" | custom-call | flops 4294967296 | bytes 16777216 | tf_op jit(solution)/shard_map/attend_forward/pallas_call | solution.py:124
  157.3 2.5 collective-permute-done.24
  164.6 2.3 pad_maximum_fusion
  171.8 4.6 collective-permute-done.26.refs_1_
  176.4 6.4 %collective-permute-done.27.refs_2_ = bf16[256,512]{1,0:T(8,128)(2,1)S(1)} collective-permute-done((bf16[256,512]{1,0:T(8,128)(2,1)S(1)}, bf16[256,512]{1,0:T(8,128)(2,1)S(1)}, u32[]{:S(2)}, u32[]{:S(2)}) %collective-permute-start.27) | collective-permute-done | bytes 262176 | tf_op jit(solution)/shard_map/ppermute | solution.py:322
  184.4 3.4 fusion.94
  187.8 4.1 fusion.91
  197.1 10.7 %collective-permute-done.30 = bf16[128,2048]{1,0:T(8,128)(2,1)S(1)} collective-permute-done((bf16[128,2048]{1,0:T(8,128)(2,1)S(1)}, bf16[128,2048]{1,0:T(8,128)(2,1)S(1)}, u32[]{:S(2)}, u32[]{:S(2)}) %collective-permute-start.30) | collective-permute-done | bytes 524320 | tf_op jit(solution)/shard_map/ppermute | solution.py:322
  209.9 9.1 %collective-permute-done.31 = bf16[128,2048]{1,0:T(8,128)(2,1)S(1)} collective-permute-done((bf16[128,2048]{1,0:T(8,128)(2,1)S(1)}, bf16[128,2048]{1,0:T(8,128)(2,1)S(1)}, u32[]{:S(2)}, u32[]{:S(2)}) %collective-permute-start.31) | collective-permute-done | bytes 524320 | tf_op jit(solution)/shard_map/ppermute | solution.py:322
  220.4 9.6 %collective-permute-done.34 = bf16[128,2048]{1,0:T(8,128)(2,1)S(1)} collective-permute-done((bf16[128,2048]{1,0:T(8,128)(2,1)S(1)}, bf16[128,2048]{1,0:T(8,128)(2,1)S(1)}, u32[]{:S(2)}, u32[]{:S(2)}) %collective-permute-start.34) | collective-permute-done | bytes 524320 | tf_op jit(solution)/shard_map/ppermute | solution.py:322
  233.9 1.9 constant_dynamic-update-slice_fusion.59
  235.7 15.2 %multiply_convert_fusion = (bf16[1024,2048]{1,0:T(8,128)(2,1)S(1)}, f32[1024,2048]{1,0:T(8,128)}) fusion(f32[2048]{0:T(1024)S(1)} %bitcast.150, bf16[1024,2048]{1,0:T(8,128)(2,1)} %copy-done.41, bf16[2048,2048]{1,0:T(8,128)(2,1)} %all-gather.6.cloned.1.call-done), kind=kOutput, calls=%fused_computation.17 | convolution fusion | flops 8602517504 | bytes 25174016 | tf_op jit(solution)/shard_map/dot_general | solution.py:38
  250.9 2.3 constant_dynamic-update-slice_fusion.58
  253.2 1.9 constant_dynamic-update-slice_fusion.57
  255.1 1.9 constant_dynamic-update-slice_fusion.56
  257.0 1.9 constant_dynamic-update-slice_fusion.55
  258.8 1.9 constant_dynamic-update-slice_fusion.54
  260.8 13.4 %convolution_convert_fusion.2 = bf16[2048,2048]{1,0:T(8,128)(2,1)} fusion(bf16[1024,2048]{1,0:T(8,128)(2,1)S(1)} %get-tuple-element.166, bf16[1024,2048]{1,0:T(8,128)(2,1)} %constant_dynamic-update-slice_fusion.54), kind=kOutput, calls=%fused_computation.21 | convolution fusion | flops 8594128896 | bytes 16777216 | tf_op jit(solution)/shard_map/dot_general | solution.py:38
  274.2 2.3 all-gather.8.cloned.1.call-done
  276.5 16.7 %convert_reduce_fusion.1 = (f32[2048]{0:T(1024)S(1)}, bf16[1024,2048]{1,0:T(8,128)(2,1)S(1)}) fusion(f32[1024,2048]{1,0:T(8,128)} %get-tuple-element.354, f32[2048]{0:T(1024)S(1)} %bitcast.151, bf16[1024,2048]{1,0:T(8,128)(2,1)} %constant_dynamic-update-slice_fusion.54, bf16[2048,2048]{1,0:T(8,128)(2,1)} %all-gather.8.cloned.1.call-done), kind=kOutput, calls=%fused_computation.15 | convolution fusion | flops 8617195520 | bytes 25182208 | tf_op jit(solution)/shard_map/dot_general | solution.py:38
  293.2 7.5 %convolution_convert_fusion.5 = bf16[256,2048]{1,0:T(8,128)(2,1)S(1)} fusion(bf16[2048,2048]{1,0:T(8,128)(2,1)} %all-gather.6.cloned.1.call-done, bf16[1024,2048]{1,0:T(8,128)(2,1)S(1)} %get-tuple-element.360), kind=kOutput, calls=%fused_computation.36 | convolution fusion | flops 2148007936 | bytes 10485760 | tf_op jit(solution)/shard_map/dot_general | solution.py:38
  303.9 10.2 %fusion.92 = (bf16[768,2048]{1,0:T(8,128)(2,1)S(1)}, f32[768,2048]{1,0:T(8,128)S(1)}) fusion(bf16[2048,2048]{1,0:T(8,128)(2,1)} %all-gather.6.cloned.1.call-done, bf16[1024,2048]{1,0:T(8,128)(2,1)} %copy-done.52), kind=kOutput, calls=%fused_computation.321 | convolution fusion | flops 6444023808 | bytes 20971520 | tf_op jit(solution)/shard_map/dot_general | solution.py:38
  317.7 10.6 %collective-permute-done.38 = bf16[128,2048]{1,0:T(8,128)(2,1)S(1)} collective-permute-done((bf16[128,2048]{1,0:T(8,128)(2,1)S(1)}, bf16[128,2048]{1,0:T(8,128)(2,1)S(1)}, u32[]{:S(2)}, u32[]{:S(2)}) %collective-permute-start.38) | collective-permute-done | bytes 524320 | tf_op jit(solution)/shard_map/ppermute | solution.py:322
  328.4 2.2 collective-permute-done.40
  333.6 11.6 %convolution_convert_fusion.1 = bf16[2048,2048]{1,0:T(8,128)(2,1)} fusion(bf16[1024,2048]{1,0:T(8,128)(2,1)S(1)} %copy-done.42, bf16[1024,2048]{1,0:T(8,128)(2,1)S(1)} %copy-done.53), kind=kOutput, calls=%fused_computation.20 | convolution fusion | flops 8594128896 | bytes 16777216 | tf_op jit(solution)/shard_map/dot_general | solution.py:38
  346.9 2.7 pad_maximum_fusion.1
  349.7 2.7 multiply_reduce_fusion
  352.4 2.3 fusion.76
  354.7 3.8 fusion.95.own_ref
  358.5 3.6 fusion.96.other_ref
  366.7 1.9 collective-permute-start.46
  368.6 11.3 %fusion.97 = f32[1024,2048]{1,0:T(8,128)} fusion(bf16[1024,2048]{1,0:T(8,128)(2,1)S(1)} %copy-done.55, bf16[2048,2048]{1,0:T(8,128)(2,1)S(1)} %bitcast.166), kind=kOutput, calls=%fused_computation.326 | convolution fusion | flops 8589934592 | bytes 20971520 | tf_op jit(solution)/shard_map/dot_general | solution.py:38
  382.9 2.6 copy-done
  391.0 22.0 %attend_backward.1 = (bf16[1024,512]{1,0:T(8,128)(2,1)S(1)}, bf16[1024,512]{1,0:T(8,128)(2,1)S(1)}, bf16[1024,512]{1,0:T(8,128)(2,1)S(1)}) custom-call(s32[1]{0:T(128)} %bitcast.8.me_ref.spot_ref, bf16[8,1024,1024]{2,1,0:T(8,128)(2,1)} %get-tuple-element.168.probs_ref, bf16[1024,1536]{1,0:T(8,128)(2,1)} %add_convert_fusion.q_ref.k_in.v_in, ...), custom_call_target="tpu_custom_call" | custom-call | flops 8589934592 | bytes 16777216 | tf_op jit(solution)/shard_map/attend_backward/pallas_call | solution.py:157
  414.9 12.9 %convolution_convert_fusion = bf16[2048,1536]{1,0:T(8,128)(2,1)} fusion(bf16[1024,1536]{1,0:T(8,128)(2,1)S(1)} %constant_dynamic-update-slice_fusion.62, bf16[1024,2048]{1,0:T(8,128)(2,1)} %constant_dynamic-update-slice_fusion, f32[2048]{0:T(1024)S(1)} %copy-done.49, f32[2048]{0:T(1024)S(1)} %copy-done.44, f32[1024]{0:T(1024)S(1)} %copy-done.51, ...), kind=kOutput, calls=%fused_computation.19 | convolution fusion | flops 6458179584 | bytes 13656064 | tf_op jit(solution)/shard_map/dot_general | solution.py:38
  434.4 4.2 convert.24
  443.6 4.3 fusion.78
  449.8 6.9 %fusion.93 = (bf16[768,2048]{1,0:T(8,128)(2,1)S(1)}, f32[768,2048]{1,0:T(8,128)}) fusion(bf16[2048,1536]{1,0:T(8,128)(2,1)S(1)} %bitcast.168, bf16[1024,1536]{1,0:T(8,128)(2,1)S(1)} %copy-done.10), kind=kOutput, calls=%fused_computation.322 | convolution fusion | flops 4833411072 | bytes 18087936 | tf_op jit(solution)/shard_map/dot_general | solution.py:38
  462.0 3.7 collective-permute-done.58
  467.9 2.8 convert_element_type.322
  470.7 6.3 %collective-permute-done.54 = bf16[128,2048]{1,0:T(8,128)(2,1)} collective-permute-done((bf16[128,2048]{1,0:T(8,128)(2,1)}, bf16[128,2048]{1,0:T(8,128)(2,1)}, u32[]{:S(2)}, u32[]{:S(2)}) %collective-permute-start.54) | collective-permute-done | bytes 524320 | tf_op jit(solution)/shard_map/ppermute | solution.py:322
  478.2 7.5 %collective-permute-done.52 = bf16[128,2048]{1,0:T(8,128)(2,1)} collective-permute-done((bf16[128,2048]{1,0:T(8,128)(2,1)}, bf16[128,2048]{1,0:T(8,128)(2,1)}, u32[]{:S(2)}, u32[]{:S(2)}) %collective-permute-start.52) | collective-permute-done | bytes 524320 | tf_op jit(solution)/shard_map/ppermute | solution.py:322
  504.5 5.5 collective-permute-done.72
  509.9 3.3 collective-permute-done.73
  515.9 8.5 %collective-permute-done.62 = bf16[128,2048]{1,0:T(8,128)(2,1)S(1)} collective-permute-done((bf16[128,2048]{1,0:T(8,128)(2,1)S(1)}, bf16[128,2048]{1,0:T(8,128)(2,1)S(1)}, u32[]{:S(2)}, u32[]{:S(2)}) %collective-permute-start.62) | collective-permute-done | bytes 524320 | tf_op jit(solution)/shard_map/ppermute | solution.py:322
  526.8 6.7 %collective-permute-done.60 = bf16[128,2048]{1,0:T(8,128)(2,1)S(1)} collective-permute-done((bf16[128,2048]{1,0:T(8,128)(2,1)S(1)}, bf16[128,2048]{1,0:T(8,128)(2,1)S(1)}, u32[]{:S(2)}, u32[]{:S(2)}) %collective-permute-start.60) | collective-permute-done | bytes 524320 | tf_op jit(solution)/shard_map/ppermute | solution.py:322
  533.5 1.9 convert_add_fusion.3
  536.5 11.7 %collective-permute-done.74 = bf16[2,64,2048]{2,1,0:T(8,128)(2,1)S(1)} collective-permute-done((bf16[2,64,2048]{2,1,0:T(8,128)(2,1)S(1)}, bf16[2,64,2048]{2,1,0:T(8,128)(2,1)S(1)}, u32[]{:S(2)}, u32[]{:S(2)}) %collective-permute-start.74) | collective-permute-done | bytes 524320 | tf_op jit(solution)/shard_map/ppermute | solution.py:414
  555.6 3.3 fusion.28
  562.8 1.9 bitcast_convert_fusion
  566.2 2.1 collective-permute-start.65
  576.7 3.0 collective-permute-done.67
  (447 shorter events, 181.2 us)
Async XLA Ops:
  7.2 104.1 %all-gather.4.cloned.1.call-start = ((), (), s32[]{:S(2)}) async-start(), calls=%async_computation.3 | async-start | bytes 7077888 | tf_op jit(solution)/shard_map/all_gather | solution.py:469
  12.2 22.0 %collective-permute-start.3 = (bf16[80,2048]{1,0:T(8,128)(2,1)S(1)}, bf16[80,2048]{1,0:T(8,128)(2,1)S(1)}, u32[]{:S(2)}, u32[]{:S(2)}) collective-permute-start(bf16[80,2048]{1,0:T(8,128)(2,1)S(1)} %pad_maximum_fusion.11), channel_id=1, source_target_pairs={{0,8},{4,12},{8,16},{12,20},{16,24},{20,28},{24,0},{28,4},{1,9},{5... | collective-permute-start | bytes 983048 | tf_op jit(solution)/shard_map/ppermute | solution.py:525
  15.2 23.9 %collective-permute-start.4 = (bf16[80,2048]{1,0:T(8,128)(2,1)S(1)}, bf16[80,2048]{1,0:T(8,128)(2,1)S(1)}, u32[]{:S(2)}, u32[]{:S(2)}) collective-permute-start(bf16[80,2048]{1,0:T(8,128)(2,1)S(1)} %pad_maximum_fusion.11), channel_id=1, source_target_pairs={{0,16},{4,20},{8,24},{12,28},{16,0},{20,4},{24,8},{28,12},{1,17},{... | collective-permute-start | bytes 983048 | tf_op jit(solution)/shard_map/ppermute | solution.py:525
  17.8 21.3 %collective-permute-start.5 = (bf16[80,2048]{1,0:T(8,128)(2,1)S(1)}, bf16[80,2048]{1,0:T(8,128)(2,1)S(1)}, u32[]{:S(2)}, u32[]{:S(2)}) collective-permute-start(bf16[80,2048]{1,0:T(8,128)(2,1)S(1)} %pad_maximum_fusion.11), channel_id=1, source_target_pairs={{0,24},{4,28},{8,0},{12,4},{16,8},{20,12},{24,16},{28,20},{1,25},{... | collective-permute-start | bytes 983048 | tf_op jit(solution)/shard_map/ppermute | solution.py:525
  40.2 195.5 %all-gather.6.cloned.1.call-start = ((), (), s32[]{:S(2)}) async-start(), calls=%async_computation.4 | async-start | bytes 9437184 | tf_op jit(solution)/shard_map/all_gather | solution.py:469
  40.5 14.9 %collective-permute-start.6 = (bf16[128,2048]{1,0:T(8,128)(2,1)S(1)}, bf16[128,2048]{1,0:T(8,128)(2,1)S(1)}, u32[]{:S(2)}, u32[]{:S(2)}) collective-permute-start(bf16[128,2048]{1,0:T(8,128)(2,1)S(1)} %get-tuple-element.308), channel_id=1, source_target_pairs={{0,1},{1,0},{2,3},{3,2},{4,5},{5,4},{6,7},{7,6},{8,9},{9,8},{10,11... | collective-permute-start | bytes 1572872 | tf_op jit(solution)/shard_map/ppermute | solution.py:322
  42.0 26.9 %collective-permute-start.8 = (bf16[128,2048]{1,0:T(8,128)(2,1)S(1)}, bf16[128,2048]{1,0:T(8,128)(2,1)S(1)}, u32[]{:S(2)}, u32[]{:S(2)}) collective-permute-start(bf16[128,2048]{1,0:T(8,128)(2,1)S(1)} %get-tuple-element.308), channel_id=1, source_target_pairs={{0,2},{1,3},{2,0},{3,1},{4,6},{5,7},{6,4},{7,5},{8,10},{9,11},{10,... | collective-permute-start | bytes 1572872 | tf_op jit(solution)/shard_map/ppermute | solution.py:322
  43.5 23.0 %collective-permute-start.7 = (bf16[128,2048]{1,0:T(8,128)(2,1)S(1)}, bf16[128,2048]{1,0:T(8,128)(2,1)S(1)}, u32[]{:S(2)}, u32[]{:S(2)}) collective-permute-start(bf16[128,2048]{1,0:T(8,128)(2,1)S(1)} %get-tuple-element.307), channel_id=1, source_target_pairs={{0,1},{1,0},{2,3},{3,2},{4,5},{5,4},{6,7},{7,6},{8,9},{9,8},{10,11... | collective-permute-start | bytes 1572872 | tf_op jit(solution)/shard_map/ppermute | solution.py:322
  44.1 26.3 %collective-permute-start.9 = (bf16[128,2048]{1,0:T(8,128)(2,1)S(1)}, bf16[128,2048]{1,0:T(8,128)(2,1)S(1)}, u32[]{:S(2)}, u32[]{:S(2)}) collective-permute-start(bf16[128,2048]{1,0:T(8,128)(2,1)S(1)} %get-tuple-element.307), channel_id=1, source_target_pairs={{0,2},{1,3},{2,0},{3,1},{4,6},{5,7},{6,4},{7,5},{8,10},{9,11},{10,... | collective-permute-start | bytes 1572872 | tf_op jit(solution)/shard_map/ppermute | solution.py:322
  53.1 40.6 %collective-permute-start.13 = (bf16[80,2048]{1,0:T(8,128)(2,1)S(1)}, bf16[80,2048]{1,0:T(8,128)(2,1)S(1)}, u32[]{:S(2)}, u32[]{:S(2)}) collective-permute-start(bf16[80,2048]{1,0:T(8,128)(2,1)S(1)} %get-tuple-element.336), channel_id=1, source_target_pairs={{0,1},{1,0},{2,3},{3,2},{4,5},{5,4},{6,7},{7,6},{8,9},{9,8},{10,11... | collective-permute-start | bytes 983048 | tf_op jit(solution)/shard_map/ppermute | solution.py:322
  55.3 38.4 %collective-permute-start.14 = (bf16[80,2048]{1,0:T(8,128)(2,1)S(1)}, bf16[80,2048]{1,0:T(8,128)(2,1)S(1)}, u32[]{:S(2)}, u32[]{:S(2)}) collective-permute-start(bf16[80,2048]{1,0:T(8,128)(2,1)S(1)} %get-tuple-element.337), channel_id=1, source_target_pairs={{0,2},{1,3},{2,0},{3,1},{4,6},{5,7},{6,4},{7,5},{8,10},{9,11},{10,... | collective-permute-start | bytes 983048 | tf_op jit(solution)/shard_map/ppermute | solution.py:322
  66.6 25.4 %collective-permute-start.10 = (bf16[128,2048]{1,0:T(8,128)(2,1)S(1)}, bf16[128,2048]{1,0:T(8,128)(2,1)S(1)}, u32[]{:S(2)}, u32[]{:S(2)}) collective-permute-start(bf16[128,2048]{1,0:T(8,128)(2,1)S(1)} %collective-permute-done.6), channel_id=1, source_target_pairs={{0,2},{1,3},{2,0},{3,1},{4,6},{5,7},{6,4},{7,5},{8,10},{9,11},{10,... | collective-permute-start | bytes 1572872 | tf_op jit(solution)/shard_map/ppermute | solution.py:322
  68.9 24.8 %collective-permute-start.15 = (bf16[80,2048]{1,0:T(8,128)(2,1)S(1)}, bf16[80,2048]{1,0:T(8,128)(2,1)S(1)}, u32[]{:S(2)}, u32[]{:S(2)}) collective-permute-start(bf16[80,2048]{1,0:T(8,128)(2,1)S(1)} %get-tuple-element.335), channel_id=1, source_target_pairs={{0,3},{1,2},{2,1},{3,0},{4,7},{5,6},{6,5},{7,4},{8,11},{9,10},{10,... | collective-permute-start | bytes 983048 | tf_op jit(solution)/shard_map/ppermute | solution.py:322
  70.4 22.5 %collective-permute-start.11 = (bf16[128,2048]{1,0:T(8,128)(2,1)S(1)}, bf16[128,2048]{1,0:T(8,128)(2,1)S(1)}, u32[]{:S(2)}, u32[]{:S(2)}) collective-permute-start(bf16[128,2048]{1,0:T(8,128)(2,1)S(1)} %collective-permute-done.9), channel_id=1, source_target_pairs={{0,1},{1,0},{2,3},{3,2},{4,5},{5,4},{6,7},{7,6},{8,9},{9,8},{10,11... | collective-permute-start | bytes 1572872 | tf_op jit(solution)/shard_map/ppermute | solution.py:322
  95.7 180.7 %all-gather.8.cloned.1.call-start = ((), (), s32[]{:S(2)}) async-start(), calls=%async_computation.5 | async-start | bytes 9437184 | tf_op jit(solution)/shard_map/all_gather | solution.py:469
  96.1 37.9 %collective-permute-start.20 = (bf16[128,2048]{1,0:T(8,128)(2,1)S(1)}, bf16[128,2048]{1,0:T(8,128)(2,1)}, u32[]{:S(2)}, u32[]{:S(2)}) collective-permute-start(bf16[128,2048]{1,0:T(8,128)(2,1)S(1)} %get-tuple-element.149), channel_id=1, source_target_pairs={{0,1},{1,0},{2,3},{3,2},{4,5},{5,4},{6,7},{7,6},{8,9},{9,8},{10,11... | collective-permute-start | bytes 1572872 | tf_op jit(solution)/shard_map/ppermute | solution.py:322
  97.6 25.5 %collective-permute-start.16 = (bf16[128,2048]{1,0:T(8,128)(2,1)}, bf16[128,2048]{1,0:T(8,128)(2,1)}, u32[]{:S(2)}, u32[]{:S(2)}) collective-permute-start(bf16[128,2048]{1,0:T(8,128)(2,1)} %get-tuple-element.133), channel_id=1, source_target_pairs={{0,1},{1,0},{2,3},{3,2},{4,5},{5,4},{6,7},{7,6},{8,9},{9,8},{10,11... | collective-permute-start | bytes 1572872 | tf_op jit(solution)/shard_map/ppermute | solution.py:322
  99.1 32.8 %collective-permute-start.18 = (bf16[128,2048]{1,0:T(8,128)(2,1)}, bf16[128,2048]{1,0:T(8,128)(2,1)S(1)}, u32[]{:S(2)}, u32[]{:S(2)}) collective-permute-start(bf16[128,2048]{1,0:T(8,128)(2,1)} %get-tuple-element.133), channel_id=1, source_target_pairs={{0,2},{1,3},{2,0},{3,1},{4,6},{5,7},{6,4},{7,5},{8,10},{9,11},{10,... | collective-permute-start | bytes 1572872 | tf_op jit(solution)/shard_map/ppermute | solution.py:322
  100.6 30.7 %collective-permute-start.17 = (bf16[128,2048]{1,0:T(8,128)(2,1)S(1)}, bf16[128,2048]{1,0:T(8,128)(2,1)S(1)}, u32[]{:S(2)}, u32[]{:S(2)}) collective-permute-start(bf16[128,2048]{1,0:T(8,128)(2,1)S(1)} %get-tuple-element.134), channel_id=1, source_target_pairs={{0,1},{1,0},{2,3},{3,2},{4,5},{5,4},{6,7},{7,6},{8,9},{9,8},{10,11... | collective-permute-start | bytes 1572872 | tf_op jit(solution)/shard_map/ppermute | solution.py:322
  101.1 32.3 %collective-permute-start.19 = (bf16[128,2048]{1,0:T(8,128)(2,1)S(1)}, bf16[128,2048]{1,0:T(8,128)(2,1)}, u32[]{:S(2)}, u32[]{:S(2)}) collective-permute-start(bf16[128,2048]{1,0:T(8,128)(2,1)S(1)} %get-tuple-element.134), channel_id=1, source_target_pairs={{0,2},{1,3},{2,0},{3,1},{4,6},{5,7},{6,4},{7,5},{8,10},{9,11},{10,... | collective-permute-start | bytes 1572872 | tf_op jit(solution)/shard_map/ppermute | solution.py:322
  123.1 34.1 %collective-permute-start.22 = (bf16[128,2048]{1,0:T(8,128)(2,1)S(1)}, bf16[128,2048]{1,0:T(8,128)(2,1)}, u32[]{:S(2)}, u32[]{:S(2)}) collective-permute-start(bf16[128,2048]{1,0:T(8,128)(2,1)S(1)} %get-tuple-element.149), channel_id=1, source_target_pairs={{0,2},{1,3},{2,0},{3,1},{4,6},{5,7},{6,4},{7,5},{8,10},{9,11},{10,... | collective-permute-start | bytes 1572872 | tf_op jit(solution)/shard_map/ppermute | solution.py:322
  131.3 25.9 %collective-permute-start.21 = (bf16[128,2048]{1,0:T(8,128)(2,1)S(1)}, bf16[128,2048]{1,0:T(8,128)(2,1)}, u32[]{:S(2)}, u32[]{:S(2)}) collective-permute-start(bf16[128,2048]{1,0:T(8,128)(2,1)S(1)} %get-tuple-element.150), channel_id=1, source_target_pairs={{0,1},{1,0},{2,3},{3,2},{4,5},{5,4},{6,7},{7,6},{8,9},{9,8},{10,11... | collective-permute-start | bytes 1572872 | tf_op jit(solution)/shard_map/ppermute | solution.py:322
  131.8 25.4 %collective-permute-start.23 = (bf16[128,2048]{1,0:T(8,128)(2,1)S(1)}, bf16[128,2048]{1,0:T(8,128)(2,1)}, u32[]{:S(2)}, u32[]{:S(2)}) collective-permute-start(bf16[128,2048]{1,0:T(8,128)(2,1)S(1)} %get-tuple-element.150), channel_id=1, source_target_pairs={{0,2},{1,3},{2,0},{3,1},{4,6},{5,7},{6,4},{7,5},{8,10},{9,11},{10,... | collective-permute-start | bytes 1572872 | tf_op jit(solution)/shard_map/ppermute | solution.py:322
  133.4 26.4 %collective-permute-start.24 = (bf16[128,2048]{1,0:T(8,128)(2,1)}, bf16[128,2048]{1,0:T(8,128)(2,1)}, u32[]{:S(2)}, u32[]{:S(2)}) collective-permute-start(bf16[128,2048]{1,0:T(8,128)(2,1)} %collective-permute-done.16), channel_id=1, source_target_pairs={{0,2},{1,3},{2,0},{3,1},{4,6},{5,7},{6,4},{7,5},{8,10},{9,11},{10,... | collective-permute-start | bytes 1572872 | tf_op jit(solution)/shard_map/ppermute | solution.py:322
  133.9 25.9 %collective-permute-start.25 = (bf16[128,2048]{1,0:T(8,128)(2,1)}, bf16[128,2048]{1,0:T(8,128)(2,1)}, u32[]{:S(2)}, u32[]{:S(2)}) collective-permute-start(bf16[128,2048]{1,0:T(8,128)(2,1)} %collective-permute-done.19), channel_id=1, source_target_pairs={{0,1},{1,0},{2,3},{3,2},{4,5},{5,4},{6,7},{7,6},{8,9},{9,8},{10,11... | collective-permute-start | bytes 1572872 | tf_op jit(solution)/shard_map/ppermute | solution.py:322
  166.9 17.5 %collective-permute-start.29 = (bf16[1024,2048]{1,0:T(8,128)(2,1)}, bf16[1024,2048]{1,0:T(8,128)(2,1)}, u32[]{:S(2)}, u32[]{:S(2)}) collective-permute-start(bf16[1024,2048]{1,0:T(8,128)(2,1)} %bitcast.30), channel_id=1, source_target_pairs={{0,4},{4,0},{8,12},{12,8},{16,20},{20,16},{24,28},{28,24},{1,5},{5... | collective-permute-start | bytes 12582920 | tf_op jit(solution)/shard_map/ppermute | solution.py:424
  166.9 260.9 %reduce-scatter.4.cloned.1.call-start = ((), (), s32[]{:S(2)}) async-start(), calls=%async_computation.6 | async-start | bytes 9437184 | tf_op jit(solution)/shard_map/reduce_scatter | solution.py:483
  192.9 14.9 %collective-permute-start.30 = (bf16[128,2048]{1,0:T(8,128)(2,1)S(1)}, bf16[128,2048]{1,0:T(8,128)(2,1)S(1)}, u32[]{:S(2)}, u32[]{:S(2)}) collective-permute-start(bf16[128,2048]{1,0:T(8,128)(2,1)S(1)} %get-tuple-element.262), channel_id=1, source_target_pairs={{0,1},{1,0},{2,3},{3,2},{4,5},{5,4},{6,7},{7,6},{8,9},{9,8},{10,11... | collective-permute-start | bytes 1572872 | tf_op jit(solution)/shard_map/ppermute | solution.py:322
  194.2 15.1 %collective-permute-start.33 = (bf16[128,2048]{1,0:T(8,128)(2,1)S(1)}, bf16[128,2048]{1,0:T(8,128)(2,1)S(1)}, u32[]{:S(2)}, u32[]{:S(2)}) collective-permute-start(bf16[128,2048]{1,0:T(8,128)(2,1)S(1)} %get-tuple-element.261), channel_id=1, source_target_pairs={{0,2},{1,3},{2,0},{3,1},{4,6},{5,7},{6,4},{7,5},{8,10},{9,11},{10,... | collective-permute-start | bytes 1572872 | tf_op jit(solution)/shard_map/ppermute | solution.py:322
  195.0 24.1 %collective-permute-start.31 = (bf16[128,2048]{1,0:T(8,128)(2,1)S(1)}, bf16[128,2048]{1,0:T(8,128)(2,1)S(1)}, u32[]{:S(2)}, u32[]{:S(2)}) collective-permute-start(bf16[128,2048]{1,0:T(8,128)(2,1)S(1)} %get-tuple-element.261), channel_id=1, source_target_pairs={{0,1},{1,0},{2,3},{3,2},{4,5},{5,4},{6,7},{7,6},{8,9},{9,8},{10,11... | collective-permute-start | bytes 1572872 | tf_op jit(solution)/shard_map/ppermute | solution.py:322
  196.5 23.8 %collective-permute-start.32 = (bf16[128,2048]{1,0:T(8,128)(2,1)S(1)}, bf16[128,2048]{1,0:T(8,128)(2,1)S(1)}, u32[]{:S(2)}, u32[]{:S(2)}) collective-permute-start(bf16[128,2048]{1,0:T(8,128)(2,1)S(1)} %get-tuple-element.262), channel_id=1, source_target_pairs={{0,2},{1,3},{2,0},{3,1},{4,6},{5,7},{6,4},{7,5},{8,10},{9,11},{10,... | collective-permute-start | bytes 1572872 | tf_op jit(solution)/shard_map/ppermute | solution.py:322
  207.8 22.2 %collective-permute-start.34 = (bf16[128,2048]{1,0:T(8,128)(2,1)S(1)}, bf16[128,2048]{1,0:T(8,128)(2,1)S(1)}, u32[]{:S(2)}, u32[]{:S(2)}) collective-permute-start(bf16[128,2048]{1,0:T(8,128)(2,1)S(1)} %collective-permute-done.30), channel_id=1, source_target_pairs={{0,2},{1,3},{2,0},{3,1},{4,6},{5,7},{6,4},{7,5},{8,10},{9,11},{10,... | collective-permute-start | bytes 1572872 | tf_op jit(solution)/shard_map/ppermute | solution.py:322
  209.3 20.7 %collective-permute-start.35 = (bf16[128,2048]{1,0:T(8,128)(2,1)S(1)}, bf16[128,2048]{1,0:T(8,128)(2,1)S(1)}, u32[]{:S(2)}, u32[]{:S(2)}) collective-permute-start(bf16[128,2048]{1,0:T(8,128)(2,1)S(1)} %collective-permute-done.33), channel_id=1, source_target_pairs={{0,1},{1,0},{2,3},{3,2},{4,5},{5,4},{6,7},{7,6},{8,9},{9,8},{10,11... | collective-permute-start | bytes 1572872 | tf_op jit(solution)/shard_map/ppermute | solution.py:322
  230.1 26.8 %collective-permute-start.36 = (bf16[128,2048]{1,0:T(8,128)(2,1)}, bf16[128,2048]{1,0:T(8,128)(2,1)}, u32[]{:S(2)}, u32[]{:S(2)}) collective-permute-start(bf16[128,2048]{1,0:T(8,128)(2,1)} %collective-permute-done.20), channel_id=1, source_target_pairs={{0,2},{1,3},{2,0},{3,1},{4,6},{5,7},{6,4},{7,5},{8,10},{9,11},{10,... | collective-permute-start | bytes 1572872 | tf_op jit(solution)/shard_map/ppermute | solution.py:322
  230.8 28.1 %collective-permute-start.37 = (bf16[128,2048]{1,0:T(8,128)(2,1)}, bf16[128,2048]{1,0:T(8,128)(2,1)}, u32[]{:S(2)}, u32[]{:S(2)}) collective-permute-start(bf16[128,2048]{1,0:T(8,128)(2,1)} %collective-permute-done.23), channel_id=1, source_target_pairs={{0,1},{1,0},{2,3},{3,2},{4,5},{5,4},{6,7},{7,6},{8,9},{9,8},{10,11... | collective-permute-start | bytes 1572872 | tf_op jit(solution)/shard_map/ppermute | solution.py:322
  276.5 209.6 %reduce-scatter.6.cloned.1.call-start = ((), (), s32[]{:S(2)}) async-start(), calls=%async_computation.7 | async-start | bytes 9437184 | tf_op jit(solution)/shard_map/reduce_scatter | solution.py:483
  300.8 14.7 %collective-permute-start.39 = (bf16[128,2048]{1,0:T(8,128)(2,1)S(1)}, bf16[128,2048]{1,0:T(8,128)(2,1)S(1)}, u32[]{:S(2)}, u32[]{:S(2)}) collective-permute-start(bf16[128,2048]{1,0:T(8,128)(2,1)S(1)} %get-tuple-element.259), channel_id=1, source_target_pairs={{0,1},{1,0},{2,3},{3,2},{4,5},{5,4},{6,7},{7,6},{8,9},{9,8},{10,11... | collective-permute-start | bytes 1572872 | tf_op jit(solution)/shard_map/ppermute | solution.py:322
  302.4 15.3 %collective-permute-start.42 = (bf16[128,2048]{1,0:T(8,128)(2,1)S(1)}, bf16[128,2048]{1,0:T(8,128)(2,1)S(1)}, u32[]{:S(2)}, u32[]{:S(2)}) collective-permute-start(bf16[128,2048]{1,0:T(8,128)(2,1)S(1)} %get-tuple-element.260), channel_id=1, source_target_pairs={{0,2},{1,3},{2,0},{3,1},{4,6},{5,7},{6,4},{7,5},{8,10},{9,11},{10,... | collective-permute-start | bytes 1572872 | tf_op jit(solution)/shard_map/ppermute | solution.py:322
  315.7 14.9 %collective-permute-start.40 = (bf16[128,2048]{1,0:T(8,128)(2,1)S(1)}, bf16[128,2048]{1,0:T(8,128)(2,1)S(1)}, u32[]{:S(2)}, u32[]{:S(2)}) collective-permute-start(bf16[128,2048]{1,0:T(8,128)(2,1)S(1)} %fusion.42), channel_id=1, source_target_pairs={{0,2},{1,3},{2,0},{3,1},{4,6},{5,7},{6,4},{7,5},{8,10},{9,11},{10,... | collective-permute-start | bytes 1572872 | tf_op jit(solution)/shard_map/ppermute | solution.py:322
  316.6 28.6 %collective-permute-start.41 = (bf16[128,2048]{1,0:T(8,128)(2,1)}, bf16[128,2048]{1,0:T(8,128)(2,1)}, u32[]{:S(2)}, u32[]{:S(2)}) collective-permute-start(bf16[128,2048]{1,0:T(8,128)(2,1)} %get-tuple-element.236), channel_id=1, source_target_pairs={{0,2},{1,3},{2,0},{3,1},{4,6},{5,7},{6,4},{7,5},{8,10},{9,11},{10,... | collective-permute-start | bytes 1572872 | tf_op jit(solution)/shard_map/ppermute | solution.py:322
  349.6 206.0 %reduce-scatter.8.cloned.1.call-start = ((), (), s32[]{:S(2)}) async-start(), calls=%async_computation.8 | async-start | bytes 7077888 | tf_op jit(solution)/shard_map/reduce_scatter | solution.py:483
  365.0 16.0 %collective-permute-start.47 = (bf16[1024,2048]{1,0:T(8,128)(2,1)S(1)}, bf16[1024,2048]{1,0:T(8,128)(2,1)S(1)}, u32[]{:S(2)}, u32[]{:S(2)}) collective-permute-start(bf16[1024,2048]{1,0:T(8,128)(2,1)S(1)} %convolution_convert_fusion.3), channel_id=1, source_target_pairs={{0,4},{4,0},{8,12},{12,8},{16,20},{20,16},{24,28},{28,24},{1,5},{5... | collective-permute-start | bytes 12582920 | tf_op jit(solution)/shard_map/ppermute | solution.py:424
  365.1 14.8 %collective-permute-start.44 = (bf16[256,512]{1,0:T(8,128)(2,1)S(1)}, bf16[256,512]{1,0:T(8,128)(2,1)S(1)}, u32[]{:S(2)}, u32[]{:S(2)}) collective-permute-start(bf16[256,512]{1,0:T(8,128)(2,1)S(1)} %get-tuple-element.162), channel_id=1, source_target_pairs={{0,1},{1,0},{2,3},{3,2},{4,5},{5,4},{6,7},{7,6},{8,9},{9,8},{10,11... | collective-permute-start | bytes 786440 | tf_op jit(solution)/shard_map/ppermute | solution.py:322
  365.8 14.1 %collective-permute-start.45 = (bf16[256,512]{1,0:T(8,128)(2,1)S(1)}, bf16[256,512]{1,0:T(8,128)(2,1)S(1)}, u32[]{:S(2)}, u32[]{:S(2)}) collective-permute-start(bf16[256,512]{1,0:T(8,128)(2,1)S(1)} %get-tuple-element.163), channel_id=1, source_target_pairs={{0,2},{1,3},{2,0},{3,1},{4,6},{5,7},{6,4},{7,5},{8,10},{9,11},{10,... | collective-permute-start | bytes 786440 | tf_op jit(solution)/shard_map/ppermute | solution.py:322
  386.9 40.9 %collective-permute-start.48 = (bf16[128,2048]{1,0:T(8,128)(2,1)}, bf16[128,2048]{1,0:T(8,128)(2,1)}, u32[]{:S(2)}, u32[]{:S(2)}) collective-permute-start(bf16[128,2048]{1,0:T(8,128)(2,1)} %bitcast.34), channel_id=1, source_target_pairs={{0,1},{1,0},{2,3},{3,2},{4,5},{5,4},{6,7},{7,6},{8,9},{9,8},{10,11... | collective-permute-start | bytes 1572872 | tf_op jit(solution)/shard_map/ppermute | solution.py:322
  388.2 39.6 %collective-permute-start.49 = (bf16[128,2048]{1,0:T(8,128)(2,1)}, bf16[128,2048]{1,0:T(8,128)(2,1)}, u32[]{:S(2)}, u32[]{:S(2)}) collective-permute-start(bf16[128,2048]{1,0:T(8,128)(2,1)} %bitcast.35), channel_id=1, source_target_pairs={{0,2},{1,3},{2,0},{3,1},{4,6},{5,7},{6,4},{7,5},{8,10},{9,11},{10,... | collective-permute-start | bytes 1572872 | tf_op jit(solution)/shard_map/ppermute | solution.py:322
  389.1 38.7 %collective-permute-start.50 = (bf16[128,2048]{1,0:T(8,128)(2,1)}, bf16[128,2048]{1,0:T(8,128)(2,1)}, u32[]{:S(2)}, u32[]{:S(2)}) collective-permute-start(bf16[128,2048]{1,0:T(8,128)(2,1)} %bitcast.36), channel_id=1, source_target_pairs={{0,1},{1,0},{2,3},{3,2},{4,5},{5,4},{6,7},{7,6},{8,9},{9,8},{10,11... | collective-permute-start | bytes 1572872 | tf_op jit(solution)/shard_map/ppermute | solution.py:322
  389.9 37.9 %collective-permute-start.51 = (bf16[128,2048]{1,0:T(8,128)(2,1)}, bf16[128,2048]{1,0:T(8,128)(2,1)}, u32[]{:S(2)}, u32[]{:S(2)}) collective-permute-start(bf16[128,2048]{1,0:T(8,128)(2,1)} %bitcast.37), channel_id=1, source_target_pairs={{0,2},{1,3},{2,0},{3,1},{4,6},{5,7},{6,4},{7,5},{8,10},{9,11},{10,... | collective-permute-start | bytes 1572872 | tf_op jit(solution)/shard_map/ppermute | solution.py:322
  439.6 20.6 %collective-permute-start.56 = (bf16[128,2048]{1,0:T(8,128)(2,1)S(1)}, bf16[128,2048]{1,0:T(8,128)(2,1)S(1)}, u32[]{:S(2)}, u32[]{:S(2)}) collective-permute-start(bf16[128,2048]{1,0:T(8,128)(2,1)S(1)} %get-tuple-element.228), channel_id=1, source_target_pairs={{0,1},{1,0},{2,3},{3,2},{4,5},{5,4},{6,7},{7,6},{8,9},{9,8},{10,11... | collective-permute-start | bytes 1572872 | tf_op jit(solution)/shard_map/ppermute | solution.py:322
  440.8 20.4 %collective-permute-start.57 = (bf16[128,2048]{1,0:T(8,128)(2,1)S(1)}, bf16[128,2048]{1,0:T(8,128)(2,1)S(1)}, u32[]{:S(2)}, u32[]{:S(2)}) collective-permute-start(bf16[128,2048]{1,0:T(8,128)(2,1)S(1)} %get-tuple-element.227), channel_id=1, source_target_pairs={{0,2},{1,3},{2,0},{3,1},{4,6},{5,7},{6,4},{7,5},{8,10},{9,11},{10,... | collective-permute-start | bytes 1572872 | tf_op jit(solution)/shard_map/ppermute | solution.py:322
  441.7 24.0 %collective-permute-start.58 = (bf16[128,2048]{1,0:T(8,128)(2,1)S(1)}, bf16[128,2048]{1,0:T(8,128)(2,1)S(1)}, u32[]{:S(2)}, u32[]{:S(2)}) collective-permute-start(bf16[128,2048]{1,0:T(8,128)(2,1)S(1)} %get-tuple-element.226), channel_id=1, source_target_pairs={{0,1},{1,0},{2,3},{3,2},{4,5},{5,4},{6,7},{7,6},{8,9},{9,8},{10,11... | collective-permute-start | bytes 1572872 | tf_op jit(solution)/shard_map/ppermute | solution.py:322
  442.4 28.3 %collective-permute-start.59 = (bf16[128,2048]{1,0:T(8,128)(2,1)}, bf16[128,2048]{1,0:T(8,128)(2,1)}, u32[]{:S(2)}, u32[]{:S(2)}) collective-permute-start(bf16[128,2048]{1,0:T(8,128)(2,1)} %get-tuple-element.225), channel_id=1, source_target_pairs={{0,2},{1,3},{2,0},{3,1},{4,6},{5,7},{6,4},{7,5},{8,10},{9,11},{10,... | collective-permute-start | bytes 1572872 | tf_op jit(solution)/shard_map/ppermute | solution.py:322
  457.8 19.2 %collective-permute-start.54 = (bf16[128,2048]{1,0:T(8,128)(2,1)}, bf16[128,2048]{1,0:T(8,128)(2,1)}, u32[]{:S(2)}, u32[]{:S(2)}) collective-permute-start(bf16[128,2048]{1,0:T(8,128)(2,1)} %get-tuple-element.234), channel_id=1, source_target_pairs={{0,1},{1,0},{2,3},{3,2},{4,5},{5,4},{6,7},{7,6},{8,9},{9,8},{10,11... | collective-permute-start | bytes 1572872 | tf_op jit(solution)/shard_map/ppermute | solution.py:322
  460.1 18.1 %collective-permute-start.55 = (bf16[128,2048]{1,0:T(8,128)(2,1)}, bf16[128,2048]{1,0:T(8,128)(2,1)}, u32[]{:S(2)}, u32[]{:S(2)}) collective-permute-start(bf16[128,2048]{1,0:T(8,128)(2,1)} %get-tuple-element.233), channel_id=1, source_target_pairs={{0,2},{1,3},{2,0},{3,1},{4,6},{5,7},{6,4},{7,5},{8,10},{9,11},{10,... | collective-permute-start | bytes 1572872 | tf_op jit(solution)/shard_map/ppermute | solution.py:322
  461.2 24.5 %collective-permute-start.52 = (bf16[128,2048]{1,0:T(8,128)(2,1)}, bf16[128,2048]{1,0:T(8,128)(2,1)}, u32[]{:S(2)}, u32[]{:S(2)}) collective-permute-start(bf16[128,2048]{1,0:T(8,128)(2,1)} %get-tuple-element.258), channel_id=1, source_target_pairs={{0,1},{1,0},{2,3},{3,2},{4,5},{5,4},{6,7},{7,6},{8,9},{9,8},{10,11... | collective-permute-start | bytes 1572872 | tf_op jit(solution)/shard_map/ppermute | solution.py:322
  465.7 20.4 %collective-permute-start.53 = (bf16[128,2048]{1,0:T(8,128)(2,1)}, bf16[128,2048]{1,0:T(8,128)(2,1)}, u32[]{:S(2)}, u32[]{:S(2)}) collective-permute-start(bf16[128,2048]{1,0:T(8,128)(2,1)} %get-tuple-element.257), channel_id=1, source_target_pairs={{0,2},{1,3},{2,0},{3,1},{4,6},{5,7},{6,4},{7,5},{8,10},{9,11},{10,... | collective-permute-start | bytes 1572872 | tf_op jit(solution)/shard_map/ppermute | solution.py:322
  492.6 17.4 %collective-permute-start.72 = (bf16[128,2048]{1,0:T(8,128)(2,1)S(1)}, bf16[128,2048]{1,0:T(8,128)(2,1)S(1)}, u32[]{:S(2)}, u32[]{:S(2)}) collective-permute-start(bf16[128,2048]{1,0:T(8,128)(2,1)S(1)} %fusion.47), channel_id=1, source_target_pairs={{0,1},{1,0},{2,3},{3,2},{4,5},{5,4},{6,7},{7,6},{8,9},{9,8},{10,11... | collective-permute-start | bytes 1572872 | tf_op jit(solution)/shard_map/ppermute | solution.py:322
  495.3 17.9 %collective-permute-start.73 = (bf16[128,2048]{1,0:T(8,128)(2,1)S(1)}, bf16[128,2048]{1,0:T(8,128)(2,1)S(1)}, u32[]{:S(2)}, u32[]{:S(2)}) collective-permute-start(bf16[128,2048]{1,0:T(8,128)(2,1)S(1)} %fusion.44), channel_id=1, source_target_pairs={{0,2},{1,3},{2,0},{3,1},{4,6},{5,7},{6,4},{7,5},{8,10},{9,11},{10,... | collective-permute-start | bytes 1572872 | tf_op jit(solution)/shard_map/ppermute | solution.py:322
  499.1 25.4 %collective-permute-start.62 = (bf16[128,2048]{1,0:T(8,128)(2,1)S(1)}, bf16[128,2048]{1,0:T(8,128)(2,1)S(1)}, u32[]{:S(2)}, u32[]{:S(2)}) collective-permute-start(bf16[128,2048]{1,0:T(8,128)(2,1)S(1)} %fusion.37), channel_id=1, source_target_pairs={{0,2},{1,3},{2,0},{3,1},{4,6},{5,7},{6,4},{7,5},{8,10},{9,11},{10,... | collective-permute-start | bytes 1572872 | tf_op jit(solution)/shard_map/ppermute | solution.py:322
  501.0 32.6 %collective-permute-start.60 = (bf16[128,2048]{1,0:T(8,128)(2,1)S(1)}, bf16[128,2048]{1,0:T(8,128)(2,1)S(1)}, u32[]{:S(2)}, u32[]{:S(2)}) collective-permute-start(bf16[128,2048]{1,0:T(8,128)(2,1)S(1)} %add_convert_fusion.3), channel_id=1, source_target_pairs={{0,2},{1,3},{2,0},{3,1},{4,6},{5,7},{6,4},{7,5},{8,10},{9,11},{10,... | collective-permute-start | bytes 1572872 | tf_op jit(solution)/shard_map/ppermute | solution.py:322
  515.1 33.1 %collective-permute-start.74 = (bf16[2,64,2048]{2,1,0:T(8,128)(2,1)S(1)}, bf16[2,64,2048]{2,1,0:T(8,128)(2,1)S(1)}, u32[]{:S(2)}, u32[]{:S(2)}) collective-permute-start(bf16[2,64,2048]{2,1,0:T(8,128)(2,1)S(1)} %bitcast.142), channel_id=1, source_target_pairs={{0,16},{4,20},{8,24},{12,28},{16,0},{20,4},{24,8},{28,12},{1,17},{... | collective-permute-start | bytes 1572872 | tf_op jit(solution)/shard_map/ppermute | solution.py:414
  526.0 23.8 %collective-permute-start.63 = (bf16[128,2048]{1,0:T(8,128)(2,1)S(1)}, bf16[128,2048]{1,0:T(8,128)(2,1)S(1)}, u32[]{:S(2)}, u32[]{:S(2)}) collective-permute-start(bf16[128,2048]{1,0:T(8,128)(2,1)S(1)} %get-tuple-element.222), channel_id=1, source_target_pairs={{0,1},{1,0},{2,3},{3,2},{4,5},{5,4},{6,7},{7,6},{8,9},{9,8},{10,11... | collective-permute-start | bytes 1572872 | tf_op jit(solution)/shard_map/ppermute | solution.py:322
  535.5 17.1 %collective-permute-start.61 = (bf16[128,2048]{1,0:T(8,128)(2,1)S(1)}, bf16[128,2048]{1,0:T(8,128)(2,1)S(1)}, u32[]{:S(2)}, u32[]{:S(2)}) collective-permute-start(bf16[128,2048]{1,0:T(8,128)(2,1)S(1)} %get-tuple-element.220), channel_id=1, source_target_pairs={{0,1},{1,0},{2,3},{3,2},{4,5},{5,4},{6,7},{7,6},{8,9},{9,8},{10,11... | collective-permute-start | bytes 1572872 | tf_op jit(solution)/shard_map/ppermute | solution.py:322
  569.6 15.4 %collective-permute-start.69 = (bf16[64,1536]{1,0:T(8,128)(2,1)S(1)}, bf16[64,1536]{1,0:T(8,128)(2,1)S(1)}, u32[]{:S(2)}, u32[]{:S(2)}) collective-permute-start(bf16[64,1536]{1,0:T(8,128)(2,1)S(1)} %get-tuple-element.311), channel_id=1, source_target_pairs={{0,1},{1,0},{2,3},{3,2},{4,5},{5,4},{6,7},{7,6},{8,9},{9,8},{10,11... | collective-permute-start | bytes 589832 | tf_op jit(solution)/shard_map/ppermute | solution.py:322
  (84 other events, 1059.5 us)
Sparse Core Ops, SparseCore 0:
  40.3 70.9 all-gather.3
  113.5 80.6 all-gather.5
  195.8 80.5 all-gather.7
  278.6 88.1 reduce-scatter.3
  368.9 87.9 reduce-scatter.5
  459.1 77.0 reduce-scatter.7
